TPU v7x, 32 devices: a whole 2x2x4 slice. The times are simulated.
32 devices in a mesh: batch: 4 (over y, x), seq: 8 (over z, core).
Axes of the slice: x: 2, y: 2, z: 4, core: 2. Of those that a mesh axis runs over, the one named last changes fastest.
Arguments:
- tokens: float32 [4, 4096, 768], P('batch', 'seq'), may hold values from -6 to 6
- lengths: int32 [4, 3], P('batch'), may hold values from 1 to 30, as said below
- cotangent: float32 [4, 4096, 768], P('batch', 'seq'), may hold values from -6 to 6
- norm_gain: float32 [768, 2], replicated, may hold values from 0.5 to 1.5
- norm_shift: float32 [768, 2], replicated, may hold values from -3 to 3
- alpha_logit: float32 [768, 16], replicated, may hold values from -1 to 1
- delta_logit: float32 [768, 16], replicated, may hold values from -10 to -3
- ema_beta: float32 [768, 16], replicated, may hold values from -0.005859375 to 0.005859375
- ema_eta: float32 [768, 16], replicated, may hold values from -1.5 to 1.5
- ema_omega: float32 [768], replicated, may hold values from -6 to 6
- w_value: bfloat16 [768, 1536], replicated, may hold values from -0.21875 to 0.21875
- b_value: float32 [1536], replicated, may hold values from -3 to 3
- w_gates: bfloat16 [768, 3200], replicated, may hold values from -0.21875 to 0.21875
- b_gates: float32 [3200], replicated, may hold values from -3 to 3
- query_key: float32 [128, 3], replicated, may hold values from -5 to 5
- position_bias: float32 [128], replicated, may hold values from -5 to 5
- w_output: bfloat16 [1536, 768], replicated, may hold values from -0.625 to 0.625
- b_output: float32 [768], replicated, may hold values from -3 to 3
- w_expand: bfloat16 [768, 1536], replicated, may hold values from -0.21875 to 0.21875
- b_expand: float32 [1536], replicated, may hold values from -3 to 3
- w_shrink: bfloat16 [1536, 768], replicated, may hold values from -0.15625 to 0.15625
- b_shrink: float32 [768], replicated, may hold values from -3 to 3
Outputs:
- out: float32 [4, 4096, 768], P('batch', 'seq')
- grad_tokens: float32 [4, 4096, 768], P('batch', 'seq')
- grad_norm_gain: float32 [768, 2], replicated
- grad_norm_shift: float32 [768, 2], replicated
- grad_alpha_logit: float32 [768, 16], replicated
- grad_delta_logit: float32 [768, 16], replicated
- grad_ema_beta: float32 [768, 16], replicated
- grad_ema_eta: float32 [768, 16], replicated
- grad_ema_omega: float32 [768], replicated
- grad_w_value: float32 [768, 1536], replicated
- grad_b_value: float32 [1536], replicated
- grad_w_gates: float32 [768, 3200], replicated
- grad_b_gates: float32 [3200], replicated
- grad_query_key: float32 [128, 3], replicated
- grad_position_bias: float32 [128], replicated
- grad_w_output: float32 [1536, 768], replicated
- grad_b_output: float32 [768], replicated
- grad_w_expand: float32 [768, 1536], replicated
- grad_b_expand: float32 [1536], replicated
- grad_w_shrink: float32 [1536, 768], replicated
- grad_b_shrink: float32 [768], replicated
Inputs may be any that keep to these rules, and one draw needn't show every extreme that they name: `lengths`: each row packs three documents, measured in groups of 128 tokens, that sum to 32; the first and the last each have 1 to 4 groups.
All inputs are finite; a program needn't handle non-finite values.
Results may differ from a plain program's by a relative error of at most 0.0003.
Values sent between devices are 32-bit elements; how exact they have to be, the bound alone decides.
A program may use at most 384 MiB of HBM per device.

v0:
```python
import math

import jax
import jax.numpy as jnp
from jax import lax
from jax.sharding import PartitionSpec as P

highest = lax.Precision.HIGHEST


def carried_in_2(array, axis, combine, identity, reverse):
    length, mine = (lax.axis_size(axis), lax.axis_index(axis))
    everything = jax.tree.map(lambda part: lax.all_gather(part, axis), array)
    start = jax.tree.map(
        lambda part, zero: jnp.broadcast_to(jnp.asarray(zero, part.dtype), part.shape),
        array,
        identity,
    )

    def turn(k, before):
        at = length - 1 - k if reverse else k
        reached = at > mine if reverse else at < mine
        new = combine(before, jax.tree.map(lambda part: part[at], everything))
        return jax.tree.map(lambda a, b: jnp.where(reached, a, b), new, before)

    return lax.fori_loop(0, length, turn, start)


def matmul(left_side, right_side):
    return jnp.dot(left_side, right_side, precision=highest, preferred_element_type=jnp.float32)


def layer_norm(inputs, gain_row, shift_row):
    centre = inputs - jnp.mean(inputs, axis=-1, keepdims=True)
    spread = jnp.mean(centre * centre, axis=-1, keepdims=True)
    return centre * lax.rsqrt(spread + 1e-05) * gain_row + shift_row


def group_keep(lengths, group_ids):
    first_end = lengths[0]
    second_end = lengths[0] + lengths[1]
    starts = (group_ids == 0) | (group_ids == first_end) | (group_ids == second_end)
    return 1.0 - starts.astype(jnp.float32)


def ema_tables(params, group_len):
    rate_in = jax.nn.sigmoid(params["alpha_logit"]).T
    damping = jax.nn.sigmoid(params["delta_logit"]).T
    inflow = rate_in * params["ema_beta"].T
    log_decay = jnp.log1p(-rate_in * damping)
    offsets = jnp.arange(group_len).astype(jnp.float32)
    powers = jnp.exp(offsets[:, None, None] * log_decay[None])
    mixing = params["ema_eta"].T
    lag_kernel = jnp.sum(powers * (mixing * inflow)[None], axis=1)
    row_index = jnp.arange(group_len)
    lag_grid = row_index[:, None] - row_index[None, :]
    toeplitz = jnp.where(
        (lag_grid >= 0)[:, :, None], lag_kernel[jnp.clip(lag_grid, 0, group_len - 1)], 0.0
    )
    end_weight = powers[::-1] * inflow[None]
    read_weight = powers * jnp.exp(log_decay)[None] * mixing[None]
    group_decay = jnp.exp(group_len * log_decay)
    return (toeplitz, end_weight, read_weight, group_decay, log_decay)


def group_states(entries, keep_mask, group_decay, initial):

    def advance(running, element):
        fresh_entry, keep_one = element
        entering = keep_one * running
        return (group_decay * entering + fresh_entry, entering)

    final_state, entering = lax.scan(advance, initial, (entries, keep_mask))
    return (entering, final_state)


def group_attention(queries, key_rows, values, position_bias, group_len):
    row_count, shared_dim = queries.shape
    blocks = row_count // group_len
    row_index = jnp.arange(group_len)
    lag_grid = row_index[:, None] - row_index[None, :]
    bias_table = position_bias[jnp.clip(lag_grid, 0, group_len - 1)]
    scores = (
        jnp.einsum(
            "cid,cjd->cij",
            queries.reshape(blocks, group_len, shared_dim),
            key_rows.reshape(blocks, group_len, shared_dim),
            precision=highest,
        )
        / math.sqrt(shared_dim)
        + bias_table[None]
    )
    scores = jnp.where((lag_grid >= 0)[None], scores, -1e30)
    weights = jax.nn.softmax(scores, axis=-1)
    attended = jnp.einsum(
        "cij,cjv->civ",
        weights,
        values.reshape(blocks, group_len, values.shape[1]),
        precision=highest,
    )
    return attended.reshape(row_count, values.shape[1])


def gated_mixer(params, tokens, keep_mask, carry_ema):
    group_len = params["position_bias"].shape[0]
    row_count, feature_dim = tokens.shape
    shared_dim = params["query_key"].shape[0]
    value_dim = params["w_value"].shape[1]
    normed = layer_norm(tokens, params["norm_gain"][:, 0], params["norm_shift"][:, 0])
    values = jax.nn.silu(matmul(normed, params["w_value"]) + params["b_value"])
    tables = ema_tables(params, group_len)
    blocks = normed.reshape(row_count // group_len, group_len, feature_dim)
    within = jnp.einsum("tsd,csd->ctd", tables[0], blocks, precision=highest)
    entries = jnp.einsum("csd,snd->cnd", blocks, tables[1], precision=highest)
    states = group_states(entries, keep_mask, tables[3], jnp.zeros_like(tables[3]))
    between = jnp.einsum("cnd,tnd->ctd", states[0], tables[2], precision=highest)
    smoothed = (within + between).reshape(row_count, feature_dim) + carry_ema
    mixed = jax.nn.silu(smoothed + params["ema_omega"] * normed)
    gate_input = matmul(mixed, params["w_gates"]) + params["b_gates"]
    update = jax.nn.sigmoid(gate_input[:, :feature_dim])
    shared = jax.nn.silu(gate_input[:, feature_dim : feature_dim + shared_dim])
    reset_gate = jax.nn.silu(
        gate_input[:, feature_dim + shared_dim : feature_dim + shared_dim + value_dim]
    )
    candidate = gate_input[:, feature_dim + shared_dim + value_dim :]
    queries = shared * params["query_key"][:, 0] + params["query_key"][:, 2]
    key_rows = shared * params["query_key"][:, 1]
    attended = group_attention(queries, key_rows, values, params["position_bias"], group_len)
    hidden = jax.nn.silu(
        candidate + matmul(attended * reset_gate, params["w_output"]) + params["b_output"]
    )
    return tokens + update * (hidden - tokens)


def feed_forward(params, tokens):
    normed = layer_norm(tokens, params["norm_gain"][:, 1], params["norm_shift"][:, 1])
    inner_act = jax.nn.silu(matmul(normed, params["w_expand"]) + params["b_expand"])
    return tokens + matmul(inner_act, params["w_shrink"]) + params["b_shrink"]


def summary(params, tokens, keep_mask):
    group_len = params["position_bias"].shape[0]
    row_count, feature_dim = tokens.shape
    normed = layer_norm(tokens, params["norm_gain"][:, 0], params["norm_shift"][:, 0])
    tables = ema_tables(params, group_len)
    blocks = normed.reshape(row_count // group_len, group_len, feature_dim)
    entries = jnp.einsum("csd,snd->cnd", blocks, tables[1], precision=highest)
    states = group_states(entries, keep_mask, tables[3], jnp.zeros_like(tables[3]))
    through = jnp.exp(row_count * tables[4]) * jnp.prod(keep_mask)
    return (through, states[1])


def carry_part(params, carried, keep_mask, row_count):
    group_len = params["position_bias"].shape[0]
    tables = ema_tables(params, group_len)
    silent = jnp.zeros((keep_mask.shape[0],) + carried.shape, jnp.float32)
    states = group_states(silent, keep_mask, tables[3], carried)
    return jnp.einsum("cnd,tnd->ctd", states[0], tables[2], precision=highest).reshape(
        row_count, carried.shape[1]
    )


def combine_affine(earlier, later_one):
    return (earlier[0] * later_one[0], later_one[0] * earlier[1] + later_one[1])


def shards(
    tokens,
    lengths,
    cotangent,
    norm_gain,
    norm_shift,
    alpha_logit,
    delta_logit,
    ema_beta,
    ema_eta,
    ema_omega,
    w_value,
    b_value,
    w_gates,
    b_gates,
    query_key,
    position_bias,
    w_output,
    b_output,
    w_expand,
    b_expand,
    w_shrink,
    b_shrink,
):
    params = dict(
        norm_gain=norm_gain,
        norm_shift=norm_shift,
        alpha_logit=alpha_logit,
        delta_logit=delta_logit,
        ema_beta=ema_beta,
        ema_eta=ema_eta,
        ema_omega=ema_omega,
        w_value=w_value.astype(jnp.float32),
        b_value=b_value,
        w_gates=w_gates.astype(jnp.float32),
        b_gates=b_gates,
        query_key=query_key,
        position_bias=position_bias,
        w_output=w_output.astype(jnp.float32),
        b_output=b_output,
        w_expand=w_expand.astype(jnp.float32),
        b_expand=b_expand,
        w_shrink=w_shrink.astype(jnp.float32),
        b_shrink=b_shrink,
    )
    local_tokens = tokens[0]
    row_count = local_tokens.shape[0]
    group_len = position_bias.shape[0]
    blocks = row_count // group_len
    keep_mask = group_keep(lengths[0], lax.axis_index("seq") * blocks + jnp.arange(blocks))
    through, final_state = summary(params, local_tokens, keep_mask)
    identity = (jnp.ones_like(through), jnp.zeros_like(final_state))
    carried = carried_in_2((through, final_state), "seq", combine_affine, identity, False)[1]
    carry_ema, carry_pull = jax.vjp(
        lambda params_in, carried_in: carry_part(params_in, carried_in, keep_mask, row_count),
        params,
        carried,
    )
    middle, mixer_pull = jax.vjp(
        lambda params_in, tokens_in, extra_in: gated_mixer(
            params_in, tokens_in, keep_mask, extra_in
        ),
        params,
        local_tokens,
        carry_ema,
    )
    output, ffn_pull = jax.vjp(feed_forward, params, middle)
    grad_ffn, grad_middle = ffn_pull(cotangent[0])
    grad_mix, grad_rows, grad_extra = mixer_pull(grad_middle)
    grad_carry, direct = carry_pull(grad_extra)
    adjoint = carried_in_2((through, direct), "seq", combine_affine, identity, True)[1]
    sum_pull = jax.vjp(
        lambda params_in, tokens_in: summary(params_in, tokens_in, keep_mask), params, local_tokens
    )[1]
    grad_sum, grad_local = sum_pull((adjoint * carried, adjoint))
    totals = jax.tree.map(
        lambda ffn_term, mix_term, carry_term, sum_term: ffn_term
        + mix_term
        + carry_term
        + sum_term,
        grad_ffn,
        grad_mix,
        grad_carry,
        grad_sum,
    )
    shares = (
        lax.psum_scatter(totals["norm_gain"], "seq", scatter_dimension=0, tiled=True),
        lax.psum_scatter(totals["norm_shift"], "seq", scatter_dimension=0, tiled=True),
        lax.psum_scatter(totals["alpha_logit"], "seq", scatter_dimension=0, tiled=True),
        lax.psum_scatter(totals["delta_logit"], "seq", scatter_dimension=0, tiled=True),
        lax.psum_scatter(totals["ema_beta"], "seq", scatter_dimension=0, tiled=True),
        lax.psum_scatter(totals["ema_eta"], "seq", scatter_dimension=0, tiled=True),
        lax.psum_scatter(totals["ema_omega"], "seq", scatter_dimension=0, tiled=True),
        lax.psum_scatter(totals["w_value"], "seq", scatter_dimension=0, tiled=True),
        lax.psum_scatter(totals["b_value"], "seq", scatter_dimension=0, tiled=True),
        lax.psum_scatter(totals["w_gates"], "seq", scatter_dimension=0, tiled=True),
        lax.psum_scatter(totals["b_gates"], "seq", scatter_dimension=0, tiled=True),
        lax.psum_scatter(totals["query_key"], "seq", scatter_dimension=0, tiled=True),
        lax.psum_scatter(totals["position_bias"], "seq", scatter_dimension=0, tiled=True),
        lax.psum_scatter(totals["w_output"], "seq", scatter_dimension=0, tiled=True),
        lax.psum_scatter(totals["b_output"], "seq", scatter_dimension=0, tiled=True),
        lax.psum_scatter(totals["w_expand"], "seq", scatter_dimension=0, tiled=True),
        lax.psum_scatter(totals["b_expand"], "seq", scatter_dimension=0, tiled=True),
        lax.psum_scatter(totals["w_shrink"], "seq", scatter_dimension=0, tiled=True),
        lax.psum_scatter(totals["b_shrink"], "seq", scatter_dimension=0, tiled=True),
    )
    summed = lax.psum(
        (
            shares[0],
            shares[1],
            shares[2],
            shares[3],
            shares[4],
            shares[5],
            shares[6],
            shares[7],
            shares[8],
            shares[9],
            shares[10],
            shares[11],
            shares[12],
            shares[13],
            shares[14],
            shares[15],
            shares[16],
            shares[17],
            shares[18],
        ),
        "batch",
    )
    results = tuple(
        (
            lax.all_gather(summed[0], "seq", axis=0, tiled=True),
            lax.all_gather(summed[1], "seq", axis=0, tiled=True),
            lax.all_gather(summed[2], "seq", axis=0, tiled=True),
            lax.all_gather(summed[3], "seq", axis=0, tiled=True),
            lax.all_gather(summed[4], "seq", axis=0, tiled=True),
            lax.all_gather(summed[5], "seq", axis=0, tiled=True),
            lax.all_gather(summed[6], "seq", axis=0, tiled=True),
            lax.all_gather(summed[7], "seq", axis=0, tiled=True),
            lax.all_gather(summed[8], "seq", axis=0, tiled=True),
            lax.all_gather(summed[9], "seq", axis=0, tiled=True),
            lax.all_gather(summed[10], "seq", axis=0, tiled=True),
            lax.all_gather(summed[11], "seq", axis=0, tiled=True),
            lax.all_gather(summed[12], "seq", axis=0, tiled=True),
            lax.all_gather(summed[13], "seq", axis=0, tiled=True),
            lax.all_gather(summed[14], "seq", axis=0, tiled=True),
            lax.all_gather(summed[15], "seq", axis=0, tiled=True),
            lax.all_gather(summed[16], "seq", axis=0, tiled=True),
            lax.all_gather(summed[17], "seq", axis=0, tiled=True),
            lax.all_gather(summed[18], "seq", axis=0, tiled=True),
        )
    )
    return (output[None], (grad_rows + grad_local)[None]) + results


def solution(mesh):
    placed = (
        P("batch", "seq", None),
        P("batch", None),
        P("batch", "seq", None),
        P(),
        P(),
        P(),
        P(),
        P(),
        P(),
        P(),
        P(),
        P(),
        P(),
        P(),
        P(),
        P(),
        P(),
        P(),
        P(),
        P(),
        P(),
        P(),
    )
    return jax.shard_map(
        shards,
        mesh=mesh,
        in_specs=placed,
        out_specs=(
            P("batch", "seq", None),
            P("batch", "seq", None),
            P(),
            P(),
            P(),
            P(),
            P(),
            P(),
            P(),
            P(),
            P(),
            P(),
            P(),
            P(),
            P(),
            P(),
            P(),
            P(),
            P(),
            P(),
            P(),
        ),
        check_vma=False,
    )
```

profile of v0, /device:TPU:1, one launch (start us, length us, event | category | flops | bytes accessed | tf_op | source)
XLA Modules:
  0.0 1853.7 jit_solution(499053274363298037)
XLA Ops:
  18.5 16.1 all-gather
  44.5 10.1 rev.11
  58.8 14.4 fusion.94
  79.9 15.5 all-gather.1
  114.6 68.8 %gather_fusion = f32[16384,768]{1,0:T(8,128)} fusion(f32[128,768]{1,0:T(8,128)S(1)} %copy.280, s32[16384]{0:T(1024)S(1)} %broadcast_clamp_fusion), kind=kCustom, calls=%fused_computation | custom fusion | bytes 100728832 | tf_op jit(solution)/shard_map/jvp()/gather | solution.py:58
  183.4 49.1 %copy.281 = f32[128,128,768]{1,0,2:T(8,128)} copy(f32[128,128,768]{2,1,0:T(8,128)} %bitcast.453) | data formatting | bytes 100663296 | tf_op jit(solution)/shard_map/jvp()/gather | solution.py:58
  232.8 10.9 while.127
  245.3 82.4 %fusion.10 = f32[768,4,128]{2,1,0:T(4,128)S(1)} fusion(f32[128,128,768]{1,0,2:T(8,128)} %copy.281, pred[128,128]{1,0:T(8,128)(4,1)S(1)} %copy.277, f32[4,128,768]{1,0,2:T(4,128)} %copy.331, f32[768]{0:T(1024)S(1)} %copy-done.57, f32[768]{0:T(1024)S(1)} %copy-done.49, f32[4,128]{1,0:T(4,128)S(1)} %copy-done.88, f32[4,128]{1,0:T(4,128)S(1)} %copy-done.85), kind=kOutput, calls=%fused_computation.34 | convolution fusion | flops 618135552 | bytes 53504000 | tf_op jit(solution)/shard_map/jvp(tsd,csd->ctd)/dot_general | solution.py:113
  327.8 12.3 fusion.24
  340.1 13.1 bitcast_add_fusion.9
  355.9 97.6 %gather_fusion.1 = f32[16384]{0:T(1024)S(1)} fusion(f32[128]{0:T(128)S(1)} %copy-done.2, s32[16384]{0:T(1024)S(1)} %copy-done.63), kind=kCustom, calls=%fused_computation.1 | custom fusion | bytes 196608 | tf_op jit(solution)/shard_map/jvp()/gather | solution.py:82
  512.3 10.1 fusion.172
  523.8 11.2 fusion.192
  536.4 11.5 fusion.99
  549.4 11.5 fusion.79
  574.3 20.1 %fusion.103 = f32[768,3200]{1,0:T(8,128)} fusion(f32[512,768]{1,0:T(8,128)S(1)} %fusion.60, f32[512,128]{1,0:T(8,128)S(1)} %get-tuple-element.1335, f32[512,1536]{1,0:T(8,128)S(1)} %copy-done.40, f32[512,768]{1,0:T(8,128)S(1)} %copy-done.19, f32[512,768]{1,0:T(8,128)S(1)} %copy-done.52), kind=kOutput, calls=%fused_computation.177 | convolution fusion | flops 15105982464 | bytes 17956864 | tf_op jit(solution)/shard_map/transpose(jvp())/dot_general | solution.py:30
  594.5 37.7 %reduce-scatter.31.cloned.1.call-done = f32[192,768]{1,0:T(8,128)} async-done(((f32[1536,768]{1,0:T(8,128)}), f32[192,768]{1,0:T(8,128)}) %reduce-scatter.31.cloned.1.call-update) | async-done | bytes 589840 | tf_op jit(solution)/shard_map/reduce_scatter | solution.py:266
  632.2 56.2 %reduce-scatter.33.cloned.1.call-done = f32[96,1536]{1,0:T(8,128)} async-done(((f32[768,1536]{1,0:T(8,128)}), f32[96,1536]{1,0:T(8,128)}) %reduce-scatter.33.cloned.1.call-update) | async-done | bytes 589840 | tf_op jit(solution)/shard_map/reduce_scatter | solution.py:268
  688.5 56.1 %reduce-scatter.35.cloned.1.call-done = f32[192,768]{1,0:T(8,128)} async-done(((f32[1536,768]{1,0:T(8,128)}), f32[192,768]{1,0:T(8,128)}) %reduce-scatter.35.cloned.1.call-update) | async-done | bytes 589840 | tf_op jit(solution)/shard_map/reduce_scatter | solution.py:270
  744.6 104.4 %reduce-scatter.29.cloned.1.call-done = f32[96,3200]{1,0:T(8,128)} async-done(((f32[768,3200]{1,0:T(8,128)}), f32[96,3200]{1,0:T(8,128)}) %reduce-scatter.29.cloned.1.call-update) | async-done | bytes 1228816 | tf_op jit(solution)/shard_map/reduce_scatter | solution.py:262
  849.9 13.7 fusion.62
  866.3 15.9 fusion.89
  882.2 46.5 %fusion.8 = f32[768,4,128]{2,1,0:T(4,128)} fusion(f32[128,128,768]{1,0,2:T(8,128)} %copy.281, pred[128,128]{1,0:T(8,128)(4,1)S(1)} %copy-done.59, f32[4,128,768]{1,0,2:T(4,128)S(1)} %copy-done.10), kind=kOutput, calls=%fused_computation.32 | convolution fusion | flops 616562688 | bytes 53493760 | tf_op jit(solution)/shard_map/transpose(jvp(tsd,csd->ctd))/dot_general | solution.py:113
  938.9 17.1 all-gather.2
  969.7 14.2 fusion.189
  993.3 9.8 add_bitcast_fusion
  1026.2 13.7 fusion.76
  1039.9 85.6 %select_bitcast_fusion = f32[128,128,768]{1,0,2:T(8,128)} fusion(pred[128,128]{1,0:T(8,128)(4,1)S(1)} %copy-done.59, f32[4,128,768]{1,0,2:T(4,128)S(1)} %copy-done.11, f32[4,128,768]{1,0,2:T(4,128)S(1)} %copy-done.6, f32[768]{0:T(1024)S(1)} %copy-done.57, f32[768]{0:T(1024)S(1)} %copy-done.49, f32[4,128]{1,0:T(4,128)S(1)} %copy-done.89, ...), kind=kOutput, calls=%fused_computation.31 | convolution fusion | flops 618135552 | bytes 53504000 | tf_op jit(solution)/shard_map/transpose(jvp(tsd,csd->ctd))/dot_general | solution.py:113
  1125.5 14.4 fusion.173
  1139.9 49.0 %copy.333 = f32[128,128,768]{2,1,0:T(8,128)} copy(f32[128,128,768]{1,0,2:T(8,128)} %select_bitcast_fusion) | data formatting | bytes 100663296 | tf_op jit(solution)/shard_map/transpose(jvp(jit(_where)))/select_n | solution.py:57
  1189.0 109.2 %scatter_custom_fusion = f32[128,768]{1,0:T(8,128)S(1)} fusion(s32[16384]{0:T(1024)S(1)} %fusion.141, f32[16384,768]{1,0:T(8,128)} %bitcast.455, f32[]{:T(128)} %constant.252.clone.1), kind=kCustom, calls=%fused_computation.211 | custom fusion | flops 12582912 | bytes 393728 | tf_op jit(solution)/shard_map/transpose(jvp())/scatter-add | solution.py:58
  1299.1 26.6 %fusion.18 = (f32[16,768]{0,1:T(8,128)S(1)}, f32[16,768]{0,1:T(8,128)S(1)}, f32[128,16,768]{0,1,2:T(8,128)}, f32[128,16,768]{0,1,2:T(8,128)}) fusion(f32[128,16,768]{0,1,2:T(8,128)} %rev.11, f32[768,16,128]{2,1,0:T(8,128)} %fusion.173, f32[16,768]{0,1:T(8,128)S(1)} %copy-done.30, f32[768,16,4]{1,2,0:T(4,128)} %copy.295, f32[4,128,768]{1,0,2:T(4,128)} %copy.331, ...), kind=kOutput, calls=%fused_computation.50 | convolution fusion | flops 86482944 | bytes 27092992 | tf_op jit(solution)/shard_map/transpose(jvp(csd,snd->cnd))/dot_general | solution.py:114
  1325.7 10.2 rev.12
  1335.8 10.2 rev.13
  1346.1 40.2 %fusion.17 = (f32[16,768]{0,1:T(8,128)}, f32[16,768]{0,1:T(8,128)}, f32[16,768]{0,1:T(8,128)}, f32[16,768]{0,1:T(8,128)}, f32[16,768]{0,1:T(8,128)}, /*index=5*/...) fusion(f32[16,768]{0,1:T(8,128)} %copy.282, f32[16,768]{0,1:T(8,128)} %copy.278, f32[128]{0:T(128)S(1)} %copy-done.138, ...), kind=kOutput, calls=%fused_computation.47 | convolution fusion | flops 119439360 | bytes 21627392 | tf_op jit(solution)/shard_map/transpose(jvp(cnd,tnd->ctd))/dot_general | solution.py:158
  1405.3 113.7 %scatter_custom_fusion.1 = f32[128]{0:T(128)S(1)} fusion(s32[16384]{0:T(1024)} %copy-done.103, f32[16384]{0:T(1024)S(1)} %bitcast.479, f32[]{:T(128)} %constant.252.clone.1), kind=kCustom, calls=%fused_computation.290 | custom fusion | flops 16384 | bytes 1024 | tf_op jit(solution)/shard_map/transpose(jvp())/scatter-add | solution.py:82
  1522.1 25.6 %all-reduce.28 = (f32[768]{0:T(1024)S(1)}, f32[1536]{0:T(1024)S(1)}, f32[3200]{0:T(1024)S(1)}, f32[128]{0:T(128)S(1)}, f32[768]{0:T(1024)S(1)}, /*index=5*/f32[1536]{0:T(1024)S(1)}, f32[768]{0:T(1024)S(1)}) all-reduce(f32[768]{0:T(1024)S(1)} %copy-done.118, ...), channel_id=11, replica_groups=mesh['batch'=4,'seq'=8] {'seq'}, use_global_device_ids=true, to_apply=%region_61.62.clone | all-reduce | flops 8704 | bytes 69632
  1568.6 12.5 all-reduce.29
  1581.1 16.1 all-gather.3
  1597.9 11.5 all-gather.4
  1610.1 14.0 all-gather.5
  1624.8 14.1 all-gather.6
  1639.6 14.1 all-gather.7
  1654.4 14.1 all-gather.8
  1669.3 12.7 all-gather.9
  1684.2 25.2 %all-reduce.27 = (f32[768]{0:T(1024)}, f32[1536]{0:T(1024)}, f32[3200]{0:T(1024)}, f32[128]{0:T(128)}, f32[768]{0:T(1024)}, /*index=5*/f32[1536]{0:T(1024)}, f32[768]{0:T(1024)}) all-reduce(f32[768]{0:T(1024)S(1)} %dynamic-update-slice, f32[1536]{0:T(1024)S(1)} %dynamic-update-slice.1, ...), channel_id=1, replica_groups=mesh['batch'=4,'seq'=8] {'seq'}, use_global_device_ids=true, to_apply=%add.13 | all-reduce | flops 8704 | bytes 69632
  1709.4 19.7 %all-gather.24.cloned.1.call-done = f32[1536,768]{1,0:T(8,128)} async-done(((f32[192,768]{1,0:T(8,128)}), f32[1536,768]{1,0:T(8,128)}) %all-gather.24.cloned.1.call-update) | async-done | bytes 4718608 | tf_op jit(solution)/shard_map/all_gather | solution.py:316
  1729.1 94.4 %all-gather.18.cloned.1.call-done = f32[768,3200]{1,0:T(8,128)} async-done(((f32[96,3200]{1,0:T(8,128)}), f32[768,3200]{1,0:T(8,128)}) %all-gather.18.cloned.1.call-update) | async-done | bytes 9830416 | tf_op jit(solution)/shard_map/all_gather | solution.py:308
  (622 shorter events, 312.4 us)
Async XLA Ops:
  7.2 468.6 %copy-start = (bf16[1536,768]{1,0:T(8,128)(2,1)S(1)}, bf16[1536,768]{1,0:T(8,128)(2,1)}, u32[]{:S(2)}) copy-start(bf16[1536,768]{1,0:T(8,128)(2,1)} %param.54) | copy-start | bytes 7077892
  7.2 587.3 %reduce-scatter.27.cloned.1.call-start = ((), (), s32[]{:S(2)}) async-start(), calls=%async_computation.12 | async-start | bytes 5308416 | tf_op jit(solution)/shard_map/reduce_scatter | solution.py:260
  7.8 106.8 %copy-start.62 = (s32[16384]{0:T(1024)}, s32[16384]{0:T(1024)S(1)}, u32[]{:S(2)}) copy-start(s32[16384]{0:T(1024)S(1)} %broadcast_clamp_fusion) | copy-start | bytes 196612
  183.4 49.1 %copy-start.77 = (pred[128,128]{0,1:T(8,128)(4,1)S(1)}, pred[128,128]{0,1:T(8,128)(4,1)}, u32[]{:S(2)}) copy-start(pred[128,128]{0,1:T(8,128)(4,1)} %subtract_compare_fusion) | copy-start | bytes 49156
  183.4 49.3 %copy-start.8 = (f32[16,768]{1,0:T(8,128)S(1)}, f32[16,768]{1,0:T(8,128)}, u32[]{:S(2)}) copy-start(f32[16,768]{1,0:T(8,128)} %copy-done.7) | copy-start | bytes 147460
  183.4 49.3 %copy-start.37 = (f32[16,768]{1,0:T(8,128)S(1)}, f32[16,768]{1,0:T(8,128)}, u32[]{:S(2)}) copy-start(f32[16,768]{1,0:T(8,128)} %custom-call) | copy-start | bytes 147460
  183.4 49.3 %copy-start.135 = (f32[4]{0:T(128)S(1)}, f32[4]{0:T(128)}, u32[]{:S(2)}) copy-start(f32[4]{0:T(128)} %copy-done.134) | copy-start | bytes 52
  243.7 84.0 %copy-start.38 = (f32[4,16,768]{2,1,0:T(8,128)}, f32[4,16,768]{2,1,0:T(8,128)S(1)}, u32[]{:S(2)}) copy-start(f32[4,16,768]{2,1,0:T(8,128)S(1)} %get-tuple-element.1860) | copy-start | bytes 589828
  245.3 82.5 %copy-start.50 = (f32[4,16,768]{1,0,2:T(4,128)S(1)}, f32[4,16,768]{1,0,2:T(4,128)}, u32[]{:S(2)}) copy-start(f32[4,16,768]{1,0,2:T(4,128)} %copy.288) | copy-start | bytes 589828
  245.3 82.5 %copy-start.55 = (f32[16,768]{0,1:T(8,128)S(1)}, f32[16,768]{0,1:T(8,128)}, u32[]{:S(2)}) copy-start(f32[16,768]{0,1:T(8,128)} %copy.278) | copy-start | bytes 147460
  245.3 82.5 %copy-start.70 = (f32[16,768]{0,1:T(8,128)S(1)}, f32[16,768]{0,1:T(8,128)}, u32[]{:S(2)}) copy-start(f32[16,768]{0,1:T(8,128)} %copy.283) | copy-start | bytes 147460
  245.3 82.5 %copy-start.72 = (f32[16,768]{0,1:T(8,128)S(1)}, f32[16,768]{0,1:T(8,128)}, u32[]{:S(2)}) copy-start(f32[16,768]{0,1:T(8,128)} %copy.282) | copy-start | bytes 147460
  245.3 82.5 %copy-start.137 = (f32[128]{0:T(128)S(1)}, f32[128]{0:T(128)}, u32[]{:S(2)}) copy-start(f32[128]{0:T(128)} %iota_convert_fusion) | copy-start | bytes 1540
  355.9 98.4 %copy-start.132 = (f32[128,3]{0,1:T(4,128)S(1)}, f32[128,3]{0,1:T(4,128)}, u32[]{:S(2)}) copy-start(f32[128,3]{0,1:T(4,128)} %param.52) | copy-start | bytes 4612
  355.9 98.4 %copy-start.92 = (f32[512]{0:T(512)S(1)}, f32[512]{0:T(512)}, u32[]{:S(2)}) copy-start(f32[512]{0:T(512)} %copy-done.91) | copy-start | bytes 6148
  355.9 98.4 %copy-start.97 = (f32[512]{0:T(512)S(1)}, f32[512]{0:T(512)}, u32[]{:S(2)}) copy-start(f32[512]{0:T(512)} %fusion.156) | copy-start | bytes 6148
  355.9 98.4 %copy-start.115 = (f32[768]{0:T(1024)S(1)}, f32[768]{0:T(1024)}, u32[]{:S(2)}) copy-start(f32[768]{0:T(1024)} %param.47) | copy-start | bytes 9220
  355.9 100.9 %copy-start.143 = (f32[1536]{0:T(1024)S(1)}, f32[1536]{0:T(1024)}, u32[]{:S(2)}) copy-start(f32[1536]{0:T(1024)} %param.49) | copy-start | bytes 18436
  471.0 28.1 %copy-start.28 = (f32[512,3200]{1,0:T(8,128)}, f32[512,3200]{1,0:T(8,128)S(1)}, u32[]{:S(2)}) copy-start(f32[512,3200]{1,0:T(8,128)S(1)} %convolution_add_fusion) | copy-start | bytes 19660804
  471.8 33.9 %copy-start.95 = (f32[4,128]{1,0:T(4,128)}, f32[4,128]{1,0:T(4,128)S(1)}, u32[]{:S(2)}) copy-start(f32[4,128]{1,0:T(4,128)S(1)} %get-tuple-element.1362) | copy-start | bytes 6148
  471.9 33.9 %copy-start.104 = (f32[4,128]{1,0:T(4,128)}, f32[4,128]{1,0:T(4,128)S(1)}, u32[]{:S(2)}) copy-start(f32[4,128]{1,0:T(4,128)S(1)} %fusion.134) | copy-start | bytes 6148
  522.4 109.8 %reduce-scatter.31.cloned.1.call-start = ((), (), s32[]{:S(2)}) async-start(), calls=%async_computation.16 | async-start | bytes 5308416 | tf_op jit(solution)/shard_map/reduce_scatter | solution.py:266
  535.0 153.5 %reduce-scatter.33.cloned.1.call-start = ((), (), s32[]{:S(2)}) async-start(), calls=%async_computation.18 | async-start | bytes 5308416 | tf_op jit(solution)/shard_map/reduce_scatter | solution.py:268
  548.0 196.6 %reduce-scatter.35.cloned.1.call-start = ((), (), s32[]{:S(2)}) async-start(), calls=%async_computation.20 | async-start | bytes 5308416 | tf_op jit(solution)/shard_map/reduce_scatter | solution.py:270
  560.9 288.0 %reduce-scatter.29.cloned.1.call-start = ((), (), s32[]{:S(2)}) async-start(), calls=%async_computation.14 | async-start | bytes 11059200 | tf_op jit(solution)/shard_map/reduce_scatter | solution.py:262
  570.7 279.2 %copy-start.60 = (f32[512,128]{1,0:T(8,128)}, f32[512,128]{1,0:T(8,128)S(1)}, u32[]{:S(2)}) copy-start(f32[512,128]{1,0:T(8,128)S(1)} %get-tuple-element.1335) | copy-start | bytes 786436
  594.4 803.2 %all-reduce.33.cloned.1.call-start = ((), (), s32[]{:S(2)}) async-start(), calls=%async_computation.29 | async-start | bytes 7176192 | tf_op jit(solution)/shard_map/psum | solution.py:273
  848.9 713.6 %reduce-scatter.49.cloned.1.call-start = ((), (), s32[]{:S(2)}) async-start(), calls=%async_computation.28 | async-start | bytes 73728
  849.8 713.6 %reduce-scatter.37.cloned.1.call-start = ((), (), s32[]{:S(2)}) async-start(), calls=%async_computation.22 | async-start | bytes 442368
  930.5 32.5 %copy-start.39 = (f32[4,16,768]{2,1,0:T(8,128)S(1)}, f32[4,16,768]{2,1,0:T(8,128)}, u32[]{:S(2)}) copy-start(f32[4,16,768]{2,1,0:T(8,128)} %copy-done.38) | copy-start | bytes 589828
  1025.0 539.2 %reduce-scatter.39.cloned.1.call-start = ((), (), s32[]{:S(2)}) async-start(), calls=%async_computation.23 | async-start | bytes 442368
  1026.1 539.0 %reduce-scatter.41.cloned.1.call-start = ((), (), s32[]{:S(2)}) async-start(), calls=%async_computation.24 | async-start | bytes 442368
  1039.9 149.0 %copy-start.103 = (s32[16384]{0:T(1024)}, s32[16384]{0:T(1024)S(1)}, u32[]{:S(2)}) copy-start(s32[16384]{0:T(1024)S(1)} %fusion.141) | copy-start | bytes 196612
  1039.9 85.6 %copy-start.22 = (f32[768,16,4]{1,2,0:T(4,128)S(1)}, f32[768,16,4]{1,2,0:T(4,128)}, u32[]{:S(2)}) copy-start(f32[768,16,4]{1,2,0:T(4,128)} %copy.299) | copy-start | bytes 589828
  1394.2 171.7 %reduce-scatter.43.cloned.1.call-start = ((), (), s32[]{:S(2)}) async-start(), calls=%async_computation.25 | async-start | bytes 442368
  1395.2 171.6 %reduce-scatter.45.cloned.1.call-start = ((), (), s32[]{:S(2)}) async-start(), calls=%async_computation.26 | async-start | bytes 442368
  1396.2 171.5 %reduce-scatter.47.cloned.1.call-start = ((), (), s32[]{:S(2)}) async-start(), calls=%async_computation.27 | async-start | bytes 442368
  1397.5 311.9 %all-gather.16.cloned.1.call-start = ((), (), s32[]{:S(2)}) async-start(), calls=%async_computation.13 | async-start | bytes 5308416 | tf_op jit(solution)/shard_map/all_gather | solution.py:306
  1398.1 311.3 %all-gather.20.cloned.1.call-start = ((), (), s32[]{:S(2)}) async-start(), calls=%async_computation.17 | async-start | bytes 5308416 | tf_op jit(solution)/shard_map/all_gather | solution.py:312
  1398.7 310.7 %all-gather.22.cloned.1.call-start = ((), (), s32[]{:S(2)}) async-start(), calls=%async_computation.19 | async-start | bytes 5308416 | tf_op jit(solution)/shard_map/all_gather | solution.py:314
  1399.3 329.8 %all-gather.24.cloned.1.call-start = ((), (), s32[]{:S(2)}) async-start(), calls=%async_computation.21 | async-start | bytes 5308416 | tf_op jit(solution)/shard_map/all_gather | solution.py:316
  1399.9 119.1 %copy-start.61 = (f32[512,128]{1,0:T(8,128)S(1)}, f32[512,128]{1,0:T(8,128)}, u32[]{:S(2)}) copy-start(f32[512,128]{1,0:T(8,128)} %copy-done.60) | copy-start | bytes 786436
  1399.9 423.6 %all-gather.18.cloned.1.call-start = ((), (), s32[]{:S(2)}) async-start(), calls=%async_computation.15 | async-start | bytes 11059200 | tf_op jit(solution)/shard_map/all_gather | solution.py:308
  1519.1 31.8 %copy-start.120 = (f32[4,128]{1,0:T(4,128)S(1)}, f32[4,128]{1,0:T(4,128)}, u32[]{:S(2)}) copy-start(f32[4,128]{1,0:T(4,128)} %get-tuple-element.1166) | copy-start | bytes 6148
  1519.1 31.8 %copy-start.119 = (f32[512]{0:T(512)S(1)}, f32[512]{0:T(512)}, u32[]{:S(2)}) copy-start(f32[512]{0:T(512)} %get-tuple-element.1164) | copy-start | bytes 6148
  1519.1 31.8 %copy-start.102 = (f32[512]{0:T(512)S(1)}, f32[512]{0:T(512)}, u32[]{:S(2)}) copy-start(f32[512]{0:T(512)} %copy-done.100) | copy-start | bytes 6148
  1519.1 31.8 %copy-start.114 = (f32[512]{0:T(512)S(1)}, f32[512]{0:T(512)}, u32[]{:S(2)}) copy-start(f32[512]{0:T(512)} %copy-done.113) | copy-start | bytes 6148
  1519.1 31.8 %copy-start.112 = (f32[512]{0:T(512)S(1)}, f32[512]{0:T(512)}, u32[]{:S(2)}) copy-start(f32[512]{0:T(512)} %copy-done.111) | copy-start | bytes 6148
  (127 other events, 748.7 us)
Sparse Core Ops, SparseCore 0:
  522.5 53.4 reduce-scatter.26
  578.9 53.2 reduce-scatter.30
  635.1 53.3 reduce-scatter.32
  691.2 53.3 reduce-scatter.34
  747.3 101.5 reduce-scatter.28
  853.0 95.7 all-reduce.32
  951.0 26.8 reduce-scatter.48
  1025.1 25.1 reduce-scatter.36
  1053.1 28.7 reduce-scatter.38
  1394.4 25.1 reduce-scatter.40
  1422.3 28.7 reduce-scatter.42
  1454.0 28.8 reduce-scatter.44
  1485.1 28.7 reduce-scatter.46
  1515.5 54.6 all-gather.15
  1571.8 51.0 all-gather.19
  1624.5 51.3 all-gather.21
  1677.5 51.5 all-gather.23
  1730.7 92.7 all-gather.17
where the time goes:
time: 1860 us; the launch traced here: 1850 us
  matrix products  534 us (29%)
  local copies, waits for them, and re-layouts  401 us (22%)
  waiting for transfers between devices  371 us (20%)
  other arithmetic  313 us (17%)
  blocking collectives  209 us (11%)
  between operations  23.1 us (1%)
    dot_general x3, matrix products, gated_mixer(): within = jnp.einsum('tsd,csd->ctd', tables[0], blocks, precision=highest)  214 us
    dot_general x15, matrix products, matmul(): jnp.dot(left_side, right_side, precision=highest, preferred_element_type=...  131 us
    gather x2, local copies, waits for them, and re-layouts, ema_tables(): lag_kernel[jnp.clip(lag_grid, 0, group_len - 1)]  118 us
    scatter-add x1, other arithmetic, group_attention(): bias_table = position_bias[jnp.clip(lag_grid, 0, group_len - 1)]  114 us
    scatter-add x1, other arithmetic, ema_tables(): lag_kernel[jnp.clip(lag_grid, 0, group_len - 1)]  109 us
    reduce_scatter x1, waiting for transfers between devices, shards(): lax.psum_scatter(totals['w_gates'], 'seq', scatter_dimension=0, tiled=True)  104 us
    gather x2, local copies, waits for them, and re-layouts, group_attention(): bias_table = position_bias[jnp.clip(lag_grid, 0, group_len - 1)]  98.3 us
    all_gather x1, waiting for transfers between devices, shards(): lax.all_gather(summed[9], 'seq', axis=0, tiled=True)  94.4 us
  transfers between devices with their start and end apart: 18, of which 6 were waited for; matrix products, arithmetic and copies ran while one was open for 40% of the time, Pallas kernels for 0%

commit v1 on v0

v1 whole, which is shorter than its diff:
```python
import functools
import math
import typing

import jax
import jax.numpy as jnp
from jax import lax
from jax.experimental import pallas as pl
from jax.experimental.pallas import tpu as pltpu
from jax.sharding import PartitionSpec as P

f32 = jnp.float32
bf16 = jnp.bfloat16
MESH = pl.DeviceIdType.MESH

SEG = 8
LANES = 128
TILE = 256

NN = (((1,), (0,)), ((), ()))
NT = (((1,), (1,)), ((), ()))


def split(value):
    high = value.astype(bf16)
    return high, (value - high.astype(f32)).astype(bf16)


def dot(a, b, dims=NN):
    return lax.dot_general(a, b, dims, preferred_element_type=f32)


def dot3(a, b, dims=NN):
    a_high, a_low = a
    b_high, b_low = b
    return dot(a_high, b_high, dims) + (dot(a_high, b_low, dims) + dot(a_low, b_high, dims))


def sigmoid(value):
    return 1.0 / (1.0 + jnp.exp(-value))


def silu(value):
    return value * sigmoid(value)


def dsilu(value):
    s = sigmoid(value)
    return s * (1.0 + value * (1.0 - s))


def row_get(ref, part):
    return jnp.concatenate([ref[d, part, :] for d in range(ref.shape[0])], axis=-1)


def row_set(ref, part, value):
    for d in range(ref.shape[0]):
        ref[d, part, :] = value[:, d * LANES : (d + 1) * LANES]


def col_get(ref, i, size=TILE):
    n = size // LANES
    return jnp.concatenate([ref[i * n + k] for k in range(n)], axis=-1)


def col_set(ref, i, value):
    n = value.shape[1] // LANES
    for k in range(n):
        ref[i * n + k] = value[:, k * LANES : (k + 1) * LANES]


def at(i, size):
    return pl.ds(pl.multiple_of(i * size, size), size)


def off(start, i, size):
    return pl.ds(pl.multiple_of(start + i * size, LANES), size)


class Refs(typing.NamedTuple):
    x: typing.Any
    cot: typing.Any
    sk: typing.Any
    pk: typing.Any
    kf: typing.Any
    tables: typing.Any
    gains: typing.Any
    w_value: typing.Any
    w_gates: typing.Any
    w_output: typing.Any
    w_expand: typing.Any
    w_shrink: typing.Any
    b_value: typing.Any
    b_gates: typing.Any
    b_expand: typing.Any
    qk: typing.Any
    bias_row: typing.Any
    out: typing.Any
    dx: typing.Any
    dw_value: typing.Any
    dw_gates: typing.Any
    dw_output: typing.Any
    dw_expand: typing.Any
    dw_shrink: typing.Any
    s768: typing.Any
    s_value: typing.Any
    s_expand: typing.Any
    s_gates: typing.Any
    s_small: typing.Any
    wv: typing.Any
    wg: typing.Any
    wo: typing.Any
    we: typing.Any
    ws: typing.Any
    normed: typing.Any
    vpre: typing.Any
    gate: typing.Any
    att: typing.Any
    hpre: typing.Any
    mid: typing.Any
    epre: typing.Any
    mpre: typing.Any
    dnorm: typing.Any
    probs: typing.Any
    lh: typing.Any
    ll: typing.Any
    th: typing.Any
    tl: typing.Any
    stage: typing.Any
    ends: typing.Any
    starts: typing.Any
    e_recv: typing.Any
    f_recv: typing.Any
    history: typing.Any
    wsem: typing.Any
    ssem: typing.Any
    send: typing.Any
    recv: typing.Any
    send2: typing.Any
    recv2: typing.Any


def kernel(seq, *refs):
    r = Refs(*refs)
    rows, width = r.x.shape
    seg_len = rows // SEG
    me_b, me = lax.axis_index("batch"), lax.axis_index("seq")
    nstate = 16
    hv = r.vpre.shape[1]
    ff = r.epre.shape[1]
    zd = r.qk.shape[1]
    group = r.probs.shape[1]
    groups = rows // group
    reset0 = width + zd
    cand0 = reset0 + hv
    scale = 1.0 / math.sqrt(zd)

    weights = [
        pltpu.make_async_copy(a, b, r.wsem.at[i])
        for i, (a, b) in enumerate(
            [
                (r.w_value, r.wv),
                (r.w_gates, r.wg),
                (r.w_output, r.wo),
                (r.w_expand, r.we),
                (r.w_shrink, r.ws),
            ]
        )
    ]
    for copy in weights:
        copy.start()

    barrier = pltpu.get_barrier_semaphore()

    def greet(k, _):
        pl.semaphore_signal(
            barrier, inc=1, device_id=(me_b, lax.rem(me + k, seq)), device_id_type=MESH
        )
        return 0

    lax.fori_loop(1, seq, greet, 0)

    gain0, shift0, gain1, shift1, omega, b_output, b_shrink = (
        r.gains[i : i + 1, :] for i in range(7)
    )
    decay, coef, dec_seg, dec_all = (r.tables.at[i] for i in range(4))

    def zero_small(i):
        r.s768[i : i + 1, :] = jnp.zeros((1, width), f32)

    for i in range(7):
        zero_small(i)

    def add768(i, value, cols=slice(None)):
        r.s768[i : i + 1, cols] += jnp.sum(value, axis=0, keepdims=True)

    RC = 32

    def norm_stats(value):
        centre = value - jnp.mean(value, axis=-1, keepdims=True)
        inv = lax.rsqrt(jnp.mean(centre * centre, axis=-1, keepdims=True) + 1e-05)
        return centre * inv, inv

    def norm_back(grad, n, inv):
        return inv * (
            grad
            - jnp.mean(grad, axis=-1, keepdims=True)
            - n * jnp.mean(grad * n, axis=-1, keepdims=True)
        )

    @pl.loop(0, rows // RC)
    def _(i):
        part = at(i, RC)
        n, _inv = norm_stats(r.x[part, :])
        value = n * gain0 + shift0
        row_set(r.normed, part, value)
        r.lh[part, :width], r.ll[part, :width] = split(value)

    def seg_rows(t):
        return pl.ds(t, SEG, stride=seg_len)

    def rows_of(ref, count, cols):
        return [jnp.broadcast_to(ref[n : n + 1, cols], (SEG, LANES)) for n in count]

    def end_states(source, reverse, target):
        @pl.loop(0, width // LANES)
        def _(d):
            cols = at(d, LANES)
            dec = rows_of(decay, range(nstate), cols)

            def turn(t, state):
                at_t = seg_len - 1 - t if reverse else t
                value = source[d, seg_rows(at_t), :]
                return tuple(a * s + value for a, s in zip(dec, state))

            zero = jnp.zeros((SEG, LANES), f32)
            state = lax.fori_loop(0, seg_len, turn, (zero,) * nstate, unroll=8)
            for n in range(nstate):
                target[d, n * SEG : (n + 1) * SEG, :] = state[n]

    def seg_of(k):
        return pl.ds(k, nstate, stride=SEG)

    def exchange(buffer, send_sem, recv_sem):
        def copy_to(k):
            peer = lax.rem(me + k, seq)
            return pltpu.make_async_remote_copy(
                src_ref=buffer.at[me],
                dst_ref=buffer.at[me],
                send_sem=send_sem.at[k],
                recv_sem=recv_sem.at[me],
                device_id=(me_b, peer),
                device_id_type=MESH,
            )

        def copy_from(k):
            peer = lax.rem(me + k, seq)
            return pltpu.make_async_remote_copy(
                src_ref=buffer.at[me],
                dst_ref=buffer.at[peer],
                send_sem=send_sem.at[k],
                recv_sem=recv_sem.at[peer],
                device_id=(me_b, peer),
                device_id_type=MESH,
            )

        def start():
            def one(k, _):
                copy_to(k).start()
                return 0

            lax.fori_loop(1, seq, one, 0)

        def wait():
            def one(k, _):
                copy_to(k).wait_send()
                copy_from(k).wait_recv()
                return 0

            lax.fori_loop(1, seq, one, 0)

        return start, wait

    end_states(r.normed, False, r.ends)
    total = jnp.zeros((nstate, width), f32)
    for k in range(SEG):
        total = r.sk[k] * total * dec_seg[...] + row_get(r.ends, seg_of(k))
    r.e_recv[me] = total
    pl.semaphore_wait(barrier, seq - 1)
    start_e, wait_e = exchange(r.e_recv, r.send, r.recv)
    start_e()

    weights[0].wait()

    @pl.loop(0, hv // TILE)
    def _(i):
        c = at(i, TILE)
        w = r.wv[:, c]
        r.vpre[:, c] = (
            dot(r.lh[:, :width], w) + dot(r.ll[:, :width], w) + r.b_value[:, c]
        )

    wait_e()

    def carry_step(k, carried):
        new = dec_all[...] * (r.pk[k] * carried) + r.e_recv[k]
        return jnp.where(k < me, new, carried)

    state = lax.fori_loop(0, seq, carry_step, jnp.zeros((nstate, width), f32))
    for k in range(SEG):
        state = r.sk[k] * state
        row_set(r.starts, seg_of(k), state)
        if k < SEG - 1:
            state = dec_seg[...] * state + row_get(r.ends, seg_of(k))

    @pl.loop(0, width // LANES)
    def _(d):
        cols = at(d, LANES)
        dec = rows_of(decay, range(nstate), cols)
        mix = rows_of(coef, range(nstate), cols)

        def turn(t, state):
            value = r.normed[d, seg_rows(t), :]
            state = tuple(a * s + value for a, s in zip(dec, state))
            terms = [m * s for m, s in zip(mix, state)]
            while len(terms) > 1:
                terms = [a + b for a, b in zip(terms[::2], terms[1::2])]
            r.mpre[d, seg_rows(t), :] = terms[0]
            return state

        first = tuple(r.starts[d, n * SEG : (n + 1) * SEG, :] for n in range(nstate))
        lax.fori_loop(0, seg_len, turn, first, unroll=4)

    @pl.loop(0, rows // RC)
    def _(i):
        part = at(i, RC)
        value = row_get(r.mpre, part) + omega * row_get(r.normed, part)
        row_set(r.mpre, part, value)
        r.lh[part, :width], r.ll[part, :width] = split(silu(value))

    weights[1].wait()

    def gate_tile(c):
        w = r.wg[:, c]
        r.gate[:, c] = (
            dot(r.lh[:, :width], w) + dot(r.ll[:, :width], w) + r.b_gates[:, c]
        )

    @pl.loop(0, width // TILE)
    def _(i):
        gate_tile(at(i, TILE))

    gate_tile(pl.ds(width, zd))

    @pl.loop(0, (hv + width) // TILE)
    def _(i):
        gate_tile(off(reset0, i, TILE))

    lag = lax.broadcasted_iota(jnp.int32, (group, group), 0) - lax.broadcasted_iota(
        jnp.int32, (group, group), 1
    )
    row_id = lax.broadcasted_iota(jnp.int32, (group, group), 0)
    causal = lag >= 0
    table = jnp.broadcast_to(r.bias_row[...], (group, group))
    for b in range(group.bit_length() - 1):
        moved = pltpu.roll(table, 1 << b, 1)
        table = jnp.where((row_id & (1 << b)) != 0, moved, table)
    q_gain, k_gain, q_shift = (r.qk[i : i + 1, :] for i in range(3))
    r.starts[0] = table

    @pl.loop(0, groups)
    def _(g):
        part = at(g, group)
        shared = silu(r.gate[part, width:reset0])
        q = split(shared * q_gain + q_shift)
        k = split(shared * k_gain)
        scores = dot3(q, k, NT) * scale + r.starts[0]
        scores = jnp.where(causal, scores, -1e30)
        p = jnp.exp(scores - jnp.max(scores, axis=-1, keepdims=True))
        p = p / jnp.sum(p, axis=-1, keepdims=True)
        r.probs[part, :] = p
        p = split(p)

        @pl.loop(0, hv // TILE)
        def _(i):
            c = at(i, TILE)
            v = split(silu(r.vpre[part, c]))
            attended = dot3(p, v)
            r.att[part, c] = attended
            gated = attended * silu(r.gate[part, off(reset0, i, TILE)])
            r.lh[part, c], r.ll[part, c] = split(gated)

    weights[2].wait()

    @pl.loop(0, width // TILE)
    def _(i):
        c = at(i, TILE)
        w = r.wo[:, c]
        value = (
            dot(r.lh[...], w)
            + dot(r.ll[...], w)
            + (r.gate[:, off(cand0, i, TILE)] + r.gains[5:6, c])
        )
        r.hpre[:, c] = value
        x = r.x[:, c]
        r.mid[:, c] = x + sigmoid(r.gate[:, c]) * (silu(value) - x)

    @pl.loop(0, rows // RC)
    def _(i):
        part = at(i, RC)
        n, _inv = norm_stats(r.mid[part, :])
        r.lh[part, :width], r.ll[part, :width] = split(n * gain1 + shift1)

    weights[3].wait()

    @pl.loop(0, ff // TILE)
    def _(i):
        c = at(i, TILE)
        w = r.we[:, c]
        r.epre[:, c] = (
            dot(r.lh[:, :width], w) + dot(r.ll[:, :width], w) + r.b_expand[:, c]
        )

    @pl.loop(0, ff // TILE)
    def _(i):
        c = at(i, TILE)
        r.lh[:, c], r.ll[:, c] = split(silu(r.epre[:, c]))

    weights[4].wait()

    @pl.loop(0, width // TILE)
    def _(i):
        c = at(i, TILE)
        w = r.ws[:, c]
        r.out[:, c] = r.mid[:, c] + (
            dot(r.lh[...], w) + dot(r.ll[...], w) + r.gains[6:7, c]
        )

    def transposed(source, count):
        @pl.loop(0, count // LANES)
        def _(i):
            value = source(i, at(i, LANES)).T
            here = at(i, LANES)
            r.th[here, :], r.tl[here, :] = split(value)

    def weight_grad(count, grad, target, tiles, first=0):
        def copy(i, slot):
            return pltpu.make_async_copy(
                r.stage.at[slot, pl.ds(0, count), :],
                target.at[:, off(first, i, TILE)],
                r.ssem.at[slot],
            )

        @pl.loop(0, tiles)
        def _(i):
            slot = lax.rem(i, 2)

            @pl.when(i >= 2)
            def _():
                copy(i - 2, slot).wait()

            g_high, g_low = split(grad(i))
            for k in range(count // TILE):
                here = slice(k * TILE, (k + 1) * TILE)
                a_high, a_low = r.th[here, :], r.tl[here, :]
                r.stage[slot, here, :] = dot3((a_high, a_low), (g_high, g_low))
            copy(i, slot).start()

        for i in range(max(tiles - 2, 0), tiles):
            copy(i, i % 2).wait()

    transposed(lambda i, c: silu(r.epre[:, c]), ff)
    weight_grad(ff, lambda i: r.cot[:, at(i, TILE)], r.dw_shrink, width // TILE)

    @pl.loop(0, rows // RC)
    def _(i):
        part = at(i, RC)
        value = r.cot[part, :]
        add768(6, value)
        r.lh[part, :width], r.ll[part, :width] = split(value)

    @pl.loop(0, ff // TILE)
    def _(i):
        c = at(i, TILE)
        w = r.ws[c, :]
        value = (dot(r.lh[:, :width], w, NT) + dot(r.ll[:, :width], w, NT)) * dsilu(
            r.epre[:, c]
        )
        r.epre[:, c] = value
        r.s_expand[:, c] = jnp.sum(value, axis=0, keepdims=True)

    @pl.loop(0, ff // TILE)
    def _(i):
        c = at(i, TILE)
        r.lh[:, c], r.ll[:, c] = split(r.epre[:, c])

    @pl.loop(0, rows // RC)
    def _(i):
        part = at(i, RC)
        n, _inv = norm_stats(r.mid[part, :])
        row_set(r.dnorm, part, n * gain1 + shift1)

    transposed(lambda i, c: r.dnorm[i], width)
    weight_grad(width, lambda i: r.epre[:, at(i, TILE)], r.dw_expand, ff // TILE)

    @pl.loop(0, width // TILE)
    def _(i):
        c = at(i, TILE)
        w = r.we[c, :]
        r.dx[:, c] = dot(r.lh[...], w, NT) + dot(r.ll[...], w, NT)

    @pl.loop(0, rows // RC)
    def _(i):
        part = at(i, RC)
        grad = r.dx[part, :]
        n, inv = norm_stats(r.mid[part, :])
        add768(2, grad * n)
        add768(3, grad)
        dmid = r.cot[part, :] + norm_back(grad * gain1, n, inv)
        update = sigmoid(r.gate[part, :width])
        pre = r.hpre[part, :]
        x = r.x[part, :]
        dhpre = dmid * update * dsilu(pre)
        r.dx[part, :] = dmid * (1.0 - update)
        dupdate = dmid * (silu(pre) - x) * (update * (1.0 - update))
        r.gate[part, :width] = dupdate
        r.gate[part, cand0:] = dhpre
        r.lh[part, :width], r.ll[part, :width] = split(dhpre)
        r.s_gates[:, :width] = (
            jnp.where(i == 0, 0.0, r.s_gates[:, :width])
            + jnp.sum(dupdate, axis=0, keepdims=True)
        )
        add768(5, dhpre)

    transposed(lambda i, c: r.att[:, c] * silu(r.gate[:, off(reset0, i, LANES)]), hv)
    weight_grad(hv, lambda i: r.gate[:, off(cand0, i, TILE)], r.dw_output, width // TILE)

    @pl.loop(0, hv // TILE)
    def _(i):
        c = at(i, TILE)
        w = r.wo[c, :]
        gated = dot(r.lh[:, :width], w, NT) + dot(r.ll[:, :width], w, NT)
        here = off(reset0, i, TILE)
        pre = r.gate[:, here]
        dreset = gated * r.att[:, c] * dsilu(pre)
        r.att[:, c] = gated * silu(pre)
        r.gate[:, here] = dreset
        r.s_gates[:, here] = jnp.sum(dreset, axis=0, keepdims=True)

    r.s_small[...] = jnp.zeros_like(r.s_small)
    r.starts[0] = jnp.zeros((group, group), f32)

    @pl.loop(0, groups)
    def _(g):
        part = at(g, group)
        p = r.probs[part, :]
        p_t = split(p.T)

        def value_tile(i, dp):
            c = at(i, TILE)
            pre = r.vpre[part, c]
            d_att = split(r.att[part, c])
            r.vpre[part, c] = dot3(p_t, d_att) * dsilu(pre)
            return dp + dot3(d_att, split(silu(pre)), NT)

        dp = lax.fori_loop(0, hv // TILE, value_tile, jnp.zeros((group, group), f32))
        ds = p * (dp - jnp.sum(dp * p, axis=-1, keepdims=True))
        r.starts[0] += ds
        ds = ds * scale
        pre = r.gate[part, width:reset0]
        shared = silu(pre)
        dq = dot3(split(ds), split(shared * k_gain))
        dk = dot3(split(ds.T), split(shared * q_gain + q_shift))
        for n, value in enumerate((dq * shared, dk * shared, dq)):
            r.s_small[n : n + 1, :] += jnp.sum(value, axis=0, keepdims=True)
        r.gate[part, width:reset0] = (dq * q_gain + dk * k_gain) * dsilu(pre)

    diagonals = r.starts[0]
    for b in range(group.bit_length() - 1):
        moved = pltpu.roll(diagonals, group - (1 << b), 1)
        diagonals = jnp.where((row_id & (1 << b)) != 0, moved, diagonals)
    r.s_small[3:4, :] = jnp.sum(diagonals, axis=0, keepdims=True)
    r.s_gates[:, width:reset0] = jnp.sum(r.gate[:, width:reset0], axis=0, keepdims=True)
    r.s_gates[:, cand0:] = r.s768[5:6, :]

    @pl.loop(0, hv // TILE)
    def _(i):
        c = at(i, TILE)
        value = r.vpre[:, c]
        r.s_value[:, c] = jnp.sum(value, axis=0, keepdims=True)
        r.lh[:, c], r.ll[:, c] = split(value)

    @pl.loop(0, width // TILE)
    def _(i):
        c = at(i, TILE)
        w = r.wv[c, :]
        col_set(r.dnorm, i, dot(r.lh[...], w, NT) + dot(r.ll[...], w, NT))

    transposed(lambda i, c: r.normed[i], width)
    weight_grad(width, lambda i: r.vpre[:, at(i, TILE)], r.dw_value, hv // TILE)

    transposed(lambda i, c: silu(r.mpre[i]), width)
    weight_grad(width, lambda i: r.gate[:, at(i, TILE)], r.dw_gates, width // TILE)
    weight_grad(
        width,
        lambda i: r.gate[:, off(reset0, i, TILE)],
        r.dw_gates,
        (hv + width) // TILE,
        reset0,
    )
    g_high, g_low = split(r.gate[:, width:reset0])
    for k in range(width // TILE):
        here = slice(k * TILE, (k + 1) * TILE)
        r.stage[0, here, :zd] = dot3((r.th[here, :], r.tl[here, :]), (g_high, g_low))
    shared_copy = pltpu.make_async_copy(
        r.stage.at[0, pl.ds(0, width), pl.ds(0, zd)],
        r.dw_gates.at[:, pl.ds(width, zd)],
        r.ssem.at[0],
    )
    shared_copy.start()

    def gate_section(start, size, first, last):
        @pl.loop(0, size // LANES)
        def _(i):
            c = at(i, LANES)
            r.lh[:, c], r.ll[:, c] = split(r.gate[:, off(start, i, LANES)])

        @pl.loop(0, width // TILE)
        def _(i):
            c = at(i, TILE)
            w = r.wg[c, start : start + size]
            value = dot(r.lh[:, :size], w, NT) + dot(r.ll[:, :size], w, NT)
            if not first:
                value += r.att[:, c]
            if last:
                value = value * dsilu(col_get(r.mpre, i))
                col_set(r.mpre, i, value)
                add768(4, value * col_get(r.normed, i), c)
                col_set(r.dnorm, i, col_get(r.dnorm, i) + r.gains[4:5, c] * value)
            else:
                r.att[:, c] = value

    shared_copy.wait()
    gate_section(0, reset0, True, False)
    gate_section(reset0, hv, False, False)
    gate_section(cand0, width, False, True)

    end_states(r.mpre, True, r.ends)
    adj = jnp.zeros((nstate, width), f32)
    for k in reversed(range(SEG)):
        if k < SEG - 1:
            adj = dec_seg[...] * (r.sk[k + 1] * adj)
        adj = adj + row_get(r.ends, seg_of(k))
    r.f_recv[me] = adj
    start_f, wait_f = exchange(r.f_recv, r.send2, r.recv2)
    start_f()

    state = lax.fori_loop(0, seq, carry_step, jnp.zeros((nstate, width), f32))
    wait_f()

    def adj_step(j, carried):
        k = seq - 1 - j
        new = r.kf[k] * r.f_recv[k] + dec_all[...] * (r.pk[k] * carried)
        return jnp.where(k > me, new, carried)

    adj = lax.fori_loop(0, seq, adj_step, jnp.zeros((nstate, width), f32))
    for k in reversed(range(SEG)):
        fresh = row_get(r.ends, seg_of(k))
        row_set(r.ends, seg_of(k), adj)
        if k > 0:
            adj = r.sk[k] * (dec_seg[...] * adj + fresh)

    end_states(r.normed, False, r.starts)
    for k in range(SEG):
        state = r.sk[k] * state
        fresh = row_get(r.starts, seg_of(k))
        row_set(r.starts, seg_of(k), state)
        state = dec_seg[...] * state + fresh

    half = nstate // 2
    for h in range(2):
        states = range(h * half, (h + 1) * half)

        @pl.loop(0, width // LANES)
        def _(d):
            cols = at(d, LANES)
            dec = rows_of(decay, states, cols)
            mix = rows_of(coef, states, cols)

            def ahead(t, state):
                value = r.normed[d, seg_rows(t), :]
                for n in range(half):
                    r.history[t, n * SEG : (n + 1) * SEG, :] = state[n]
                return tuple(a * s + value for a, s in zip(dec, state))

            first = tuple(r.starts[d, n * SEG : (n + 1) * SEG, :] for n in states)
            lax.fori_loop(0, seg_len, ahead, first, unroll=4)

            def back(j, carried):
                t = seg_len - 1 - j
                adj, p_sum, q_sum = carried
                grad = r.mpre[d, seg_rows(t), :]
                value = r.normed[d, seg_rows(t), :]
                adj = tuple(a * s + grad for a, s in zip(dec, adj))
                p_sum = tuple(p + a * value for p, a in zip(p_sum, adj))
                q_sum = tuple(
                    q + a * r.history[t, n * SEG : (n + 1) * SEG, :]
                    for n, (q, a) in enumerate(zip(q_sum, adj))
                )
                terms = [m * a for m, a in zip(mix, adj)]
                while len(terms) > 1:
                    terms = [a + b for a, b in zip(terms[::2], terms[1::2])]
                r.dnorm[d, seg_rows(t), :] += terms[0]
                return adj, p_sum, q_sum

            zero = (jnp.zeros((SEG, LANES), f32),) * half
            last = tuple(r.ends[d, n * SEG : (n + 1) * SEG, :] for n in states)
            _adj, p_sum, q_sum = lax.fori_loop(0, seg_len, back, (last, zero, zero), unroll=4)
            for n in range(half):
                row = 8 + h * half + n
                r.s768[row : row + 1, cols] = jnp.sum(p_sum[n], axis=0, keepdims=True)
                row = row + nstate
                r.s768[row : row + 1, cols] = jnp.sum(q_sum[n], axis=0, keepdims=True)

    @pl.loop(0, rows // RC)
    def _(i):
        part = at(i, RC)
        grad = row_get(r.dnorm, part)
        n, inv = norm_stats(r.x[part, :])
        add768(0, grad * n)
        add768(1, grad)
        r.dx[part, :] += norm_back(grad * gain0, n, inv)

    zero_small(7)


def layer(x, cot, sk, pk, kf, tables, gains, weights, biases, qk, bias_row, seq):
    rows, width = x.shape
    w_value, w_gates, w_output, w_expand, w_shrink = weights
    hv, gates, ff = w_value.shape[1], w_gates.shape[1], w_expand.shape[1]
    zd, group = qk.shape[1], bias_row.shape[1]
    nstate = tables.shape[1]
    vmem = pl.BlockSpec(memory_space=pltpu.VMEM)
    smem = pl.BlockSpec(memory_space=pltpu.SMEM)
    hbm = pl.BlockSpec(memory_space=pl.ANY)

    def shape(*dims, kind=f32):
        return jax.ShapeDtypeStruct(dims, kind)

    return pl.pallas_call(
        functools.partial(kernel, seq),
        out_shape=(
            shape(rows, width),
            shape(rows, width),
            shape(width, hv),
            shape(width, gates),
            shape(hv, width),
            shape(width, ff),
            shape(ff, width),
            shape(8 + 2 * nstate, width),
            shape(1, hv),
            shape(1, ff),
            shape(1, gates),
            shape(8, zd),
        ),
        in_specs=[vmem, vmem, smem, smem, smem, vmem, vmem] + [hbm] * 5 + [vmem] * 5,
        out_specs=(vmem, vmem, hbm, hbm, hbm, hbm, hbm, vmem, vmem, vmem, vmem, vmem),
        scratch_shapes=[
            pltpu.VMEM(w_value.shape, bf16),
            pltpu.VMEM(w_gates.shape, bf16),
            pltpu.VMEM(w_output.shape, bf16),
            pltpu.VMEM(w_expand.shape, bf16),
            pltpu.VMEM(w_shrink.shape, bf16),
            pltpu.VMEM((width // LANES, rows, LANES), f32),
            pltpu.VMEM((rows, hv), f32),
            pltpu.VMEM((rows, gates), f32),
            pltpu.VMEM((rows, hv), f32),
            pltpu.VMEM((rows, width), f32),
            pltpu.VMEM((rows, width), f32),
            pltpu.VMEM((rows, ff), f32),
            pltpu.VMEM((width // LANES, rows, LANES), f32),
            pltpu.VMEM((width // LANES, rows, LANES), f32),
            pltpu.VMEM((rows, group), f32),
            pltpu.VMEM((rows, max(hv, ff)), bf16),
            pltpu.VMEM((rows, max(hv, ff)), bf16),
            pltpu.VMEM((max(hv, ff), rows), bf16),
            pltpu.VMEM((max(hv, ff), rows), bf16),
            pltpu.VMEM((2, max(hv, ff), TILE), f32),
            pltpu.VMEM((width // LANES, nstate * SEG, LANES), f32),
            pltpu.VMEM((width // LANES, nstate * SEG, LANES), f32),
            pltpu.VMEM((seq, nstate, width), f32),
            pltpu.VMEM((seq, nstate, width), f32),
            pltpu.VMEM((rows // SEG, nstate // 2 * SEG, LANES), f32),
            pltpu.SemaphoreType.DMA((5,)),
            pltpu.SemaphoreType.DMA((2,)),
            pltpu.SemaphoreType.DMA((seq,)),
            pltpu.SemaphoreType.DMA((seq,)),
            pltpu.SemaphoreType.DMA((seq,)),
            pltpu.SemaphoreType.DMA((seq,)),
        ],
        compiler_params=pltpu.CompilerParams(
            collective_id=0, has_side_effects=True, vmem_limit_bytes=63 << 20
        ),
        cost_estimate=pl.CostEstimate(
            flops=52_000_000_000, bytes_accessed=60_000_000, transcendentals=20_000_000
        ),
    )(
        x, cot, sk, pk, kf, tables, gains, *weights, *biases, qk, bias_row
    )


def shards(
    seq,
    tokens,
    lengths,
    cotangent,
    norm_gain,
    norm_shift,
    alpha_logit,
    delta_logit,
    ema_beta,
    ema_eta,
    ema_omega,
    w_value,
    b_value,
    w_gates,
    b_gates,
    query_key,
    position_bias,
    w_output,
    b_output,
    w_expand,
    b_expand,
    w_shrink,
    b_shrink,
):
    rows, width = tokens.shape[1:]
    group = position_bias.shape[0]
    blocks = rows // group
    me = lax.axis_index("seq")

    alpha = jax.nn.sigmoid(alpha_logit).T
    damping = jax.nn.sigmoid(delta_logit).T
    beta, eta = ema_beta.T, ema_eta.T
    inflow = alpha * beta
    log_decay = jnp.log1p(-alpha * damping)
    tables = jnp.stack(
        [
            jnp.exp(log_decay),
            inflow * eta,
            jnp.exp((rows // SEG) * log_decay),
            jnp.exp(rows * log_decay),
        ]
    )
    ids = jnp.arange(seq * blocks)
    first_end = lengths[0, 0]
    second_end = first_end + lengths[0, 1]
    keep = 1.0 - ((ids == 0) | (ids == first_end) | (ids == second_end)).astype(f32)
    keep = keep.reshape(seq, blocks)
    mine = lax.dynamic_index_in_dim(keep, me, 0, keepdims=False)
    sk = jnp.ones((blocks, SEG // blocks), f32).at[:, 0].set(mine).reshape(SEG)
    gains = jnp.stack(
        [
            norm_gain[:, 0],
            norm_shift[:, 0],
            norm_gain[:, 1],
            norm_shift[:, 1],
            ema_omega,
            b_output,
            b_shrink,
            jnp.zeros_like(b_shrink),
        ]
    )
    outs = layer(
        tokens[0],
        cotangent[0],
        sk,
        jnp.prod(keep, axis=1),
        keep[:, 0],
        tables,
        gains,
        (w_value, w_gates, w_output, w_expand, w_shrink),
        (b_value[None], b_gates[None], b_expand[None]),
        query_key.T,
        jnp.roll(position_bias[::-1], 1)[None],
        seq,
    )
    output, grad_tokens = outs[:2]
    summed = lax.psum(outs[2:], ("batch", "seq"))
    dw_value, dw_gates, dw_output, dw_expand, dw_shrink, s768, s_value, s_expand, s_gates, small = (
        summed
    )
    nstate = alpha.shape[0]
    p_sum, q_sum = s768[8 : 8 + nstate], s768[8 + nstate : 8 + 2 * nstate]
    d_inflow = eta * p_sum
    d_eta = inflow * p_sum
    d_decay = eta * inflow * q_sum
    d_alpha = d_inflow * beta - d_decay * damping
    return (
        output[None],
        grad_tokens[None],
        jnp.stack([s768[0], s768[2]], axis=1),
        jnp.stack([s768[1], s768[3]], axis=1),
        (d_alpha * alpha * (1.0 - alpha)).T,
        (-d_decay * alpha * damping * (1.0 - damping)).T,
        (d_inflow * alpha).T,
        d_eta.T,
        s768[4],
        dw_value,
        s_value[0],
        dw_gates,
        s_gates[0],
        small[:3].T,
        jnp.roll(small[3][::-1], 1),
        dw_output,
        s768[5],
        dw_expand,
        s_expand[0],
        dw_shrink,
        s768[6],
    )


def solution(mesh):
    token_spec = P("batch", "seq", None)
    return jax.shard_map(
        functools.partial(shards, mesh.shape["seq"]),
        mesh=mesh,
        in_specs=(token_spec, P("batch", None), token_spec) + (P(),) * 19,
        out_specs=(token_spec, token_spec) + (P(),) * 19,
        check_vma=False,
    )
```

time: 1860 us -> 683 us (0.37)
  matrix products: 534 us -> 0 us
  local copies, waits for them, and re-layouts: 401 us -> 34.9 us
  other arithmetic: 313 us -> 8.1 us
  Pallas kernels: 0 us -> 180 us
  blocking collectives: 209 us -> 43.2 us
  waiting for transfers between devices: 371 us -> 401 us
    dot_general x34 -> x0, matrix products: 534 us -> none  [the longest x3 214 us: gated_mixer(): within = jnp.einsum('tsd,csd->ctd', tables[0], blocks, precision=highest)]
    psum x1, waiting for transfers between devices: 0.02 us -> 401 us  [shards(): summed = lax.psum(outs[2:], ('batch', 'seq'))]
    reduce_scatter x5 -> x0, waiting for transfers between devices: 254 us -> none  [the longest x1 104 us: shards(): lax.psum_scatter(totals['w_gates'], 'seq', scatter_dimension=0, tiled=True)]
    scatter-add x2 -> x0, other arithmetic: 223 us -> none  [the longest x1 114 us: group_attention(): bias_table = position_bias[jnp.clip(lag_grid, 0, group_len - 1)]]
    gather x4 -> x0, local copies, waits for them, and re-layouts: 216 us -> none  [the longest x2 118 us: ema_tables(): lag_kernel[jnp.clip(lag_grid, 0, group_len - 1)]]
    pallas_call x0 -> x1, Pallas kernels: none -> 180 us  [layer(): pl.pallas_call(functools.partial(kernel, seq), out_shape=(shape(rows, wid...]
    all_gather x10 -> x0, blocking collectives: 145 us -> none  [the longest x3 48.7 us: carried_in_2(): everything = jax.tree.map(lambda part: lax.all_gather(part, axis), array)]
    all_gather x5 -> x0, waiting for transfers between devices: 114 us -> none  [the longest x1 94.4 us: shards(): lax.all_gather(summed[9], 'seq', axis=0, tiled=True)]
  transfers between devices with their start and end apart: 18 -> 1, of which waited for: 6 -> 1; matrix products, arithmetic and copies ran while one was open for 40% -> 0% of each run, Pallas kernels for 0% -> 0%
where the time goes in v1:
time: 683 us; the launch traced here: 682 us
  waiting for transfers between devices  401 us (59%)
  Pallas kernels  180 us (26%)
  blocking collectives  43.2 us (6%)
  local copies, waits for them, and re-layouts  34.9 us (5%)
  between operations  15.5 us (2%)
  other arithmetic  8.1 us (1%)
    psum x1, waiting for transfers between devices, shards(): summed = lax.psum(outs[2:], ('batch', 'seq'))  401 us
    pallas_call x1, Pallas kernels, layer(): pl.pallas_call(functools.partial(kernel, seq), out_shape=(shape(rows, wid...  180 us
    psum x1, blocking collectives, shards(): summed = lax.psum(outs[2:], ('batch', 'seq'))  43.2 us
    unnamed x40, local copies, waits for them, and re-layouts  21.2 us
  transfers between devices with their start and end apart: 1, of which 1 were waited for; matrix products, arithmetic and copies ran while one was open for 0% of the time, Pallas kernels for 0%

profile of v1, /device:TPU:1, one launch (start us, length us, event | category | flops | bytes accessed | tf_op | source)
XLA Modules:
  0.0 681.9 jit_solution(16038034795325257776)
XLA Ops:
  7.2 0.0 all-reduce.5.cloned.1.call-start
  7.2 0.7 slice.104
  8.0 0.1 slice.105
  8.1 1.3 fusion.15
  10.7 1.2 convert_subtract_fusion
  11.9 0.5 slice_bitcast_fusion.10.refs_4_
  12.4 0.2 dynamic-slice_reduce_fusion
  12.6 0.1 copy.45
  12.7 0.6 reshape.82.refs_2_
  13.3 0.7 stack.38
  13.9 0.7 stack.39
  14.6 0.7 stack.40
  15.3 1.3 broadcast_in_dim.18.refs_12_
  16.6 1.3 broadcast_in_dim.20.refs_14_
  17.9 1.3 broadcast_in_dim.19.refs_13_
  19.2 1.2 maximum_bitcast_fusion.refs_16_
  20.5 0.8 slice_bitcast_fusion.4
  21.3 0.9 exponential_bitcast_fusion.2
  22.2 0.7 pad_maximum_fusion.refs_5_
  22.9 0.6 stack.41.refs_6_
  23.6 179.6 %shard_map.373 = (f32[512,768]{1,0:T(8,128)}, f32[512,768]{1,0:T(8,128)}, f32[768,1536]{1,0:T(8,128)}, f32[768,3200]{1,0:T(8,128)}, f32[1536,768]{1,0:T(8,128)},...) custom-call(f32[512,768]{1,0:T(8,128)} %bitcast.143, ...), custom_call_target="tpu_custom_call" | custom-call | flops 51999997952 | bytes 60000000 | tf_op jit(solution)/shard_map/pallas_call | solution.py:750
  203.2 0.0 copy-start.4
  203.2 0.0 copy-start.5
  203.2 0.0 copy-start.6
  203.2 0.0 copy-start.7
  203.3 0.0 all-reduce.5.cloned.1.call-update
  203.3 0.6 copy-done.10
  204.0 43.2 %all-reduce.1 = (f32[1536]{0:T(1024)}, f32[3200]{0:T(1024)}, f32[8,128]{1,0:T(8,128)S(1)}, f32[1536]{0:T(1024)}) all-reduce(f32[1536]{0:T(1024)S(1)} %reduce.4, f32[3200]{0:T(1024)S(1)} %reduce.5, f32[8,128]{1,0:T(8,128)S(1)} %copy-done.11, f32[1536]{0:T(1024)S(1)} %reduce.7), channel_id=1, replica_groups=mesh['batch'=4,'seq'=8] {'batch','seq'}, use_global_device_ids=true, to_apply=%region_3.4 | all-reduce | flops 7296 | bytes 58368 | tf_op jit(solution)/shard_map/psum | solution.py:889
  247.2 0.5 slice.114
  247.7 0.1 slice_bitcast_fusion.9
  247.8 0.1 slice.118
  247.9 1.2 pad_maximum_fusion.3
  249.1 0.6 slice_bitcast_fusion.8
  249.7 400.5 %all-reduce.5.cloned.1.call-done = (f32[40,768]{1,0:T(8,128)}, f32[768,1536]{1,0:T(8,128)}, f32[768,3200]{1,0:T(8,128)}, f32[1536,768]{1,0:T(8,128)}, f32[768,1536]{1,0:T(8,128)}, /*index=5*/f32[1536,768]{1,0:T(8,128)}) async-done(((f32[40,768]{1,0:T(8,128)}, f32[768,1536]{1,0:T(8,128)}, f32[768,3200]{1,0:T(8,128)}, f32[1536,768]{1,0:T(8,128)}, f32[768,1536]{1,0:T(8,128)}, ...) | async-done | bytes 28827664 | tf_op jit(solution)/shard_map/psum | solution.py:889
  650.2 1.6 slice_reduce_fusion
  651.8 0.0 copy-done.6
  651.9 1.5 fusion.6
  653.4 0.6 pad_maximum_fusion.2
  654.0 0.6 pad_maximum_fusion.1
  654.6 1.1 copy.59
  655.7 0.0 copy-done.2
  655.7 1.1 copy.60
  656.9 2.4 copy.61
  659.3 2.5 copy-done
  661.8 3.9 copy.62
  665.7 5.0 copy.63
  670.7 2.2 copy.64
  672.9 2.2 copy.65
  (31 shorter events, 0.1 us)
Async XLA Ops:
  7.2 643.0 %all-reduce.5.cloned.1.call-start = ((), (), s32[]{:S(2)}) async-start(), calls=%async_computation | async-start | bytes 57655296 | tf_op jit(solution)/shard_map/psum | solution.py:889
  203.2 0.7 copy-start.10
  203.2 0.7 copy-start.9
  203.2 0.7 copy-start.8
  203.2 0.8 copy-start.11
  203.2 448.6 %copy-start.4 = (f32[768,16]{0,1:T(8,128)S(1)}, f32[768,16]{0,1:T(8,128)}, u32[]{:S(2)}) copy-start(f32[768,16]{0,1:T(8,128)} %param.30) | copy-start | bytes 147460
  203.2 448.6 %copy-start.5 = (f32[768,16]{0,1:T(8,128)S(1)}, f32[768,16]{0,1:T(8,128)}, u32[]{:S(2)}) copy-start(f32[768,16]{0,1:T(8,128)} %param.29) | copy-start | bytes 147460
  203.2 448.6 %copy-start.6 = (f32[768,16]{0,1:T(8,128)S(1)}, f32[768,16]{0,1:T(8,128)}, u32[]{:S(2)}) copy-start(f32[768,16]{0,1:T(8,128)} %param.32) | copy-start | bytes 147460
  203.2 448.6 %copy-start.7 = (f32[768,16]{0,1:T(8,128)S(1)}, f32[768,16]{0,1:T(8,128)}, u32[]{:S(2)}) copy-start(f32[768,16]{0,1:T(8,128)} %param.31) | copy-start | bytes 147460
  203.3 451.3 %copy-start.3 = (f32[512,768]{1,0:T(8,128)S(1)}, f32[512,768]{1,0:T(8,128)}, u32[]{:S(2)}) copy-start(f32[512,768]{1,0:T(8,128)} %get-tuple-element.45) | copy-start | bytes 4718596
  203.3 452.5 %copy-start.2 = (f32[512,768]{1,0:T(8,128)S(1)}, f32[512,768]{1,0:T(8,128)}, u32[]{:S(2)}) copy-start(f32[512,768]{1,0:T(8,128)} %get-tuple-element.46) | copy-start | bytes 4718596
  650.2 6.7 copy-start.1
  655.7 6.1 copy-start
  656.9 13.8 %slice-start.2 = ((s8[4718592]{0:T(1024)(128)(4,1)}), s8[4194304]{0:T(1024)(128)(4,1)S(1)}, s32[]{:S(2)}) async-start(s8[4718592]{0:T(1024)(128)(4,1)} %bitcast.138), calls=%async_computation.3 | async-start | bytes 8388608
  661.8 8.9 %slice-start.3 = ((s8[4718592]{0:T(1024)(128)(4,1)}), s8[524288]{0:T(1024)(128)(4,1)S(1)}, s32[]{:S(2)}) async-start(s8[4718592]{0:T(1024)(128)(4,1)} %bitcast.138), calls=%async_computation.4 | async-start | bytes 1048576
  665.7 7.2 %slice-start = ((s8[4718592]{0:T(1024)(128)(4,1)}), s8[4194304]{0:T(1024)(128)(4,1)S(1)}, s32[]{:S(2)}) async-start(s8[4718592]{0:T(1024)(128)(4,1)} %bitcast.136), calls=%async_computation.1 | async-start | bytes 8388608
  670.7 2.2 slice-start.1
Sparse Core Ops, SparseCore 0:
  203.4 446.7 all-reduce.4

commit v2 on v1

--- a/solution.py
+++ b/solution.py
@@ -75,6 +75,233 @@
 
 def off(start, i, size):
     return pl.ds(pl.multiple_of(start + i * size, LANES), size)
+
+
+def bit_of(bit):
+    name, step = bit
+    return lax.rem(lax.div(lax.axis_index(name), step), 2)
+
+
+def partner(bit):
+    name, step = bit
+    where = {"batch": lax.axis_index("batch"), "seq": lax.axis_index("seq")}
+    where[name] = where[name] + step * (1 - 2 * bit_of(bit))
+    return (where["batch"], where["seq"])
+
+
+HALVINGS = 5
+BLOCK = 768
+TILES = 2
+
+
+def slot_count(seq):
+    return 8 if seq <= 16 else 4
+
+
+def bits_of(batch, seq):
+    chips = [("batch", 1 << k) for k in range(batch.bit_length() - 1)]
+    line = [("seq", 1 << k) for k in range(1, seq.bit_length() - 1)]
+    return ("seq", 1), chips, line
+
+
+def stage_orders(batch, seq):
+    core, chips, line = bits_of(batch, seq)
+    flipped = chips[::-1]
+    return (
+        [core] + chips + line,
+        [core] + flipped + line,
+        [core] + line + chips,
+        [core] + line + flipped,
+    )
+
+
+def stage_rows(count):
+    return [BLOCK >> (min(s, HALVINGS - 1) + 1) for s in range(count)]
+
+
+class Reducer:
+    def __init__(self, orders, slots, kinds, subs, tile, red, gathered, sems):
+        self.slots = slots
+        self.orders, self.kinds, self.subs = orders, kinds, subs
+        self.tile, self.red, self.gathered = tile, red, gathered
+        self.send, self.recv, self.credit, self.local, self.gsend, self.grecv = sems
+        self.stages = len(orders[0])
+        self.halvings = min(HALVINGS, self.stages)
+        self.rows = stage_rows(self.stages)
+        self.jobs = len(subs)
+        self.first = [sum(subs[:j]) for j in range(self.jobs)]
+        self.now = 0.0
+        self.free = {}
+        self.due = {}
+        self.done = [-1] * self.jobs
+
+    def order(self, j):
+        return self.orders[self.kinds[j]]
+
+    def part(self, ref, slot, j, start, size):
+        if not isinstance(start, int):
+            start = pl.multiple_of(start, 8)
+        return ref.at[slot, pl.ds(0, self.subs[j]), pl.ds(start, size), :]
+
+    def held(self, j, s):
+        if s < 0:
+            return self.tile, j % TILES, BLOCK
+        return self.red[s], j % self.slots, self.rows[s]
+
+    def keep_start(self, j, s):
+        return bit_of(self.order(j)[s]) * self.rows[s] if s < self.halvings else 0
+
+    def give_start(self, j, s):
+        return (1 - bit_of(self.order(j)[s])) * self.rows[s] if s < self.halvings else 0
+
+    def scatter_copy(self, j, s):
+        ref, slot, _rows = self.held(j, s - 1)
+        into, into_slot, rows = self.held(j, s)
+        return pltpu.make_async_remote_copy(
+            src_ref=self.part(ref, slot, j, self.give_start(j, s), rows),
+            dst_ref=self.part(into, into_slot, j, 0, rows),
+            send_sem=self.send.at[s, into_slot],
+            recv_sem=self.recv.at[s, into_slot],
+            device_id=partner(self.order(j)[s]),
+            device_id_type=MESH,
+        )
+
+    def owned(self, j, s, flip=False):
+        start = 0
+        for t in range(s + 1):
+            bit = bit_of(self.order(j)[t])
+            if flip and t == s:
+                bit = 1 - bit
+            start = start + bit * self.rows[t]
+        return self.gathered.at[
+            pl.ds(self.first[j], self.subs[j]), pl.ds(pl.multiple_of(start, 8), self.rows[s]), :
+        ]
+
+    def final(self, j):
+        ref, slot, rows = self.held(j, self.stages - 1)
+        return self.part(ref, slot, j, 0, rows)
+
+    def gather_copy(self, j, s, arriving=False):
+        last = s == self.halvings - 1
+        return pltpu.make_async_remote_copy(
+            src_ref=self.final(j) if last else self.owned(j, s),
+            dst_ref=self.owned(j, s, flip=arriving),
+            send_sem=self.gsend.at[j, s],
+            recv_sem=self.grecv.at[j, s],
+            device_id=partner(self.order(j)[s]),
+            device_id_type=MESH,
+        )
+
+    def local_copy(self, j):
+        return pltpu.make_async_copy(
+            self.final(j), self.owned(j, self.halvings - 1), self.local.at[j]
+        )
+
+    def arrival(self, j, s):
+        name, step = self.order(j)[s]
+        rows = self.rows[s] * self.subs[j]
+        size = rows * TILE * 4e-6
+        if (name, step) == ("seq", 1):
+            link, cost = "core", size / 0.6
+        else:
+            link = name + (str(step) if name == "batch" else "")
+            cost = 2 * size / 0.09 * (step // 2 if name == "seq" else 1)
+        start = max(self.now, self.free.get(link, 0.0))
+        self.free[link] = start + cost
+        return start + cost + 2.0
+
+    def advance(self, us):
+        self.now += us
+
+    def set_due(self, j, event, when):
+        self.due[j] = (event, when)
+
+    def run(self, j):
+        event, when = self.due.pop(j)
+        self.now = max(self.now, when)
+        n = self.stages
+        if event < n:
+            s = event
+            copy = self.scatter_copy(j, s)
+            copy.wait_send()
+            copy.wait_recv()
+            self.add(j, s)
+            if s > 0:
+                self.give_credit(j, s - 1)
+            if s < n - 1:
+                self.start_scatter(j, s + 1)
+            else:
+                self.local_copy(j).start()
+                self.gather_copy(j, self.halvings - 1).start()
+                self.set_due(j, event + 1, self.arrival(j, self.halvings - 1))
+        else:
+            s = self.halvings - 1 - (event - n)
+            self.gather_copy(j, s, True).wait_recv()
+            if s == self.halvings - 1:
+                self.gather_copy(j, s).wait_send()
+                self.local_copy(j).wait()
+                self.give_credit(j, n - 1)
+            if s > 0:
+                self.gather_copy(j, s - 1).start()
+                self.set_due(j, event + 1, self.arrival(j, s - 1))
+        self.done[j] = event
+        self.now += 0.5
+
+    def add(self, j, s):
+        ref, slot, _rows = self.held(j, s - 1)
+        into, into_slot, rows = self.held(j, s)
+        start = self.keep_start(j, s)
+        step = min(48, rows)
+
+        @pl.loop(0, rows // step)
+        def _(i):
+            for b in range(self.subs[j]):
+                here = pl.ds(pl.multiple_of(start + i * step, 8), step)
+                there = pl.ds(pl.multiple_of(i * step, 8), step)
+                into[into_slot, b, there, :] += ref[slot, b, here, :]
+
+    def give_credit(self, j, s):
+        if j + self.slots < self.jobs:
+            pl.semaphore_signal(
+                self.credit.at[s, j % self.slots],
+                inc=1,
+                device_id=partner(self.order(j + self.slots)[s]),
+                device_id_type=MESH,
+            )
+
+    def start_scatter(self, j, s):
+        if j >= self.slots:
+            self.reach(j - self.slots, s + 1)
+            pl.semaphore_wait(self.credit.at[s, j % self.slots], 1)
+        self.scatter_copy(j, s).start()
+        self.set_due(j, s, self.arrival(j, s))
+
+    def reach(self, j, event):
+        while self.done[j] < event:
+            self.run(j)
+
+    def acquire(self, j):
+        if j >= TILES:
+            self.reach(j - TILES, 0)
+        return j % TILES
+
+    def produced(self, j):
+        self.start_scatter(j, 0)
+
+    def tick(self, us=0.0):
+        self.advance(us)
+        while self.due:
+            j = min(self.due, key=lambda k: self.due[k][1])
+            if self.due[j][1] > self.now:
+                break
+            self.run(j)
+
+    def drain(self):
+        while self.due:
+            self.run(min(self.due, key=lambda k: self.due[k][1]))
+        for j in range(self.jobs):
+            for s in range(self.halvings - 1):
+                self.gather_copy(j, s).wait_send()
 
 
 class Refs(typing.NamedTuple):
@@ -97,21 +324,10 @@
     bias_row: typing.Any
     out: typing.Any
     dx: typing.Any
-    dw_value: typing.Any
-    dw_gates: typing.Any
-    dw_output: typing.Any
-    dw_expand: typing.Any
-    dw_shrink: typing.Any
-    s768: typing.Any
-    s_value: typing.Any
-    s_expand: typing.Any
-    s_gates: typing.Any
-    s_small: typing.Any
-    wv: typing.Any
+    gathered: typing.Any
+    wa: typing.Any
+    wb: typing.Any
     wg: typing.Any
-    wo: typing.Any
-    we: typing.Any
-    ws: typing.Any
     normed: typing.Any
     vpre: typing.Any
     gate: typing.Any
@@ -126,22 +342,28 @@
     ll: typing.Any
     th: typing.Any
     tl: typing.Any
-    stage: typing.Any
+    s768: typing.Any
+    s_value: typing.Any
+    s_expand: typing.Any
+    s_gates: typing.Any
+    s_small: typing.Any
     ends: typing.Any
     starts: typing.Any
     e_recv: typing.Any
     f_recv: typing.Any
-    history: typing.Any
     wsem: typing.Any
-    ssem: typing.Any
     send: typing.Any
     recv: typing.Any
     send2: typing.Any
     recv2: typing.Any
-
-
-def kernel(seq, *refs):
-    r = Refs(*refs)
+    tile: typing.Any
+    sems: typing.Any
+    red: typing.Any
+
+
+def kernel(batch, seq, plan, *refs):
+    n = len(Refs._fields) - 2
+    r = Refs(*refs[:n], refs[n : n + 6], refs[n + 6 :])
     rows, width = r.x.shape
     seg_len = rows // SEG
     me_b, me = lax.axis_index("batch"), lax.axis_index("seq")
@@ -155,20 +377,19 @@
     cand0 = reset0 + hv
     scale = 1.0 / math.sqrt(zd)
 
+    sources = (r.w_value, r.w_gates, r.w_output, r.w_expand, r.w_shrink, r.w_output, r.w_value)
+    places = (r.wa, r.wg, r.wb, r.wa, r.wb, r.wb, r.wa)
     weights = [
-        pltpu.make_async_copy(a, b, r.wsem.at[i])
-        for i, (a, b) in enumerate(
-            [
-                (r.w_value, r.wv),
-                (r.w_gates, r.wg),
-                (r.w_output, r.wo),
-                (r.w_expand, r.we),
-                (r.w_shrink, r.ws),
-            ]
-        )
+        pltpu.make_async_copy(a, b, r.wsem.at[i]) for i, (a, b) in enumerate(zip(sources, places))
     ]
-    for copy in weights:
+    for copy in weights[:3]:
         copy.start()
+
+    kinds, subs = plan
+    comm = Reducer(
+        stage_orders(batch, seq), slot_count(seq), kinds, subs, r.tile, r.red, r.gathered, r.sems
+    )
+    _core, chips, _line = bits_of(batch, seq)
 
     barrier = pltpu.get_barrier_semaphore()
 
@@ -179,6 +400,8 @@
         return 0
 
     lax.fori_loop(1, seq, greet, 0)
+    for bit in chips:
+        pl.semaphore_signal(barrier, inc=1, device_id=partner(bit), device_id_type=MESH)
 
     gain0, shift0, gain1, shift1, omega, b_output, b_shrink = (
         r.gains[i : i + 1, :] for i in range(7)
@@ -188,7 +411,7 @@
     def zero_small(i):
         r.s768[i : i + 1, :] = jnp.zeros((1, width), f32)
 
-    for i in range(7):
+    for i in range(8):
         zero_small(i)
 
     def add768(i, value, cols=slice(None)):
@@ -286,7 +509,7 @@
     for k in range(SEG):
         total = r.sk[k] * total * dec_seg[...] + row_get(r.ends, seg_of(k))
     r.e_recv[me] = total
-    pl.semaphore_wait(barrier, seq - 1)
+    pl.semaphore_wait(barrier, seq - 1 + len(chips))
     start_e, wait_e = exchange(r.e_recv, r.send, r.recv)
     start_e()
 
@@ -295,10 +518,12 @@
     @pl.loop(0, hv // TILE)
     def _(i):
         c = at(i, TILE)
-        w = r.wv[:, c]
+        w = r.wa[:, c]
         r.vpre[:, c] = (
             dot(r.lh[:, :width], w) + dot(r.ll[:, :width], w) + r.b_value[:, c]
         )
+
+    weights[3].start()
 
     wait_e()
 
@@ -395,7 +620,7 @@
     @pl.loop(0, width // TILE)
     def _(i):
         c = at(i, TILE)
-        w = r.wo[:, c]
+        w = r.wb[:, c]
         value = (
             dot(r.lh[...], w)
             + dot(r.ll[...], w)
@@ -405,6 +630,8 @@
         x = r.x[:, c]
         r.mid[:, c] = x + sigmoid(r.gate[:, c]) * (silu(value) - x)
 
+    weights[4].start()
+
     @pl.loop(0, rows // RC)
     def _(i):
         part = at(i, RC)
@@ -416,7 +643,7 @@
     @pl.loop(0, ff // TILE)
     def _(i):
         c = at(i, TILE)
-        w = r.we[:, c]
+        w = r.wa[:, c]
         r.epre[:, c] = (
             dot(r.lh[:, :width], w) + dot(r.ll[:, :width], w) + r.b_expand[:, c]
         )
@@ -431,46 +658,54 @@
     @pl.loop(0, width // TILE)
     def _(i):
         c = at(i, TILE)
-        w = r.ws[:, c]
+        w = r.wb[:, c]
         r.out[:, c] = r.mid[:, c] + (
             dot(r.lh[...], w) + dot(r.ll[...], w) + r.gains[6:7, c]
         )
 
-    def transposed(source, count):
+    comm.advance(56.0)
+
+    def transposed(source, count, first=0):
         @pl.loop(0, count // LANES)
         def _(i):
-            value = source(i, at(i, LANES)).T
-            here = at(i, LANES)
-            r.th[here, :], r.tl[here, :] = split(value)
-
-    def weight_grad(count, grad, target, tiles, first=0):
-        def copy(i, slot):
-            return pltpu.make_async_copy(
-                r.stage.at[slot, pl.ds(0, count), :],
-                target.at[:, off(first, i, TILE)],
-                r.ssem.at[slot],
-            )
-
-        @pl.loop(0, tiles)
-        def _(i):
-            slot = lax.rem(i, 2)
-
-            @pl.when(i >= 2)
-            def _():
-                copy(i - 2, slot).wait()
-
-            g_high, g_low = split(grad(i))
-            for k in range(count // TILE):
-                here = slice(k * TILE, (k + 1) * TILE)
-                a_high, a_low = r.th[here, :], r.tl[here, :]
-                r.stage[slot, here, :] = dot3((a_high, a_low), (g_high, g_low))
-            copy(i, slot).start()
-
-        for i in range(max(tiles - 2, 0), tiles):
-            copy(i, i % 2).wait()
+            here = off(first, i, LANES)
+            r.th[here, :], r.tl[here, :] = split(source(i, at(i, LANES)).T)
+
+    def products(j, pairs):
+        slot = comm.acquire(j)
+        for b, (first, grad) in enumerate(pairs):
+            g = split(grad)
+            cols = grad.shape[1]
+
+            @pl.loop(0, BLOCK // TILE)
+            def _(k):
+                a = off(first, k, TILE)
+                value = dot3((r.th[a, :], r.tl[a, :]), g)
+                if cols == TILE:
+                    r.tile[slot, b, at(k, TILE), :] = value
+                else:
+                    r.tile[slot, b, at(k, TILE), :cols] = value
+
+        comm.advance(2.5 * len(pairs))
+        return slot
+
+    def tall(j, grad):
+        products(j, [(0, grad), (BLOCK, grad)])
+        comm.produced(j)
+        comm.tick()
+
+    def wide(j, first, left, right):
+        products(j, [(first, left), (first, right)])
+        comm.produced(j)
+        comm.tick()
+
+    def cols_of(ref, i, start=0):
+        return ref[:, start + i * TILE : start + (i + 1) * TILE]
 
     transposed(lambda i, c: silu(r.epre[:, c]), ff)
-    weight_grad(ff, lambda i: r.cot[:, at(i, TILE)], r.dw_shrink, width // TILE)
+    comm.advance(4.0)
+    for i in range(width // TILE):
+        tall(i, cols_of(r.cot, i))
 
     @pl.loop(0, rows // RC)
     def _(i):
@@ -482,7 +717,7 @@
     @pl.loop(0, ff // TILE)
     def _(i):
         c = at(i, TILE)
-        w = r.ws[c, :]
+        w = r.wb[c, :]
         value = (dot(r.lh[:, :width], w, NT) + dot(r.ll[:, :width], w, NT)) * dsilu(
             r.epre[:, c]
         )
@@ -494,6 +729,9 @@
         c = at(i, TILE)
         r.lh[:, c], r.ll[:, c] = split(r.epre[:, c])
 
+    weights[5].start()
+    comm.tick(7.0)
+
     @pl.loop(0, rows // RC)
     def _(i):
         part = at(i, RC)
@@ -501,13 +739,18 @@
         row_set(r.dnorm, part, n * gain1 + shift1)
 
     transposed(lambda i, c: r.dnorm[i], width)
-    weight_grad(width, lambda i: r.epre[:, at(i, TILE)], r.dw_expand, ff // TILE)
+    comm.advance(3.0)
+    for i in range(ff // (2 * TILE)):
+        wide(3 + i, 0, cols_of(r.epre, 2 * i), cols_of(r.epre, 2 * i + 1))
 
     @pl.loop(0, width // TILE)
     def _(i):
         c = at(i, TILE)
-        w = r.we[c, :]
+        w = r.wa[c, :]
         r.dx[:, c] = dot(r.lh[...], w, NT) + dot(r.ll[...], w, NT)
+
+    weights[6].start()
+    comm.tick(4.0)
 
     @pl.loop(0, rows // RC)
     def _(i):
@@ -533,12 +776,15 @@
         add768(5, dhpre)
 
     transposed(lambda i, c: r.att[:, c] * silu(r.gate[:, off(reset0, i, LANES)]), hv)
-    weight_grad(hv, lambda i: r.gate[:, off(cand0, i, TILE)], r.dw_output, width // TILE)
+    weights[5].wait()
+    comm.tick(9.0)
+    for i in range(width // TILE):
+        tall(6 + i, cols_of(r.gate, i, cand0))
 
     @pl.loop(0, hv // TILE)
     def _(i):
         c = at(i, TILE)
-        w = r.wo[c, :]
+        w = r.wb[c, :]
         gated = dot(r.lh[:, :width], w, NT) + dot(r.ll[:, :width], w, NT)
         here = off(reset0, i, TILE)
         pre = r.gate[:, here]
@@ -546,6 +792,8 @@
         r.att[:, c] = gated * silu(pre)
         r.gate[:, here] = dreset
         r.s_gates[:, here] = jnp.sum(dreset, axis=0, keepdims=True)
+
+    comm.tick(6.0)
 
     r.s_small[...] = jnp.zeros_like(r.s_small)
     r.starts[0] = jnp.zeros((group, group), f32)
@@ -583,6 +831,9 @@
     r.s_gates[:, width:reset0] = jnp.sum(r.gate[:, width:reset0], axis=0, keepdims=True)
     r.s_gates[:, cand0:] = r.s768[5:6, :]
 
+    comm.tick(12.0)
+    weights[6].wait()
+
     @pl.loop(0, hv // TILE)
     def _(i):
         c = at(i, TILE)
@@ -593,31 +844,12 @@
     @pl.loop(0, width // TILE)
     def _(i):
         c = at(i, TILE)
-        w = r.wv[c, :]
+        w = r.wa[c, :]
         col_set(r.dnorm, i, dot(r.lh[...], w, NT) + dot(r.ll[...], w, NT))
 
-    transposed(lambda i, c: r.normed[i], width)
-    weight_grad(width, lambda i: r.vpre[:, at(i, TILE)], r.dw_value, hv // TILE)
-
+    transposed(lambda i, c: r.normed[i], width, width)
     transposed(lambda i, c: silu(r.mpre[i]), width)
-    weight_grad(width, lambda i: r.gate[:, at(i, TILE)], r.dw_gates, width // TILE)
-    weight_grad(
-        width,
-        lambda i: r.gate[:, off(reset0, i, TILE)],
-        r.dw_gates,
-        (hv + width) // TILE,
-        reset0,
-    )
-    g_high, g_low = split(r.gate[:, width:reset0])
-    for k in range(width // TILE):
-        here = slice(k * TILE, (k + 1) * TILE)
-        r.stage[0, here, :zd] = dot3((r.th[here, :], r.tl[here, :]), (g_high, g_low))
-    shared_copy = pltpu.make_async_copy(
-        r.stage.at[0, pl.ds(0, width), pl.ds(0, zd)],
-        r.dw_gates.at[:, pl.ds(width, zd)],
-        r.ssem.at[0],
-    )
-    shared_copy.start()
+    comm.tick(10.0)
 
     def gate_section(start, size, first, last):
         @pl.loop(0, size // LANES)
@@ -640,10 +872,11 @@
             else:
                 r.att[:, c] = value
 
-    shared_copy.wait()
     gate_section(0, reset0, True, False)
     gate_section(reset0, hv, False, False)
     gate_section(cand0, width, False, True)
+
+    comm.tick(10.0)
 
     end_states(r.mpre, True, r.ends)
     adj = jnp.zeros((nstate, width), f32)
@@ -677,6 +910,7 @@
         row_set(r.starts, seg_of(k), state)
         state = dec_seg[...] * state + fresh
 
+    comm.tick(6.0)
     half = nstate // 2
     for h in range(2):
         states = range(h * half, (h + 1) * half)
@@ -690,7 +924,7 @@
             def ahead(t, state):
                 value = r.normed[d, seg_rows(t), :]
                 for n in range(half):
-                    r.history[t, n * SEG : (n + 1) * SEG, :] = state[n]
+                    r.epre[at(t, SEG), n * LANES : (n + 1) * LANES] = state[n]
                 return tuple(a * s + value for a, s in zip(dec, state))
 
             first = tuple(r.starts[d, n * SEG : (n + 1) * SEG, :] for n in states)
@@ -704,7 +938,7 @@
                 adj = tuple(a * s + grad for a, s in zip(dec, adj))
                 p_sum = tuple(p + a * value for p, a in zip(p_sum, adj))
                 q_sum = tuple(
-                    q + a * r.history[t, n * SEG : (n + 1) * SEG, :]
+                    q + a * r.epre[at(t, SEG), n * LANES : (n + 1) * LANES]
                     for n, (q, a) in enumerate(zip(q_sum, adj))
                 )
                 terms = [m * a for m, a in zip(mix, adj)]
@@ -722,6 +956,8 @@
                 row = row + nstate
                 r.s768[row : row + 1, cols] = jnp.sum(q_sum[n], axis=0, keepdims=True)
 
+        comm.tick(9.0)
+
     @pl.loop(0, rows // RC)
     def _(i):
         part = at(i, RC)
@@ -731,10 +967,37 @@
         add768(1, grad)
         r.dx[part, :] += norm_back(grad * gain0, n, inv)
 
-    zero_small(7)
-
-
-def layer(x, cot, sk, pk, kf, tables, gains, weights, biases, qk, bias_row, seq):
+    comm.tick(3.0)
+
+    for i in range(hv // (2 * TILE)):
+        wide(9 + i, width, cols_of(r.vpre, 2 * i), cols_of(r.vpre, 2 * i + 1))
+    starts = [i * TILE for i in range(width // TILE)]
+    starts += [reset0 + i * TILE for i in range((hv + width) // TILE)]
+    for i in range(len(starts) // 2):
+        left, right = starts[2 * i : 2 * i + 2]
+        wide(12 + i, 0, cols_of(r.gate, 0, left), cols_of(r.gate, 0, right))
+
+    slot = products(comm.jobs - 1, [(0, r.gate[:, width:reset0])])
+    r.tile[slot, 0, :, zd:] = jnp.zeros((BLOCK, TILE - zd), f32)
+    place = 0
+
+    def put(value):
+        nonlocal place
+        count = value.shape[0]
+        r.tile[slot, 0, place : place + count, zd:] = value
+        place += count
+
+    for d in range(width // LANES):
+        put(r.s768[:, d * LANES : (d + 1) * LANES])
+    put(r.s_small[...])
+    for ref in (r.s_value, r.s_expand, r.s_gates):
+        for d in range(ref.shape[1] // LANES):
+            put(ref[:, d * LANES : (d + 1) * LANES])
+    comm.produced(comm.jobs - 1)
+    comm.drain()
+
+
+def layer(x, cot, sk, pk, kf, tables, gains, weights, biases, qk, bias_row, batch, seq):
     rows, width = x.shape
     w_value, w_gates, w_output, w_expand, w_shrink = weights
     hv, gates, ff = w_value.shape[1], w_gates.shape[1], w_expand.shape[1]
@@ -743,34 +1006,22 @@
     vmem = pl.BlockSpec(memory_space=pltpu.VMEM)
     smem = pl.BlockSpec(memory_space=pltpu.SMEM)
     hbm = pl.BlockSpec(memory_space=pl.ANY)
+    subs = [2] * 18 + [1]
+    kinds = [(0, 1, 0, 1, 2, 0, 1, 0, 1, 3)[j % 10] for j in range(len(subs))]
+    stages, slots = len(stage_orders(batch, seq)[0]), slot_count(seq)
 
     def shape(*dims, kind=f32):
         return jax.ShapeDtypeStruct(dims, kind)
 
     return pl.pallas_call(
-        functools.partial(kernel, seq),
-        out_shape=(
-            shape(rows, width),
-            shape(rows, width),
-            shape(width, hv),
-            shape(width, gates),
-            shape(hv, width),
-            shape(width, ff),
-            shape(ff, width),
-            shape(8 + 2 * nstate, width),
-            shape(1, hv),
-            shape(1, ff),
-            shape(1, gates),
-            shape(8, zd),
-        ),
+        functools.partial(kernel, batch, seq, (kinds, subs)),
+        out_shape=(shape(rows, width), shape(rows, width), shape(sum(subs), BLOCK, TILE)),
         in_specs=[vmem, vmem, smem, smem, smem, vmem, vmem] + [hbm] * 5 + [vmem] * 5,
-        out_specs=(vmem, vmem, hbm, hbm, hbm, hbm, hbm, vmem, vmem, vmem, vmem, vmem),
+        out_specs=(vmem, vmem, hbm),
         scratch_shapes=[
             pltpu.VMEM(w_value.shape, bf16),
+            pltpu.VMEM(w_output.shape, bf16),
             pltpu.VMEM(w_gates.shape, bf16),
-            pltpu.VMEM(w_output.shape, bf16),
-            pltpu.VMEM(w_expand.shape, bf16),
-            pltpu.VMEM(w_shrink.shape, bf16),
             pltpu.VMEM((width // LANES, rows, LANES), f32),
             pltpu.VMEM((rows, hv), f32),
             pltpu.VMEM((rows, gates), f32),
@@ -785,19 +1036,29 @@
             pltpu.VMEM((rows, max(hv, ff)), bf16),
             pltpu.VMEM((max(hv, ff), rows), bf16),
             pltpu.VMEM((max(hv, ff), rows), bf16),
-            pltpu.VMEM((2, max(hv, ff), TILE), f32),
+            pltpu.VMEM((8 + 2 * nstate, width), f32),
+            pltpu.VMEM((1, hv), f32),
+            pltpu.VMEM((1, ff), f32),
+            pltpu.VMEM((1, gates), f32),
+            pltpu.VMEM((8, zd), f32),
             pltpu.VMEM((width // LANES, nstate * SEG, LANES), f32),
             pltpu.VMEM((width // LANES, nstate * SEG, LANES), f32),
             pltpu.VMEM((seq, nstate, width), f32),
             pltpu.VMEM((seq, nstate, width), f32),
-            pltpu.VMEM((rows // SEG, nstate // 2 * SEG, LANES), f32),
-            pltpu.SemaphoreType.DMA((5,)),
-            pltpu.SemaphoreType.DMA((2,)),
+            pltpu.SemaphoreType.DMA((7,)),
             pltpu.SemaphoreType.DMA((seq,)),
             pltpu.SemaphoreType.DMA((seq,)),
             pltpu.SemaphoreType.DMA((seq,)),
             pltpu.SemaphoreType.DMA((seq,)),
-        ],
+            pltpu.VMEM((TILES, 2, BLOCK, TILE), f32),
+            pltpu.SemaphoreType.DMA((stages, slots)),
+            pltpu.SemaphoreType.DMA((stages, slots)),
+            pltpu.SemaphoreType.REGULAR((stages, slots)),
+            pltpu.SemaphoreType.DMA((len(subs),)),
+            pltpu.SemaphoreType.DMA((len(subs), HALVINGS)),
+            pltpu.SemaphoreType.DMA((len(subs), HALVINGS)),
+        ]
+        + [pltpu.VMEM((slots, 2, count, TILE), f32) for count in stage_rows(stages)],
         compiler_params=pltpu.CompilerParams(
             collective_id=0, has_side_effects=True, vmem_limit_bytes=63 << 20
         ),
@@ -810,6 +1071,7 @@
 
 
 def shards(
+    batch,
     seq,
     tokens,
     lengths,
@@ -883,14 +1145,38 @@
         (b_value[None], b_gates[None], b_expand[None]),
         query_key.T,
         jnp.roll(position_bias[::-1], 1)[None],
+        batch,
         seq,
     )
-    output, grad_tokens = outs[:2]
-    summed = lax.psum(outs[2:], ("batch", "seq"))
-    dw_value, dw_gates, dw_output, dw_expand, dw_shrink, s768, s_value, s_expand, s_gates, small = (
-        summed
+    output, grad_tokens, blocks_out = outs
+
+    def tall(first, count):
+        parts = blocks_out[first : first + count].reshape(count // 2, 2, BLOCK, TILE)
+        return parts.transpose(1, 2, 0, 3).reshape(2 * BLOCK, count // 2 * TILE)
+
+    def wide(first, count):
+        return blocks_out[first : first + count].transpose(1, 0, 2).reshape(BLOCK, count * TILE)
+
+    nstate = alpha.shape[0]
+    hv, gates, ff = b_value.shape[0], b_gates.shape[0], b_expand.shape[0]
+    zd = query_key.shape[0]
+    dw_shrink, dw_expand, dw_output, dw_value = tall(0, 6), wide(6, 6), tall(12, 6), wide(18, 6)
+    dw_gates = jnp.concatenate(
+        [wide(24, width // TILE), blocks_out[36, :, :zd], wide(24 + width // TILE, 9)], axis=1
     )
-    nstate = alpha.shape[0]
+    rest = blocks_out[36, :, zd:]
+    tall_rows = 8 + 2 * nstate
+    lanes = width // LANES
+    s768 = rest[: lanes * tall_rows].reshape(lanes, tall_rows, LANES)
+    s768 = s768.transpose(1, 0, 2).reshape(tall_rows, width)
+    place = lanes * tall_rows
+    small = rest[place : place + 8]
+    place += 8
+    sums = []
+    for count in (hv, ff, gates):
+        sums.append(rest[place : place + count // LANES].reshape(count))
+        place += count // LANES
+    s_value, s_expand, s_gates = sums
     p_sum, q_sum = s768[8 : 8 + nstate], s768[8 + nstate : 8 + 2 * nstate]
     d_inflow = eta * p_sum
     d_eta = inflow * p_sum
@@ -907,15 +1193,15 @@
         d_eta.T,
         s768[4],
         dw_value,
-        s_value[0],
+        s_value,
         dw_gates,
-        s_gates[0],
+        s_gates,
         small[:3].T,
         jnp.roll(small[3][::-1], 1),
         dw_output,
         s768[5],
         dw_expand,
-        s_expand[0],
+        s_expand,
         dw_shrink,
         s768[6],
     )
@@ -924,7 +1210,7 @@
 def solution(mesh):
     token_spec = P("batch", "seq", None)
     return jax.shard_map(
-        functools.partial(shards, mesh.shape["seq"]),
+        functools.partial(shards, mesh.shape["batch"], mesh.shape["seq"]),
         mesh=mesh,
         in_specs=(token_spec, P("batch", None), token_spec) + (P(),) * 19,
         out_specs=(token_spec, token_spec) + (P(),) * 19,

time: 683 us -> 510 us (0.75)
  waiting for transfers between devices: 401 us -> 0 us
  Pallas kernels: 180 us -> 363 us
  local copies, waits for them, and re-layouts: 34.9 us -> 128 us
  blocking collectives: 43.2 us -> 0 us
  between operations: 15.5 us -> 2.06 us
    psum x1 -> x0, waiting for transfers between devices: 401 us -> none  [shards(): summed = lax.psum(outs[2:], ('batch', 'seq'))]
    pallas_call x1, Pallas kernels: 180 us -> 363 us  [layer(): pl.pallas_call(functools.partial(kernel, batch, seq, (kinds, subs)), out_...]
    psum x1 -> x0, blocking collectives: 43.2 us -> none  [shards(): summed = lax.psum(outs[2:], ('batch', 'seq'))]
    transpose x0 -> x6, local copies, waits for them, and re-layouts: none -> 31.8 us  [wide(): blocks_out[first:first + count].transpose(1, 0, 2)]
    unnamed x40 -> x26, local copies, waits for them, and re-layouts: 21.2 us -> 46.9 us
    reshape x0 -> x5, local copies, waits for them, and re-layouts: none -> 19.1 us  [the longest x2 16.4 us: tall(): parts = blocks_out[first:first + count].reshape(count // 2, 2, BLOCK, TILE)]
    slice x1 -> x3, local copies, waits for them, and re-layouts: 1.63 us -> 14.5 us  [the longest x1 13.6 us: tall(): parts = blocks_out[first:first + count].reshape(count // 2, 2, BLOCK, TILE)]
    concatenate x0 -> x1, other arithmetic: none -> 7.41 us  [shards(): jnp.concatenate([wide(24, width // TILE), blocks_out[36, :, :zd], wide(24...]
  transfers between devices with their start and end apart: 1 -> 0, of which waited for: 1 -> 0; matrix products, arithmetic and copies ran while one was open for 0% -> 0% of each run, Pallas kernels for 0% -> 0%
where the time goes in v2:
time: 510 us; the launch traced here: 508 us
  Pallas kernels  363 us (71%)
  local copies, waits for them, and re-layouts  128 us (25%)
  other arithmetic  14.6 us (3%)
    pallas_call x1, Pallas kernels, layer(): pl.pallas_call(functools.partial(kernel, batch, seq, (kinds, subs)), out_...  363 us
    unnamed x26, local copies, waits for them, and re-layouts  46.9 us
    transpose x6, local copies, waits for them, and re-layouts, wide(): blocks_out[first:first + count].transpose(1, 0, 2)  31.8 us
    reshape x2, local copies, waits for them, and re-layouts, tall(): parts = blocks_out[first:first + count].reshape(count // 2, 2, BLOCK, TILE)  16.4 us
    slice x1, local copies, waits for them, and re-layouts, tall(): parts = blocks_out[first:first + count].reshape(count // 2, 2, BLOCK, TILE)  13.6 us

profile of v2, /device:TPU:1, one launch (start us, length us, event | category | flops | bytes accessed | tf_op | source)
XLA Modules:
  0.0 508.3 jit_solution(15796327382134400151)
XLA Ops:
  0.7 0.7 slice.168
  1.5 1.2 maximum_bitcast_fusion.refs_16_
  2.7 1.3 fusion.18
  5.3 1.2 convert_subtract_fusion
  6.7 0.5 slice_bitcast_fusion.21.refs_4_
  7.3 0.6 reshape.147.refs_2_
  7.9 0.7 stack.38
  8.6 0.7 stack.39
  9.3 0.7 stack.40
  10.0 1.3 broadcast_in_dim.18.refs_12_
  11.3 1.3 broadcast_in_dim.20.refs_14_
  12.6 0.8 slice_bitcast_fusion.15
  13.4 0.7 stack.41.refs_6_
  14.0 1.3 broadcast_in_dim.19.refs_13_
  15.3 0.9 exponential_bitcast_fusion.2
  16.3 0.7 pad_maximum_fusion.1.refs_5_
  17.0 363.5 %shard_map.373 = (f32[512,768]{1,0:T(8,128)}, f32[512,768]{1,0:T(8,128)}, f32[37,768,256]{2,1,0:T(8,128)}) custom-call(f32[512,768]{1,0:T(8,128)} %bitcast.237, f32[512,768]{1,0:T(8,128)} %bitcast.238, f32[8]{0:T(128)} %reshape.147.refs_2_, f32[8]{0:T(128)} %get-tuple-element.90.refs_3_, f32[8]{0:T(128)} %slice_bitcast_fusion.21.refs_4_, ...), custom_call_target="tpu_custom_call" | custom-call | flops 51999997952 | bytes 60000000 | tf_op jit(solution)/shard_map/pallas_call | solution.py:1016
  380.5 1.2 slice.188
  381.7 0.7 slice_bitcast_fusion.20
  382.5 1.2 pad_maximum_fusion.4
  383.7 1.3 slice_bitcast_fusion.19
  385.0 1.3 slice_bitcast_fusion.5
  386.3 1.4 slice_bitcast_fusion.6
  387.7 0.9 slice.170
  388.6 0.6 slice_bitcast_fusion.8
  389.3 0.6 pad_maximum_fusion.3
  389.9 0.6 pad_maximum_fusion.2
  390.5 0.7 fusion.7
  391.2 1.0 slice_bitcast_fusion.4
  392.4 3.2 slice_bitcast_fusion.3
  395.6 2.0 copy.50
  397.7 6.4 %slice_bitcast_fusion = f32[768,9,256]{2,0,1:T(8,128)} fusion(f32[37,768,256]{2,1,0:T(8,128)} %get-tuple-element.38), kind=kLoop, calls=%fused_computation.1 | loop fusion | bytes 14155776 | tf_op jit(solution)/shard_map/transpose | solution.py:1158
  404.1 13.6 %fusion.16 = (f32[6,768,256]{2,1,0:T(8,128)}, f32[768,6,256]{2,0,1:T(8,128)}, f32[6,768,256]{2,1,0:T(8,128)}, f32[768,6,256]{2,0,1:T(8,128)}) fusion(f32[37,768,256]{2,1,0:T(8,128)} %get-tuple-element.38), kind=kLoop, calls=%fused_computation.71 | loop fusion | bytes 37748736 | tf_op jit(solution)/shard_map/slice | solution.py:1154
  417.7 8.2 %copy.55 = f32[3,2,768,256]{2,1,3,0:T(2,128)} copy(f32[3,2,768,256]{3,2,1,0:T(8,128)} %bitcast.217) | data formatting | bytes 9437184 | tf_op jit(solution)/shard_map/reshape | solution.py:1154
  425.9 4.8 copy.69
  430.7 6.0 %copy.60 = f32[1536,768]{1,0:T(8,128)} copy(f32[1536,768]{0,1:T(8,128)} %bitcast.219) | data formatting | bytes 9437184
  436.8 8.0 %copy.51 = f32[768,9,256]{0,2,1:T(8,128)} copy(f32[768,9,256]{2,0,1:T(8,128)} %slice_bitcast_fusion) | data formatting | bytes 14155776 | tf_op jit(solution)/shard_map/transpose | solution.py:1158
  444.7 7.4 %pad_maximum_fusion = f32[768,3200]{0,1:T(8,128)} fusion(f32[768,2304]{0,1:T(8,128)} %bitcast.215, f32[768,128]{0,1:T(8,128)S(1)} %copy.52, f32[768,768]{0,1:T(8,128)S(1)} %bitcast.224), kind=kLoop, calls=%fused_computation | loop fusion | flops 4915200 | bytes 19660800 | tf_op jit(solution)/shard_map/concatenate | solution.py:1164
  452.2 10.4 %copy.57 = f32[768,3200]{1,0:T(8,128)} copy(f32[768,3200]{0,1:T(8,128)} %pad_maximum_fusion) | data formatting | bytes 19660800
  462.6 6.1 %copy.54 = f32[768,6,256]{0,2,1:T(8,128)} copy(f32[768,6,256]{2,0,1:T(8,128)} %get-tuple-element.61) | data formatting | bytes 9437184 | tf_op jit(solution)/shard_map/transpose | solution.py:1158
  468.6 6.0 %copy.59 = f32[768,1536]{1,0:T(8,128)} copy(f32[768,1536]{0,1:T(8,128)} %bitcast.220) | data formatting | bytes 9437184
  474.7 8.2 %copy.53 = f32[3,2,768,256]{2,1,3,0:T(2,128)} copy(f32[3,2,768,256]{3,2,1,0:T(8,128)} %bitcast.216) | data formatting | bytes 9437184 | tf_op jit(solution)/shard_map/reshape | solution.py:1154
  482.9 4.8 copy.68
  487.7 6.0 %copy.58 = f32[1536,768]{1,0:T(8,128)} copy(f32[1536,768]{0,1:T(8,128)} %bitcast.222) | data formatting | bytes 9437184
  493.8 6.1 %copy.49 = f32[768,6,256]{0,2,1:T(8,128)} copy(f32[768,6,256]{2,0,1:T(8,128)} %get-tuple-element.63) | data formatting | bytes 9437184 | tf_op jit(solution)/shard_map/transpose | solution.py:1158
  499.8 6.2 %copy.56 = f32[768,1536]{1,0:T(8,128)} copy(f32[768,1536]{0,1:T(8,128)} %bitcast.223) | data formatting | bytes 9437184
  506.0 1.1 copy.93
  507.2 1.1 copy.94
  (25 shorter events, 0.7 us)
Async XLA Ops:
  17.0 373.5 %copy-start.2 = (f32[768,16]{0,1:T(8,128)S(1)}, f32[768,16]{0,1:T(8,128)}, u32[]{:S(2)}) copy-start(f32[768,16]{0,1:T(8,128)} %param.30) | copy-start | bytes 147460
  17.0 373.5 %copy-start.3 = (f32[768,16]{0,1:T(8,128)S(1)}, f32[768,16]{0,1:T(8,128)}, u32[]{:S(2)}) copy-start(f32[768,16]{0,1:T(8,128)} %param.29) | copy-start | bytes 147460
  17.0 373.5 %copy-start.4 = (f32[768,16]{0,1:T(8,128)S(1)}, f32[768,16]{0,1:T(8,128)}, u32[]{:S(2)}) copy-start(f32[768,16]{0,1:T(8,128)} %param.32) | copy-start | bytes 147460
  17.0 373.5 %copy-start.5 = (f32[768,16]{0,1:T(8,128)S(1)}, f32[768,16]{0,1:T(8,128)}, u32[]{:S(2)}) copy-start(f32[768,16]{0,1:T(8,128)} %param.31) | copy-start | bytes 147460
  499.8 6.2 %copy-start.1 = (f32[512,768]{1,0:T(8,128)S(1)}, f32[512,768]{1,0:T(8,128)}, u32[]{:S(2)}) copy-start(f32[512,768]{1,0:T(8,128)} %get-tuple-element.36) | copy-start | bytes 4718596
  499.8 7.3 %copy-start = (f32[512,768]{1,0:T(8,128)S(1)}, f32[512,768]{1,0:T(8,128)}, u32[]{:S(2)}) copy-start(f32[512,768]{1,0:T(8,128)} %get-tuple-element.37) | copy-start | bytes 4718596

commit v3 on v2

--- a/solution.py
+++ b/solution.py
@@ -92,10 +92,13 @@
 HALVINGS = 5
 BLOCK = 768
 TILES = 2
+SERVICE = 0.7
+JOBS = 19
+KINDS = (0, 1, 0, 1, 2, 0, 1, 0, 1, 3)
 
 
 def slot_count(seq):
-    return 8 if seq <= 16 else 4
+    return 7 if seq <= 16 else 3
 
 
 def bits_of(batch, seq):
@@ -119,19 +122,69 @@
     return [BLOCK >> (min(s, HALVINGS - 1) + 1) for s in range(count)]
 
 
+class Links:
+    LATENCY = 1.5
+    CORE, LINE = 0.6, 0.0455
+
+    def __init__(self):
+        self.now = 0.0
+        self.active = {}
+        self.arrived = {}
+
+    def uses(self, bit):
+        name, step = bit
+        if bit == ("seq", 1):
+            return (("core", 1),)
+        if name == "batch":
+            return ((name + str(step), 1),)
+        return (("ends", 1),) if step == 2 else (("ends", 1), ("middle", 2))
+
+    def start(self, key, size, bit):
+        self.active[key] = [size, self.uses(bit)]
+
+    def rates(self):
+        load = {}
+        for _size, uses in self.active.values():
+            for link, weight in uses:
+                load[link] = load.get(link, 0) + weight
+        return {
+            key: min((self.CORE if link == "core" else self.LINE) / load[link] for link, _w in uses)
+            for key, (_size, uses) in self.active.items()
+        }
+
+    def forward(self, until=None):
+        while self.active:
+            rates = self.rates()
+            key = min(self.active, key=lambda k: self.active[k][0] / rates[k])
+            step = self.active[key][0] / rates[key]
+            if until is not None and self.now + step > until:
+                step = until - self.now
+                key = None
+            for k in self.active:
+                self.active[k][0] -= step * rates[k]
+            self.now += step
+            if key is None:
+                return
+            del self.active[key]
+            self.arrived[key] = self.now + self.LATENCY
+            if until is None:
+                return
+        if until is not None:
+            self.now = max(self.now, until)
+
+
 class Reducer:
-    def __init__(self, orders, slots, kinds, subs, tile, red, gathered, sems):
+    def __init__(self, orders, slots, kinds, pieces, tile, red, sems):
         self.slots = slots
-        self.orders, self.kinds, self.subs = orders, kinds, subs
-        self.tile, self.red, self.gathered = tile, red, gathered
+        self.orders, self.kinds, self.pieces = orders, kinds, pieces
+        self.subs = [max(p[0] for p in job) + 1 for job in pieces]
+        self.tile, self.red = tile, red
         self.send, self.recv, self.credit, self.local, self.gsend, self.grecv = sems
         self.stages = len(orders[0])
         self.halvings = min(HALVINGS, self.stages)
         self.rows = stage_rows(self.stages)
-        self.jobs = len(subs)
-        self.first = [sum(subs[:j]) for j in range(self.jobs)]
-        self.now = 0.0
-        self.free = {}
+        self.jobs = len(pieces)
+        self.links = Links()
         self.due = {}
         self.done = [-1] * self.jobs
 
@@ -173,52 +226,55 @@
             if flip and t == s:
                 bit = 1 - bit
             start = start + bit * self.rows[t]
-        return self.gathered.at[
-            pl.ds(self.first[j], self.subs[j]), pl.ds(pl.multiple_of(start, 8), self.rows[s]), :
+        return [
+            target.at[
+                pl.ds(pl.multiple_of(row + start, 8), self.rows[s]), pl.ds(col, count)
+            ]
+            for _block, _from, count, target, row, col in self.pieces[j]
         ]
 
     def final(self, j):
         ref, slot, rows = self.held(j, self.stages - 1)
-        return self.part(ref, slot, j, 0, rows)
-
-    def gather_copy(self, j, s, arriving=False):
+        return [
+            ref.at[slot, block, pl.ds(0, rows), pl.ds(from_col, count)]
+            for block, from_col, count, _target, _row, _col in self.pieces[j]
+        ]
+
+    def gather_copies(self, j, s, arriving=False):
         last = s == self.halvings - 1
-        return pltpu.make_async_remote_copy(
-            src_ref=self.final(j) if last else self.owned(j, s),
-            dst_ref=self.owned(j, s, flip=arriving),
-            send_sem=self.gsend.at[j, s],
-            recv_sem=self.grecv.at[j, s],
-            device_id=partner(self.order(j)[s]),
-            device_id_type=MESH,
-        )
-
-    def local_copy(self, j):
-        return pltpu.make_async_copy(
-            self.final(j), self.owned(j, self.halvings - 1), self.local.at[j]
-        )
-
-    def arrival(self, j, s):
-        name, step = self.order(j)[s]
-        rows = self.rows[s] * self.subs[j]
-        size = rows * TILE * 4e-6
-        if (name, step) == ("seq", 1):
-            link, cost = "core", size / 0.6
-        else:
-            link = name + (str(step) if name == "batch" else "")
-            cost = 2 * size / 0.09 * (step // 2 if name == "seq" else 1)
-        start = max(self.now, self.free.get(link, 0.0))
-        self.free[link] = start + cost
-        return start + cost + 2.0
+        sources = self.final(j) if last else self.owned(j, s)
+        return [
+            pltpu.make_async_remote_copy(
+                src_ref=source,
+                dst_ref=target,
+                send_sem=self.gsend.at[j, s, p],
+                recv_sem=self.grecv.at[j, s, p],
+                device_id=partner(self.order(j)[s]),
+                device_id_type=MESH,
+            )
+            for p, (source, target) in enumerate(zip(sources, self.owned(j, s, flip=arriving)))
+        ]
+
+    def local_copies(self, j):
+        pairs = zip(self.final(j), self.owned(j, self.halvings - 1))
+        return [
+            pltpu.make_async_copy(source, target, self.local.at[j, p])
+            for p, (source, target) in enumerate(pairs)
+        ]
+
+    def sent(self, j, event, s):
+        size = self.rows[s] * self.subs[j] * TILE * 4e-6
+        self.links.start((j, event), size, self.order(j)[s])
+        self.due[j] = event
 
     def advance(self, us):
-        self.now += us
-
-    def set_due(self, j, event, when):
-        self.due[j] = (event, when)
+        self.links.forward(self.links.now + us)
 
     def run(self, j):
-        event, when = self.due.pop(j)
-        self.now = max(self.now, when)
+        event = self.due.pop(j)
+        while (j, event) not in self.links.arrived:
+            self.links.forward()
+        self.links.forward(max(self.links.now, self.links.arrived.pop((j, event))))
         n = self.stages
         if event < n:
             s = event
@@ -231,21 +287,25 @@
             if s < n - 1:
                 self.start_scatter(j, s + 1)
             else:
-                self.local_copy(j).start()
-                self.gather_copy(j, self.halvings - 1).start()
-                self.set_due(j, event + 1, self.arrival(j, self.halvings - 1))
+                for copy in self.local_copies(j) + self.gather_copies(j, self.halvings - 1):
+                    copy.start()
+                self.sent(j, event + 1, self.halvings - 1)
         else:
             s = self.halvings - 1 - (event - n)
-            self.gather_copy(j, s, True).wait_recv()
+            for copy in self.gather_copies(j, s, True):
+                copy.wait_recv()
             if s == self.halvings - 1:
-                self.gather_copy(j, s).wait_send()
-                self.local_copy(j).wait()
+                for copy in self.gather_copies(j, s):
+                    copy.wait_send()
+                for copy in self.local_copies(j):
+                    copy.wait()
                 self.give_credit(j, n - 1)
             if s > 0:
-                self.gather_copy(j, s - 1).start()
-                self.set_due(j, event + 1, self.arrival(j, s - 1))
+                for copy in self.gather_copies(j, s - 1):
+                    copy.start()
+                self.sent(j, event + 1, s - 1)
         self.done[j] = event
-        self.now += 0.5
+        self.advance(SERVICE)
 
     def add(self, j, s):
         ref, slot, _rows = self.held(j, s - 1)
@@ -274,7 +334,7 @@
             self.reach(j - self.slots, s + 1)
             pl.semaphore_wait(self.credit.at[s, j % self.slots], 1)
         self.scatter_copy(j, s).start()
-        self.set_due(j, s, self.arrival(j, s))
+        self.sent(j, s, s)
 
     def reach(self, j, event):
         while self.done[j] < event:
@@ -290,44 +350,65 @@
 
     def tick(self, us=0.0):
         self.advance(us)
-        while self.due:
-            j = min(self.due, key=lambda k: self.due[k][1])
-            if self.due[j][1] > self.now:
+        while True:
+            ready = {k: t for k, t in self.links.arrived.items() if t <= self.links.now}
+            if not ready:
                 break
-            self.run(j)
+            self.run(min(ready, key=ready.get)[0])
 
     def drain(self):
         while self.due:
-            self.run(min(self.due, key=lambda k: self.due[k][1]))
+            if not self.links.arrived:
+                self.links.forward()
+            self.run(min(self.links.arrived, key=self.links.arrived.get)[0])
         for j in range(self.jobs):
             for s in range(self.halvings - 1):
-                self.gather_copy(j, s).wait_send()
+                for copy in self.gather_copies(j, s):
+                    copy.wait_send()
 
 
 class Refs(typing.NamedTuple):
     x: typing.Any
     cot: typing.Any
-    sk: typing.Any
-    pk: typing.Any
-    kf: typing.Any
-    tables: typing.Any
-    gains: typing.Any
+    lengths: typing.Any
+    norm_gain: typing.Any
+    norm_shift: typing.Any
+    alpha: typing.Any
+    delta: typing.Any
+    beta: typing.Any
+    eta: typing.Any
+    omega_in: typing.Any
+    b_output_in: typing.Any
+    b_shrink_in: typing.Any
+    b_value_in: typing.Any
+    b_gates_in: typing.Any
+    b_expand_in: typing.Any
+    qk: typing.Any
+    bias: typing.Any
     w_value: typing.Any
     w_gates: typing.Any
     w_output: typing.Any
     w_expand: typing.Any
     w_shrink: typing.Any
+    out_hbm: typing.Any
+    dx_hbm: typing.Any
+    dw_value: typing.Any
+    dw_gates: typing.Any
+    dw_output: typing.Any
+    dw_expand: typing.Any
+    dw_shrink: typing.Any
+    sums: typing.Any
+    wa: typing.Any
+    wb: typing.Any
+    wg: typing.Any
+    cot_v: typing.Any
+    out: typing.Any
+    dx: typing.Any
+    tables: typing.Any
+    gains: typing.Any
     b_value: typing.Any
     b_gates: typing.Any
     b_expand: typing.Any
-    qk: typing.Any
-    bias_row: typing.Any
-    out: typing.Any
-    dx: typing.Any
-    gathered: typing.Any
-    wa: typing.Any
-    wb: typing.Any
-    wg: typing.Any
     normed: typing.Any
     vpre: typing.Any
     gate: typing.Any
@@ -338,6 +419,7 @@
     mpre: typing.Any
     dnorm: typing.Any
     probs: typing.Any
+    square: typing.Any
     lh: typing.Any
     ll: typing.Any
     th: typing.Any
@@ -352,6 +434,7 @@
     e_recv: typing.Any
     f_recv: typing.Any
     wsem: typing.Any
+    osem: typing.Any
     send: typing.Any
     recv: typing.Any
     send2: typing.Any
@@ -361,7 +444,7 @@
     red: typing.Any
 
 
-def kernel(batch, seq, plan, *refs):
+def kernel(batch, seq, *refs):
     n = len(Refs._fields) - 2
     r = Refs(*refs[:n], refs[n : n + 6], refs[n + 6 :])
     rows, width = r.x.shape
@@ -375,6 +458,7 @@
     groups = rows // group
     reset0 = width + zd
     cand0 = reset0 + hv
+    gates = cand0 + width
     scale = 1.0 / math.sqrt(zd)
 
     sources = (r.w_value, r.w_gates, r.w_output, r.w_expand, r.w_shrink, r.w_output, r.w_value)
@@ -382,12 +466,28 @@
     weights = [
         pltpu.make_async_copy(a, b, r.wsem.at[i]) for i, (a, b) in enumerate(zip(sources, places))
     ]
-    for copy in weights[:3]:
+    cot_copy = pltpu.make_async_copy(r.cot, r.cot_v, r.wsem.at[len(weights)])
+    for copy in weights[:3] + [cot_copy]:
         copy.start()
 
-    kinds, subs = plan
+    gate_cols = [i * TILE for i in range(width // TILE)]
+    gate_cols += [reset0 + i * TILE for i in range((hv + width) // TILE)]
+
+    def tall_job(ref, i):
+        return [(b, 0, TILE, ref, b * BLOCK, i * TILE) for b in range(2)]
+
+    def wide_job(ref, cols):
+        return [(b, 0, TILE, ref, 0, cols[b]) for b in range(2)]
+
+    pieces = [tall_job(r.dw_shrink, i) for i in range(width // TILE)]
+    pieces += [wide_job(r.dw_expand, (i, i + TILE)) for i in range(0, ff, 2 * TILE)]
+    pieces += [tall_job(r.dw_output, i) for i in range(width // TILE)]
+    pieces += [wide_job(r.dw_value, (i, i + TILE)) for i in range(0, hv, 2 * TILE)]
+    pieces += [wide_job(r.dw_gates, gate_cols[i : i + 2]) for i in range(0, len(gate_cols), 2)]
+    pieces.append([(0, 0, zd, r.dw_gates, 0, width), (0, zd, TILE - zd, r.sums, 0, 0)])
+    kinds = [KINDS[j % len(KINDS)] for j in range(len(pieces))]
     comm = Reducer(
-        stage_orders(batch, seq), slot_count(seq), kinds, subs, r.tile, r.red, r.gathered, r.sems
+        stage_orders(batch, seq), slot_count(seq), kinds, pieces, r.tile, r.red, r.sems
     )
     _core, chips, _line = bits_of(batch, seq)
 
@@ -403,10 +503,61 @@
     for bit in chips:
         pl.semaphore_signal(barrier, inc=1, device_id=partner(bit), device_id_type=MESH)
 
+    alpha, damping = sigmoid(r.alpha[...]), sigmoid(r.delta[...])
+    rate = alpha * damping
+    series = jnp.full_like(rate, 1.0 / 7.0)
+    for n in range(6, 0, -1):
+        series = series * rate + 1.0 / n
+    log_decay = -rate * series
+    for i, value in enumerate(
+        (
+            1.0 - rate,
+            alpha * r.beta[...] * r.eta[...],
+            jnp.exp(seg_len * log_decay),
+            jnp.exp(rows * log_decay),
+        )
+    ):
+        r.tables[i] = value
+    decay, coef, dec_seg, dec_all = (r.tables.at[i] for i in range(4))
+
+    def unfold(source, target, row=0):
+        for d in range(source.shape[0]):
+            target[row : row + 1, d * LANES : (d + 1) * LANES] = source[d : d + 1, :]
+
+    unfold(r.b_value_in, r.b_value)
+    unfold(r.b_gates_in, r.b_gates)
+    unfold(r.b_expand_in, r.b_expand)
+    for i in range(2):
+        r.gains[2 * i : 2 * i + 1, :] = r.norm_gain[i : i + 1, :]
+        r.gains[2 * i + 1 : 2 * i + 2, :] = r.norm_shift[i : i + 1, :]
+    for i, source in enumerate((r.omega_in, r.b_output_in, r.b_shrink_in)):
+        unfold(source, r.gains, 4 + i)
     gain0, shift0, gain1, shift1, omega, b_output, b_shrink = (
         r.gains[i : i + 1, :] for i in range(7)
     )
-    decay, coef, dec_seg, dec_all = (r.tables.at[i] for i in range(4))
+
+    first_end = r.lengths[0, 0]
+    second_end = first_end + r.lengths[0, 1]
+
+    def keep(group_id):
+        starts = (group_id == 0) | (group_id == first_end) | (group_id == second_end)
+        return jnp.where(starts, 0.0, 1.0)
+
+    def keep_block(k):
+        value = keep(k * groups)
+        for g in range(1, groups):
+            value = value * keep(k * groups + g)
+        return value
+
+    keep_seg = [
+        keep(me * groups + k * groups // SEG) if k % (SEG // groups) == 0 else 1.0
+        for k in range(SEG)
+    ]
+
+    def tiles(count, body, us, parts=1):
+        for p in range(parts):
+            pl.loop(count * p // parts, count * (p + 1) // parts)(body)
+            comm.tick(us / parts)
 
     def zero_small(i):
         r.s768[i : i + 1, :] = jnp.zeros((1, width), f32)
@@ -507,7 +658,7 @@
     end_states(r.normed, False, r.ends)
     total = jnp.zeros((nstate, width), f32)
     for k in range(SEG):
-        total = r.sk[k] * total * dec_seg[...] + row_get(r.ends, seg_of(k))
+        total = keep_seg[k] * total * dec_seg[...] + row_get(r.ends, seg_of(k))
     r.e_recv[me] = total
     pl.semaphore_wait(barrier, seq - 1 + len(chips))
     start_e, wait_e = exchange(r.e_recv, r.send, r.recv)
@@ -528,12 +679,12 @@
     wait_e()
 
     def carry_step(k, carried):
-        new = dec_all[...] * (r.pk[k] * carried) + r.e_recv[k]
+        new = dec_all[...] * (keep_block(k) * carried) + r.e_recv[k]
         return jnp.where(k < me, new, carried)
 
     state = lax.fori_loop(0, seq, carry_step, jnp.zeros((nstate, width), f32))
     for k in range(SEG):
-        state = r.sk[k] * state
+        state = keep_seg[k] * state
         row_set(r.starts, seg_of(k), state)
         if k < SEG - 1:
             state = dec_seg[...] * state + row_get(r.ends, seg_of(k))
@@ -586,12 +737,12 @@
     )
     row_id = lax.broadcasted_iota(jnp.int32, (group, group), 0)
     causal = lag >= 0
-    table = jnp.broadcast_to(r.bias_row[...], (group, group))
+    table = jnp.broadcast_to(r.bias[...], (group, group))
     for b in range(group.bit_length() - 1):
         moved = pltpu.roll(table, 1 << b, 1)
         table = jnp.where((row_id & (1 << b)) != 0, moved, table)
     q_gain, k_gain, q_shift = (r.qk[i : i + 1, :] for i in range(3))
-    r.starts[0] = table
+    r.square[...] = table.T
 
     @pl.loop(0, groups)
     def _(g):
@@ -599,7 +750,7 @@
         shared = silu(r.gate[part, width:reset0])
         q = split(shared * q_gain + q_shift)
         k = split(shared * k_gain)
-        scores = dot3(q, k, NT) * scale + r.starts[0]
+        scores = dot3(q, k, NT) * scale + r.square[...]
         scores = jnp.where(causal, scores, -1e30)
         p = jnp.exp(scores - jnp.max(scores, axis=-1, keepdims=True))
         p = p / jnp.sum(p, axis=-1, keepdims=True)
@@ -648,22 +799,8 @@
             dot(r.lh[:, :width], w) + dot(r.ll[:, :width], w) + r.b_expand[:, c]
         )
 
-    @pl.loop(0, ff // TILE)
-    def _(i):
-        c = at(i, TILE)
-        r.lh[:, c], r.ll[:, c] = split(silu(r.epre[:, c]))
-
-    weights[4].wait()
-
-    @pl.loop(0, width // TILE)
-    def _(i):
-        c = at(i, TILE)
-        w = r.wb[:, c]
-        r.out[:, c] = r.mid[:, c] + (
-            dot(r.lh[...], w) + dot(r.ll[...], w) + r.gains[6:7, c]
-        )
-
-    comm.advance(56.0)
+    comm.advance(50.0)
+    cot_copy.wait()
 
     def transposed(source, count, first=0):
         @pl.loop(0, count // LANES)
@@ -686,7 +823,7 @@
                 else:
                     r.tile[slot, b, at(k, TILE), :cols] = value
 
-        comm.advance(2.5 * len(pairs))
+        comm.advance(1.0 * len(pairs))
         return slot
 
     def tall(j, grad):
@@ -703,19 +840,35 @@
         return ref[:, start + i * TILE : start + (i + 1) * TILE]
 
     transposed(lambda i, c: silu(r.epre[:, c]), ff)
-    comm.advance(4.0)
+    comm.advance(2.0)
     for i in range(width // TILE):
-        tall(i, cols_of(r.cot, i))
-
-    @pl.loop(0, rows // RC)
-    def _(i):
+        tall(i, cols_of(r.cot_v, i))
+
+    def inner_halves(i):
+        c = at(i, TILE)
+        r.lh[:, c], r.ll[:, c] = split(silu(r.epre[:, c]))
+
+    tiles(ff // TILE, inner_halves, 1.2)
+    weights[4].wait()
+
+    def out_tile(i):
+        c = at(i, TILE)
+        w = r.wb[:, c]
+        r.out[:, c] = r.mid[:, c] + (dot(r.lh[...], w) + dot(r.ll[...], w) + r.gains[6:7, c])
+
+    tiles(width // TILE, out_tile, 3.0)
+    out_copy = pltpu.make_async_copy(r.out, r.out_hbm, r.osem.at[0])
+    out_copy.start()
+
+    def cot_halves(i):
         part = at(i, RC)
-        value = r.cot[part, :]
+        value = r.cot_v[part, :]
         add768(6, value)
         r.lh[part, :width], r.ll[part, :width] = split(value)
 
-    @pl.loop(0, ff // TILE)
-    def _(i):
+    tiles(rows // RC, cot_halves, 1.0)
+
+    def inner_back(i):
         c = at(i, TILE)
         w = r.wb[c, :]
         value = (dot(r.lh[:, :width], w, NT) + dot(r.ll[:, :width], w, NT)) * dsilu(
@@ -724,13 +877,14 @@
         r.epre[:, c] = value
         r.s_expand[:, c] = jnp.sum(value, axis=0, keepdims=True)
 
-    @pl.loop(0, ff // TILE)
-    def _(i):
+    tiles(ff // TILE, inner_back, 3.2)
+    weights[5].start()
+
+    def expand_halves(i):
         c = at(i, TILE)
         r.lh[:, c], r.ll[:, c] = split(r.epre[:, c])
 
-    weights[5].start()
-    comm.tick(7.0)
+    tiles(ff // TILE, expand_halves, 0.8)
 
     @pl.loop(0, rows // RC)
     def _(i):
@@ -739,7 +893,7 @@
         row_set(r.dnorm, part, n * gain1 + shift1)
 
     transposed(lambda i, c: r.dnorm[i], width)
-    comm.advance(3.0)
+    comm.tick(2.0)
     for i in range(ff // (2 * TILE)):
         wide(3 + i, 0, cols_of(r.epre, 2 * i), cols_of(r.epre, 2 * i + 1))
 
@@ -750,16 +904,15 @@
         r.dx[:, c] = dot(r.lh[...], w, NT) + dot(r.ll[...], w, NT)
 
     weights[6].start()
-    comm.tick(4.0)
-
-    @pl.loop(0, rows // RC)
-    def _(i):
+    comm.tick(3.0)
+
+    def middle_back(i):
         part = at(i, RC)
         grad = r.dx[part, :]
         n, inv = norm_stats(r.mid[part, :])
         add768(2, grad * n)
         add768(3, grad)
-        dmid = r.cot[part, :] + norm_back(grad * gain1, n, inv)
+        dmid = r.cot_v[part, :] + norm_back(grad * gain1, n, inv)
         update = sigmoid(r.gate[part, :width])
         pre = r.hpre[part, :]
         x = r.x[part, :]
@@ -775,14 +928,15 @@
         )
         add768(5, dhpre)
 
+    tiles(rows // RC, middle_back, 5.0, 2)
+
     transposed(lambda i, c: r.att[:, c] * silu(r.gate[:, off(reset0, i, LANES)]), hv)
     weights[5].wait()
-    comm.tick(9.0)
+    comm.tick(3.0)
     for i in range(width // TILE):
         tall(6 + i, cols_of(r.gate, i, cand0))
 
-    @pl.loop(0, hv // TILE)
-    def _(i):
+    def attended_back(i):
         c = at(i, TILE)
         w = r.wb[c, :]
         gated = dot(r.lh[:, :width], w, NT) + dot(r.ll[:, :width], w, NT)
@@ -793,13 +947,12 @@
         r.gate[:, here] = dreset
         r.s_gates[:, here] = jnp.sum(dreset, axis=0, keepdims=True)
 
-    comm.tick(6.0)
+    tiles(hv // TILE, attended_back, 3.5)
 
     r.s_small[...] = jnp.zeros_like(r.s_small)
-    r.starts[0] = jnp.zeros((group, group), f32)
-
-    @pl.loop(0, groups)
-    def _(g):
+    r.square[...] = jnp.zeros((group, group), f32)
+
+    def attention_back(g):
         part = at(g, group)
         p = r.probs[part, :]
         p_t = split(p.T)
@@ -813,7 +966,7 @@
 
         dp = lax.fori_loop(0, hv // TILE, value_tile, jnp.zeros((group, group), f32))
         ds = p * (dp - jnp.sum(dp * p, axis=-1, keepdims=True))
-        r.starts[0] += ds
+        r.square[...] += ds
         ds = ds * scale
         pre = r.gate[part, width:reset0]
         shared = silu(pre)
@@ -823,7 +976,8 @@
             r.s_small[n : n + 1, :] += jnp.sum(value, axis=0, keepdims=True)
         r.gate[part, width:reset0] = (dq * q_gain + dk * k_gain) * dsilu(pre)
 
-    diagonals = r.starts[0]
+    tiles(groups, attention_back, 8.4, 4)
+    diagonals = r.square[...].T
     for b in range(group.bit_length() - 1):
         moved = pltpu.roll(diagonals, group - (1 << b), 1)
         diagonals = jnp.where((row_id & (1 << b)) != 0, moved, diagonals)
@@ -831,7 +985,7 @@
     r.s_gates[:, width:reset0] = jnp.sum(r.gate[:, width:reset0], axis=0, keepdims=True)
     r.s_gates[:, cand0:] = r.s768[5:6, :]
 
-    comm.tick(12.0)
+    comm.tick(0.5)
     weights[6].wait()
 
     @pl.loop(0, hv // TILE)
@@ -847,9 +1001,10 @@
         w = r.wa[c, :]
         col_set(r.dnorm, i, dot(r.lh[...], w, NT) + dot(r.ll[...], w, NT))
 
+    comm.tick(4.2)
     transposed(lambda i, c: r.normed[i], width, width)
     transposed(lambda i, c: silu(r.mpre[i]), width)
-    comm.tick(10.0)
+    comm.tick(2.5)
 
     def gate_section(start, size, first, last):
         @pl.loop(0, size // LANES)
@@ -872,28 +1027,29 @@
             else:
                 r.att[:, c] = value
 
+        comm.tick(size * 8.0 / gates)
+
     gate_section(0, reset0, True, False)
     gate_section(reset0, hv, False, False)
     gate_section(cand0, width, False, True)
-
-    comm.tick(10.0)
 
     end_states(r.mpre, True, r.ends)
     adj = jnp.zeros((nstate, width), f32)
     for k in reversed(range(SEG)):
         if k < SEG - 1:
-            adj = dec_seg[...] * (r.sk[k + 1] * adj)
+            adj = dec_seg[...] * (keep_seg[k + 1] * adj)
         adj = adj + row_get(r.ends, seg_of(k))
     r.f_recv[me] = adj
     start_f, wait_f = exchange(r.f_recv, r.send2, r.recv2)
     start_f()
 
-    state = lax.fori_loop(0, seq, carry_step, jnp.zeros((nstate, width), f32))
+    comm.tick(4.0)
     wait_f()
+    comm.tick(7.0)
 
     def adj_step(j, carried):
         k = seq - 1 - j
-        new = r.kf[k] * r.f_recv[k] + dec_all[...] * (r.pk[k] * carried)
+        new = keep(k * groups) * r.f_recv[k] + dec_all[...] * (keep_block(k) * carried)
         return jnp.where(k > me, new, carried)
 
     adj = lax.fori_loop(0, seq, adj_step, jnp.zeros((nstate, width), f32))
@@ -901,22 +1057,13 @@
         fresh = row_get(r.ends, seg_of(k))
         row_set(r.ends, seg_of(k), adj)
         if k > 0:
-            adj = r.sk[k] * (dec_seg[...] * adj + fresh)
-
-    end_states(r.normed, False, r.starts)
-    for k in range(SEG):
-        state = r.sk[k] * state
-        fresh = row_get(r.starts, seg_of(k))
-        row_set(r.starts, seg_of(k), state)
-        state = dec_seg[...] * state + fresh
-
-    comm.tick(6.0)
+            adj = keep_seg[k] * (dec_seg[...] * adj + fresh)
+
     half = nstate // 2
     for h in range(2):
         states = range(h * half, (h + 1) * half)
 
-        @pl.loop(0, width // LANES)
-        def _(d):
+        def average_back(d):
             cols = at(d, LANES)
             dec = rows_of(decay, states, cols)
             mix = rows_of(coef, states, cols)
@@ -956,10 +1103,9 @@
                 row = row + nstate
                 r.s768[row : row + 1, cols] = jnp.sum(q_sum[n], axis=0, keepdims=True)
 
-        comm.tick(9.0)
-
-    @pl.loop(0, rows // RC)
-    def _(i):
+        tiles(width // LANES, average_back, 12.0, 6)
+
+    def first_back(i):
         part = at(i, RC)
         grad = row_get(r.dnorm, part)
         n, inv = norm_stats(r.x[part, :])
@@ -967,14 +1113,14 @@
         add768(1, grad)
         r.dx[part, :] += norm_back(grad * gain0, n, inv)
 
-    comm.tick(3.0)
+    tiles(rows // RC, first_back, 3.0)
+    dx_copy = pltpu.make_async_copy(r.dx, r.dx_hbm, r.osem.at[1])
+    dx_copy.start()
 
     for i in range(hv // (2 * TILE)):
         wide(9 + i, width, cols_of(r.vpre, 2 * i), cols_of(r.vpre, 2 * i + 1))
-    starts = [i * TILE for i in range(width // TILE)]
-    starts += [reset0 + i * TILE for i in range((hv + width) // TILE)]
-    for i in range(len(starts) // 2):
-        left, right = starts[2 * i : 2 * i + 2]
+    for i in range(len(gate_cols) // 2):
+        left, right = gate_cols[2 * i : 2 * i + 2]
         wide(12 + i, 0, cols_of(r.gate, 0, left), cols_of(r.gate, 0, right))
 
     slot = products(comm.jobs - 1, [(0, r.gate[:, width:reset0])])
@@ -995,33 +1141,81 @@
             put(ref[:, d * LANES : (d + 1) * LANES])
     comm.produced(comm.jobs - 1)
     comm.drain()
-
-
-def layer(x, cot, sk, pk, kf, tables, gains, weights, biases, qk, bias_row, batch, seq):
-    rows, width = x.shape
-    w_value, w_gates, w_output, w_expand, w_shrink = weights
+    out_copy.wait()
+    dx_copy.wait()
+
+
+def finish(sums, alpha, delta, beta, eta, *outs):
+    gain, shift, d_alpha, d_delta, d_beta, d_eta, omega, b_output, b_shrink = outs[:9]
+    qk, bias, b_value, b_expand, b_gates = outs[9:]
+    nstate, width = alpha.shape
+    tall_rows = 8 + 2 * nstate
+    for d in range(width // LANES):
+        cols = slice(d * LANES, (d + 1) * LANES)
+        row = d * tall_rows
+        for n in range(2):
+            gain[n : n + 1, cols] = sums[row + 2 * n : row + 2 * n + 1, :]
+            shift[n : n + 1, cols] = sums[row + 2 * n + 1 : row + 2 * n + 2, :]
+        for n, target in enumerate((omega, b_output, b_shrink)):
+            target[d : d + 1, :] = sums[row + 4 + n : row + 5 + n, :]
+        p_sum = sums[row + 8 : row + 8 + nstate, :]
+        q_sum = sums[row + 8 + nstate : row + 8 + 2 * nstate, :]
+        rate, damping = sigmoid(alpha[:, cols]), sigmoid(delta[:, cols])
+        d_inflow = eta[:, cols] * p_sum
+        d_eta[:, cols] = rate * beta[:, cols] * p_sum
+        d_decay = eta[:, cols] * (rate * beta[:, cols]) * q_sum
+        d_rate = d_inflow * beta[:, cols] - d_decay * damping
+        d_alpha[:, cols] = d_rate * rate * (1.0 - rate)
+        d_delta[:, cols] = -d_decay * rate * damping * (1.0 - damping)
+        d_beta[:, cols] = d_inflow * rate
+    place = width // LANES * tall_rows
+    qk[...] = sums[place : place + 3, :]
+    bias[...] = sums[place + 3 : place + 4, :]
+    place += 8
+    for target in (b_value, b_expand, b_gates):
+        target[...] = sums[place : place + target.shape[0], :]
+        place += target.shape[0]
+
+
+def layer(operands, batch, seq):
+    rows, width = operands[0].shape
+    w_value, w_gates, w_output, w_expand, w_shrink = operands[-5:]
     hv, gates, ff = w_value.shape[1], w_gates.shape[1], w_expand.shape[1]
-    zd, group = qk.shape[1], bias_row.shape[1]
-    nstate = tables.shape[1]
+    zd, group, nstate = operands[15].shape[1], operands[16].shape[1], operands[5].shape[0]
     vmem = pl.BlockSpec(memory_space=pltpu.VMEM)
     smem = pl.BlockSpec(memory_space=pltpu.SMEM)
     hbm = pl.BlockSpec(memory_space=pl.ANY)
-    subs = [2] * 18 + [1]
-    kinds = [(0, 1, 0, 1, 2, 0, 1, 0, 1, 3)[j % 10] for j in range(len(subs))]
     stages, slots = len(stage_orders(batch, seq)[0]), slot_count(seq)
 
     def shape(*dims, kind=f32):
         return jax.ShapeDtypeStruct(dims, kind)
 
     return pl.pallas_call(
-        functools.partial(kernel, batch, seq, (kinds, subs)),
-        out_shape=(shape(rows, width), shape(rows, width), shape(sum(subs), BLOCK, TILE)),
-        in_specs=[vmem, vmem, smem, smem, smem, vmem, vmem] + [hbm] * 5 + [vmem] * 5,
-        out_specs=(vmem, vmem, hbm),
+        functools.partial(kernel, batch, seq),
+        out_shape=(
+            shape(rows, width),
+            shape(rows, width),
+            shape(width, hv),
+            shape(width, gates),
+            shape(hv, width),
+            shape(width, ff),
+            shape(ff, width),
+            shape(BLOCK, TILE - zd),
+        ),
+        in_specs=[vmem, hbm, smem] + [vmem] * 14 + [hbm] * 5,
+        out_specs=(hbm,) * 8,
         scratch_shapes=[
             pltpu.VMEM(w_value.shape, bf16),
             pltpu.VMEM(w_output.shape, bf16),
             pltpu.VMEM(w_gates.shape, bf16),
+            pltpu.VMEM((rows, width), f32),
+            pltpu.VMEM((rows, width), f32),
+            pltpu.VMEM((rows, width), f32),
+            pltpu.VMEM((4, nstate, width), f32),
+            pltpu.VMEM((8, width), f32),
+            pltpu.VMEM((1, hv), f32),
+            pltpu.VMEM((1, gates), f32),
+            pltpu.VMEM((1, ff), f32),
             pltpu.VMEM((width // LANES, rows, LANES), f32),
             pltpu.VMEM((rows, hv), f32),
             pltpu.VMEM((rows, gates), f32),
@@ -1032,6 +1226,7 @@
             pltpu.VMEM((width // LANES, rows, LANES), f32),
             pltpu.VMEM((width // LANES, rows, LANES), f32),
             pltpu.VMEM((rows, group), f32),
+            pltpu.VMEM((group, group), f32),
             pltpu.VMEM((rows, max(hv, ff)), bf16),
             pltpu.VMEM((rows, max(hv, ff)), bf16),
             pltpu.VMEM((max(hv, ff), rows), bf16),
@@ -1045,7 +1240,8 @@
             pltpu.VMEM((width // LANES, nstate * SEG, LANES), f32),
             pltpu.VMEM((seq, nstate, width), f32),
             pltpu.VMEM((seq, nstate, width), f32),
-            pltpu.SemaphoreType.DMA((7,)),
+            pltpu.SemaphoreType.DMA((8,)),
+            pltpu.SemaphoreType.DMA((2,)),
             pltpu.SemaphoreType.DMA((seq,)),
             pltpu.SemaphoreType.DMA((seq,)),
             pltpu.SemaphoreType.DMA((seq,)),
@@ -1054,9 +1250,9 @@
             pltpu.SemaphoreType.DMA((stages, slots)),
             pltpu.SemaphoreType.DMA((stages, slots)),
             pltpu.SemaphoreType.REGULAR((stages, slots)),
-            pltpu.SemaphoreType.DMA((len(subs),)),
-            pltpu.SemaphoreType.DMA((len(subs), HALVINGS)),
-            pltpu.SemaphoreType.DMA((len(subs), HALVINGS)),
+            pltpu.SemaphoreType.DMA((JOBS, 2)),
+            pltpu.SemaphoreType.DMA((JOBS, HALVINGS, 2)),
+            pltpu.SemaphoreType.DMA((JOBS, HALVINGS, 2)),
         ]
         + [pltpu.VMEM((slots, 2, count, TILE), f32) for count in stage_rows(stages)],
         compiler_params=pltpu.CompilerParams(
@@ -1065,9 +1261,7 @@
         cost_estimate=pl.CostEstimate(
             flops=52_000_000_000, bytes_accessed=60_000_000, transcendentals=20_000_000
         ),
-    )(
-        x, cot, sk, pk, kf, tables, gains, *weights, *biases, qk, bias_row
-    )
+    )(*operands)
 
 
 def shards(
@@ -1096,114 +1290,48 @@
     w_shrink,
     b_shrink,
 ):
-    rows, width = tokens.shape[1:]
-    group = position_bias.shape[0]
-    blocks = rows // group
-    me = lax.axis_index("seq")
-
-    alpha = jax.nn.sigmoid(alpha_logit).T
-    damping = jax.nn.sigmoid(delta_logit).T
-    beta, eta = ema_beta.T, ema_eta.T
-    inflow = alpha * beta
-    log_decay = jnp.log1p(-alpha * damping)
-    tables = jnp.stack(
-        [
-            jnp.exp(log_decay),
-            inflow * eta,
-            jnp.exp((rows // SEG) * log_decay),
-            jnp.exp(rows * log_decay),
-        ]
+    def lines(vector):
+        return vector.reshape(-1, LANES)
+
+    averages = (alpha_logit.T, delta_logit.T, ema_beta.T, ema_eta.T)
+    operands = (tokens[0], cotangent[0], lengths, norm_gain.T, norm_shift.T) + averages
+    operands += (lines(ema_omega), lines(b_output), lines(b_shrink))
+    operands += (lines(b_value), lines(b_gates), lines(b_expand))
+    operands += (query_key.T, position_bias[None])
+    operands += (w_value, w_gates, w_output, w_expand, w_shrink)
+    output, grad_tokens, dw_value, dw_gates, dw_output, dw_expand, dw_shrink, sums = layer(
+        operands, batch, seq
     )
-    ids = jnp.arange(seq * blocks)
-    first_end = lengths[0, 0]
-    second_end = first_end + lengths[0, 1]
-    keep = 1.0 - ((ids == 0) | (ids == first_end) | (ids == second_end)).astype(f32)
-    keep = keep.reshape(seq, blocks)
-    mine = lax.dynamic_index_in_dim(keep, me, 0, keepdims=False)
-    sk = jnp.ones((blocks, SEG // blocks), f32).at[:, 0].set(mine).reshape(SEG)
-    gains = jnp.stack(
-        [
-            norm_gain[:, 0],
-            norm_shift[:, 0],
-            norm_gain[:, 1],
-            norm_shift[:, 1],
-            ema_omega,
-            b_output,
-            b_shrink,
-            jnp.zeros_like(b_shrink),
-        ]
-    )
-    outs = layer(
-        tokens[0],
-        cotangent[0],
-        sk,
-        jnp.prod(keep, axis=1),
-        keep[:, 0],
-        tables,
-        gains,
-        (w_value, w_gates, w_output, w_expand, w_shrink),
-        (b_value[None], b_gates[None], b_expand[None]),
-        query_key.T,
-        jnp.roll(position_bias[::-1], 1)[None],
-        batch,
-        seq,
-    )
-    output, grad_tokens, blocks_out = outs
-
-    def tall(first, count):
-        parts = blocks_out[first : first + count].reshape(count // 2, 2, BLOCK, TILE)
-        return parts.transpose(1, 2, 0, 3).reshape(2 * BLOCK, count // 2 * TILE)
-
-    def wide(first, count):
-        return blocks_out[first : first + count].transpose(1, 0, 2).reshape(BLOCK, count * TILE)
-
-    nstate = alpha.shape[0]
-    hv, gates, ff = b_value.shape[0], b_gates.shape[0], b_expand.shape[0]
-    zd = query_key.shape[0]
-    dw_shrink, dw_expand, dw_output, dw_value = tall(0, 6), wide(6, 6), tall(12, 6), wide(18, 6)
-    dw_gates = jnp.concatenate(
-        [wide(24, width // TILE), blocks_out[36, :, :zd], wide(24 + width // TILE, 9)], axis=1
-    )
-    rest = blocks_out[36, :, zd:]
-    tall_rows = 8 + 2 * nstate
-    lanes = width // LANES
-    s768 = rest[: lanes * tall_rows].reshape(lanes, tall_rows, LANES)
-    s768 = s768.transpose(1, 0, 2).reshape(tall_rows, width)
-    place = lanes * tall_rows
-    small = rest[place : place + 8]
-    place += 8
-    sums = []
-    for count in (hv, ff, gates):
-        sums.append(rest[place : place + count // LANES].reshape(count))
-        place += count // LANES
-    s_value, s_expand, s_gates = sums
-    p_sum, q_sum = s768[8 : 8 + nstate], s768[8 + nstate : 8 + 2 * nstate]
-    d_inflow = eta * p_sum
-    d_eta = inflow * p_sum
-    d_decay = eta * inflow * q_sum
-    d_alpha = d_inflow * beta - d_decay * damping
+    like = (norm_gain.T, norm_shift.T) + averages
+    like += (lines(ema_omega), lines(b_output), lines(b_shrink), query_key.T)
+    like += (position_bias[None], lines(b_value), lines(b_expand), lines(b_gates))
+    small = pl.pallas_call(
+        finish, out_shape=tuple(jax.ShapeDtypeStruct(a.shape, f32) for a in like)
+    )(sums, *averages)
+    gain, shift, d_alpha, d_delta, d_beta, d_eta, d_omega, d_output, d_shrink = small[:9]
+    d_qk, d_bias, d_value, d_expand, d_gates = small[9:]
     return (
         output[None],
         grad_tokens[None],
-        jnp.stack([s768[0], s768[2]], axis=1),
-        jnp.stack([s768[1], s768[3]], axis=1),
-        (d_alpha * alpha * (1.0 - alpha)).T,
-        (-d_decay * alpha * damping * (1.0 - damping)).T,
-        (d_inflow * alpha).T,
+        gain.T,
+        shift.T,
+        d_alpha.T,
+        d_delta.T,
+        d_beta.T,
         d_eta.T,
-        s768[4],
+        d_omega.reshape(-1),
         dw_value,
-        s_value,
+        d_value.reshape(-1),
         dw_gates,
-        s_gates,
-        small[:3].T,
-        jnp.roll(small[3][::-1], 1),
+        d_gates.reshape(-1),
+        d_qk.T,
+        d_bias[0],
         dw_output,
-        s768[5],
+        d_output.reshape(-1),
         dw_expand,
-        s_expand,
+        d_expand.reshape(-1),
         dw_shrink,
-        s768[6],
+        d_shrink.reshape(-1),
     )
 
 

time: 510 us -> 405 us (0.79)
  local copies, waits for them, and re-layouts: 128 us -> 22.2 us
  Pallas kernels: 363 us -> 382 us
  other arithmetic: 14.6 us -> 0.01 us
    transpose x7 -> x0, local copies, waits for them, and re-layouts: 33 us -> none  [the longest x6 31.8 us: wide(): blocks_out[first:first + count].transpose(1, 0, 2)]
    unnamed x26 -> x21, local copies, waits for them, and re-layouts: 46.9 us -> 22.2 us
    reshape x6 -> x0, local copies, waits for them, and re-layouts: 19.7 us -> none  [the longest x2 16.4 us: tall(): parts = blocks_out[first:first + count].reshape(count // 2, 2, BLOCK, TILE)]
    slice x9 -> x0, local copies, waits for them, and re-layouts: 18.6 us -> none  [the longest x1 13.6 us: tall(): parts = blocks_out[first:first + count].reshape(count // 2, 2, BLOCK, TILE)]
    pallas_call x1 -> x2, Pallas kernels: 363 us -> 382 us  [the longest x1 380 us: layer(): pl.pallas_call(functools.partial(kernel, batch, seq), out_shape=(shape(ro...]
    concatenate x2 -> x0, other arithmetic: 8.64 us -> none  [the longest x1 7.41 us: shards(): jnp.concatenate([wide(24, width // TILE), blocks_out[36, :, :zd], wide(24...]
where the time goes in v3:
time: 405 us
  Pallas kernels  382 us (94%)
  local copies, waits for them, and re-layouts  22.2 us (5%)
    pallas_call x1, Pallas kernels, layer(): pl.pallas_call(functools.partial(kernel, batch, seq), out_shape=(shape(ro...  380 us
    unnamed x21, local copies, waits for them, and re-layouts  22.2 us

profile of v3, /device:TPU:1, one launch (start us, length us, event | category | flops | bytes accessed | tf_op | source)
XLA Modules:
  0.0 404.9 jit_solution(2361875337605034547)
XLA Ops:
  0.7 380.0 %shard_map.373 = (f32[512,768]{1,0:T(8,128)}, f32[512,768]{1,0:T(8,128)}, f32[768,1536]{1,0:T(8,128)}, f32[768,3200]{1,0:T(8,128)}, f32[1536,768]{1,0:T(8,128)},...) custom-call(f32[512,768]{1,0:T(8,128)} %bitcast.46, f32[512,768]{1,0:T(8,128)} %bitcast.47, ...), custom_call_target="tpu_custom_call" | custom-call | flops 51999997952 | bytes 60000000 | tf_op jit(solution)/shard_map/pallas_call | solution.py:1193
  380.7 0.0 copy-start.2
  380.7 1.9 shard_map.374
  382.6 0.0 copy-start.1
  382.6 2.8 copy.50
  385.4 0.0 copy-done.2
  385.5 0.0 copy-start
  385.5 1.1 copy.51
  386.6 0.0 copy-done.1
  386.6 0.0 slice-start.2
  386.6 2.4 copy.52
  389.0 2.6 copy-done
  391.6 0.0 slice-start.3
  391.6 3.9 copy.53
  395.5 0.0 slice-start
  395.5 5.0 %copy.54 = f32[1536,768]{1,0:T(8,128)} copy(f32[1536,768]{1,0:T(8,128)} %get-tuple-element.101) | data formatting | bytes 9437184
  400.5 0.0 slice-done.2
  400.5 0.0 slice-done.3
  400.5 0.0 slice-start.1
  400.5 2.2 copy.55
  402.7 0.0 slice-done
  402.7 0.0 slice-done.1
  402.7 2.2 copy.56
  (2 shorter events, 0.0 us)
Async XLA Ops:
  380.7 4.8 %copy-start.2 = (f32[512,768]{1,0:T(8,128)S(1)}, f32[512,768]{1,0:T(8,128)}, u32[]{:S(2)}) copy-start(f32[512,768]{1,0:T(8,128)} %get-tuple-element.44) | copy-start | bytes 4718596
  382.6 4.0 copy-start.1
  385.5 6.2 %copy-start = (f32[768,3200]{1,0:T(8,128)S(1)}, f32[768,3200]{1,0:T(8,128)}, u32[]{:S(2)}) copy-start(f32[768,3200]{1,0:T(8,128)} %get-tuple-element.97) | copy-start | bytes 29491204
  386.6 13.9 %slice-start.2 = ((s8[4718592]{0:T(1024)(128)(4,1)}), s8[4194304]{0:T(1024)(128)(4,1)S(1)}, s32[]{:S(2)}) async-start(s8[4718592]{0:T(1024)(128)(4,1)} %bitcast.34), calls=%async_computation.2 | async-start | bytes 8388608
  391.6 8.9 %slice-start.3 = ((s8[4718592]{0:T(1024)(128)(4,1)}), s8[524288]{0:T(1024)(128)(4,1)S(1)}, s32[]{:S(2)}) async-start(s8[4718592]{0:T(1024)(128)(4,1)} %bitcast.34), calls=%async_computation.3 | async-start | bytes 1048576
  395.5 7.2 %slice-start = ((s8[4718592]{0:T(1024)(128)(4,1)}), s8[4194304]{0:T(1024)(128)(4,1)S(1)}, s32[]{:S(2)}) async-start(s8[4718592]{0:T(1024)(128)(4,1)} %bitcast.32), calls=%async_computation | async-start | bytes 8388608
  400.5 2.2 slice-start.1

commit v4 on v3

--- a/solution.py
+++ b/solution.py
@@ -92,13 +92,13 @@
 HALVINGS = 5
 BLOCK = 768
 TILES = 2
-SERVICE = 0.7
+SERVICE = 0.5
 JOBS = 19
 KINDS = (0, 1, 0, 1, 2, 0, 1, 0, 1, 3)
 
 
 def slot_count(seq):
-    return 7 if seq <= 16 else 3
+    return 8 if seq <= 16 else 4
 
 
 def bits_of(batch, seq):
@@ -123,8 +123,8 @@
 
 
 class Links:
-    LATENCY = 1.5
-    CORE, LINE = 0.6, 0.0455
+    LATENCY = 8.0
+    CORE, LINE = 0.6, 0.041
 
     def __init__(self):
         self.now = 0.0
@@ -402,7 +402,6 @@
     wb: typing.Any
     wg: typing.Any
     cot_v: typing.Any
-    out: typing.Any
     dx: typing.Any
     tables: typing.Any
     gains: typing.Any
@@ -854,10 +853,10 @@
     def out_tile(i):
         c = at(i, TILE)
         w = r.wb[:, c]
-        r.out[:, c] = r.mid[:, c] + (dot(r.lh[...], w) + dot(r.ll[...], w) + r.gains[6:7, c])
+        r.dx[:, c] = r.mid[:, c] + (dot(r.lh[...], w) + dot(r.ll[...], w) + r.gains[6:7, c])
 
     tiles(width // TILE, out_tile, 3.0)
-    out_copy = pltpu.make_async_copy(r.out, r.out_hbm, r.osem.at[0])
+    out_copy = pltpu.make_async_copy(r.dx, r.out_hbm, r.osem.at[0])
     out_copy.start()
 
     def cot_halves(i):
@@ -896,6 +895,8 @@
     comm.tick(2.0)
     for i in range(ff // (2 * TILE)):
         wide(3 + i, 0, cols_of(r.epre, 2 * i), cols_of(r.epre, 2 * i + 1))
+
+    out_copy.wait()
 
     @pl.loop(0, width // TILE)
     def _(i):
@@ -1006,6 +1007,12 @@
     transposed(lambda i, c: silu(r.mpre[i]), width)
     comm.tick(2.5)
 
+    for i in range(hv // (2 * TILE)):
+        wide(9 + i, width, cols_of(r.vpre, 2 * i), cols_of(r.vpre, 2 * i + 1))
+    for i in range(len(gate_cols) // 2):
+        left, right = gate_cols[2 * i : 2 * i + 2]
+        wide(12 + i, 0, cols_of(r.gate, 0, left), cols_of(r.gate, 0, right))
+
     def gate_section(start, size, first, last):
         @pl.loop(0, size // LANES)
         def _(i):
@@ -1117,12 +1124,6 @@
     dx_copy = pltpu.make_async_copy(r.dx, r.dx_hbm, r.osem.at[1])
     dx_copy.start()
 
-    for i in range(hv // (2 * TILE)):
-        wide(9 + i, width, cols_of(r.vpre, 2 * i), cols_of(r.vpre, 2 * i + 1))
-    for i in range(len(gate_cols) // 2):
-        left, right = gate_cols[2 * i : 2 * i + 2]
-        wide(12 + i, 0, cols_of(r.gate, 0, left), cols_of(r.gate, 0, right))
-
     slot = products(comm.jobs - 1, [(0, r.gate[:, width:reset0])])
     r.tile[slot, 0, :, zd:] = jnp.zeros((BLOCK, TILE - zd), f32)
     place = 0
@@ -1141,7 +1142,6 @@
             put(ref[:, d * LANES : (d + 1) * LANES])
     comm.produced(comm.jobs - 1)
     comm.drain()
-    out_copy.wait()
     dx_copy.wait()
 
 
@@ -1208,7 +1208,6 @@
             pltpu.VMEM(w_value.shape, bf16),
             pltpu.VMEM(w_output.shape, bf16),
             pltpu.VMEM(w_gates.shape, bf16),
-            pltpu.VMEM((rows, width), f32),
             pltpu.VMEM((rows, width), f32),
             pltpu.VMEM((rows, width), f32),
             pltpu.VMEM((4, nstate, width), f32),

time: 405 us -> 346 us (0.85)
  Pallas kernels: 382 us -> 323 us
    pallas_call x1, Pallas kernels: 380 us -> 321 us  [layer(): pl.pallas_call(functools.partial(kernel, batch, seq), out_shape=(shape(ro...]
where the time goes in v4:
time: 346 us
  Pallas kernels  323 us (93%)
  local copies, waits for them, and re-layouts  22.2 us (6%)
    pallas_call x1, Pallas kernels, layer(): pl.pallas_call(functools.partial(kernel, batch, seq), out_shape=(shape(ro...  321 us
    unnamed x21, local copies, waits for them, and re-layouts  22.2 us

profile of v4, /device:TPU:1, one launch (start us, length us, event | category | flops | bytes accessed | tf_op | source)
XLA Modules:
  0.0 345.8 jit_solution(609875265168300140)
XLA Ops:
  0.7 321.0 %shard_map.373 = (f32[512,768]{1,0:T(8,128)}, f32[512,768]{1,0:T(8,128)}, f32[768,1536]{1,0:T(8,128)}, f32[768,3200]{1,0:T(8,128)}, f32[1536,768]{1,0:T(8,128)},...) custom-call(f32[512,768]{1,0:T(8,128)} %bitcast.46, f32[512,768]{1,0:T(8,128)} %bitcast.47, ...), custom_call_target="tpu_custom_call" | custom-call | flops 51999997952 | bytes 60000000 | tf_op jit(solution)/shard_map/pallas_call | solution.py:1193
  321.6 0.0 copy-start.2
  321.6 1.9 shard_map.374
  323.6 0.0 copy-start.1
  323.6 2.8 copy.50
  326.4 0.0 copy-done.2
  326.4 0.0 copy-start
  326.4 1.1 copy.51
  327.5 0.0 copy-done.1
  327.5 0.0 slice-start.2
  327.6 2.4 copy.52
  330.0 2.6 copy-done
  332.6 0.0 slice-start.3
  332.6 3.9 %copy.53 = f32[768,3200]{1,0:T(8,128)} copy(f32[768,3200]{1,0:T(8,128)S(1)} %copy-done) | data formatting | bytes 19660800
  336.5 0.0 slice-start
  336.5 5.0 %copy.54 = f32[1536,768]{1,0:T(8,128)} copy(f32[1536,768]{1,0:T(8,128)} %get-tuple-element.101) | data formatting | bytes 9437184
  341.5 0.0 slice-done.2
  341.5 0.0 slice-done.3
  341.5 0.0 slice-start.1
  341.5 2.2 copy.55
  343.7 0.0 slice-done
  343.7 0.0 slice-done.1
  343.7 2.2 copy.56
  (2 shorter events, 0.0 us)
Async XLA Ops:
  321.6 4.8 %copy-start.2 = (f32[512,768]{1,0:T(8,128)S(1)}, f32[512,768]{1,0:T(8,128)}, u32[]{:S(2)}) copy-start(f32[512,768]{1,0:T(8,128)} %get-tuple-element.44) | copy-start | bytes 4718596
  323.6 4.0 %copy-start.1 = (f32[768,1536]{1,0:T(8,128)S(1)}, f32[768,1536]{1,0:T(8,128)}, u32[]{:S(2)}) copy-start(f32[768,1536]{1,0:T(8,128)} %get-tuple-element.95) | copy-start | bytes 14155780
  326.4 6.2 %copy-start = (f32[768,3200]{1,0:T(8,128)S(1)}, f32[768,3200]{1,0:T(8,128)}, u32[]{:S(2)}) copy-start(f32[768,3200]{1,0:T(8,128)} %get-tuple-element.97) | copy-start | bytes 29491204
  327.5 13.9 %slice-start.2 = ((s8[4718592]{0:T(1024)(128)(4,1)}), s8[4194304]{0:T(1024)(128)(4,1)S(1)}, s32[]{:S(2)}) async-start(s8[4718592]{0:T(1024)(128)(4,1)} %bitcast.34), calls=%async_computation.2 | async-start | bytes 8388608
  332.6 8.9 %slice-start.3 = ((s8[4718592]{0:T(1024)(128)(4,1)}), s8[524288]{0:T(1024)(128)(4,1)S(1)}, s32[]{:S(2)}) async-start(s8[4718592]{0:T(1024)(128)(4,1)} %bitcast.34), calls=%async_computation.3 | async-start | bytes 1048576
  336.5 7.2 %slice-start = ((s8[4718592]{0:T(1024)(128)(4,1)}), s8[4194304]{0:T(1024)(128)(4,1)S(1)}, s32[]{:S(2)}) async-start(s8[4718592]{0:T(1024)(128)(4,1)} %bitcast.32), calls=%async_computation | async-start | bytes 8388608
  341.5 2.2 slice-start.1

commit v5 on v4

--- a/solution.py
+++ b/solution.py
@@ -94,7 +94,7 @@
 TILES = 2
 SERVICE = 0.5
 JOBS = 19
-KINDS = (0, 1, 0, 1, 2, 0, 1, 0, 1, 3)
+KINDS = ((0, 3), (0, 1), (1, 0), (1, 2), (0, 3), (1, 2), (0, 1), (0, 0), (1, 2), (0, 1), (1, 0), (0, 1), (1, 3), (0, 1), (0, 3), (1, 0), (0, 1), (1, 2), (1, 2))
 
 
 def slot_count(seq):
@@ -188,50 +188,53 @@
         self.due = {}
         self.done = [-1] * self.jobs
 
-    def order(self, j):
-        return self.orders[self.kinds[j]]
-
-    def part(self, ref, slot, j, start, size):
-        if not isinstance(start, int):
-            start = pl.multiple_of(start, 8)
-        return ref.at[slot, pl.ds(0, self.subs[j]), pl.ds(start, size), :]
+    def order(self, j, b):
+        return self.orders[self.kinds[j][b]]
 
     def held(self, j, s):
         if s < 0:
             return self.tile, j % TILES, BLOCK
         return self.red[s], j % self.slots, self.rows[s]
 
-    def keep_start(self, j, s):
-        return bit_of(self.order(j)[s]) * self.rows[s] if s < self.halvings else 0
-
-    def give_start(self, j, s):
-        return (1 - bit_of(self.order(j)[s])) * self.rows[s] if s < self.halvings else 0
-
-    def scatter_copy(self, j, s):
+    def keep_start(self, j, b, s):
+        return bit_of(self.order(j, b)[s]) * self.rows[s] if s < self.halvings else 0
+
+    def give_start(self, j, b, s):
+        return (1 - bit_of(self.order(j, b)[s])) * self.rows[s] if s < self.halvings else 0
+
+    def scatter_copies(self, j, s):
         ref, slot, _rows = self.held(j, s - 1)
         into, into_slot, rows = self.held(j, s)
-        return pltpu.make_async_remote_copy(
-            src_ref=self.part(ref, slot, j, self.give_start(j, s), rows),
-            dst_ref=self.part(into, into_slot, j, 0, rows),
-            send_sem=self.send.at[s, into_slot],
-            recv_sem=self.recv.at[s, into_slot],
-            device_id=partner(self.order(j)[s]),
-            device_id_type=MESH,
-        )
+        copies = []
+        for b in range(self.subs[j]):
+            start = self.give_start(j, b, s)
+            if not isinstance(start, int):
+                start = pl.multiple_of(start, 8)
+            copies.append(
+                pltpu.make_async_remote_copy(
+                    src_ref=ref.at[slot, b, pl.ds(start, rows), :],
+                    dst_ref=into.at[into_slot, b],
+                    send_sem=self.send.at[s, into_slot, b],
+                    recv_sem=self.recv.at[s, into_slot, b],
+                    device_id=partner(self.order(j, b)[s]),
+                    device_id_type=MESH,
+                )
+            )
+        return copies
 
     def owned(self, j, s, flip=False):
-        start = 0
-        for t in range(s + 1):
-            bit = bit_of(self.order(j)[t])
-            if flip and t == s:
-                bit = 1 - bit
-            start = start + bit * self.rows[t]
-        return [
-            target.at[
-                pl.ds(pl.multiple_of(row + start, 8), self.rows[s]), pl.ds(col, count)
-            ]
-            for _block, _from, count, target, row, col in self.pieces[j]
-        ]
+        views = []
+        for block, _from, count, target, row, col in self.pieces[j]:
+            start = row
+            for t in range(s + 1):
+                bit = bit_of(self.order(j, block)[t])
+                if flip and t == s:
+                    bit = 1 - bit
+                start = start + bit * self.rows[t]
+            views.append(
+                target.at[pl.ds(pl.multiple_of(start, 8), self.rows[s]), pl.ds(col, count)]
+            )
+        return views
 
     def final(self, j):
         ref, slot, rows = self.held(j, self.stages - 1)
@@ -243,13 +246,14 @@
     def gather_copies(self, j, s, arriving=False):
         last = s == self.halvings - 1
         sources = self.final(j) if last else self.owned(j, s)
+        blocks = [piece[0] for piece in self.pieces[j]]
         return [
             pltpu.make_async_remote_copy(
                 src_ref=source,
                 dst_ref=target,
                 send_sem=self.gsend.at[j, s, p],
                 recv_sem=self.grecv.at[j, s, p],
-                device_id=partner(self.order(j)[s]),
+                device_id=partner(self.order(j, blocks[p])[s]),
                 device_id_type=MESH,
             )
             for p, (source, target) in enumerate(zip(sources, self.owned(j, s, flip=arriving)))
@@ -263,24 +267,39 @@
         ]
 
     def sent(self, j, event, s):
-        size = self.rows[s] * self.subs[j] * TILE * 4e-6
-        self.links.start((j, event), size, self.order(j)[s])
+        size = self.rows[s] * TILE * 4e-6
+        for b in range(self.subs[j]):
+            self.links.start((j, event, b), size, self.order(j, b)[s])
         self.due[j] = event
+
+    def arrival(self, j):
+        times = [self.links.arrived.get((j, self.due[j], b)) for b in range(self.subs[j])]
+        return None if None in times else max(times)
+
+    def first_due(self):
+        times = {j: self.arrival(j) for j in self.due}
+        times = {j: time for j, time in times.items() if time is not None}
+        if not times:
+            return None, None
+        j = min(times, key=times.get)
+        return j, times[j]
 
     def advance(self, us):
         self.links.forward(self.links.now + us)
 
     def run(self, j):
+        while self.arrival(j) is None:
+            self.links.forward()
+        self.links.forward(max(self.links.now, self.arrival(j)))
         event = self.due.pop(j)
-        while (j, event) not in self.links.arrived:
-            self.links.forward()
-        self.links.forward(max(self.links.now, self.links.arrived.pop((j, event))))
+        for b in range(self.subs[j]):
+            self.links.arrived.pop((j, event, b))
         n = self.stages
         if event < n:
             s = event
-            copy = self.scatter_copy(j, s)
-            copy.wait_send()
-            copy.wait_recv()
+            for copy in self.scatter_copies(j, s):
+                copy.wait_send()
+                copy.wait_recv()
             self.add(j, s)
             if s > 0:
                 self.give_credit(j, s - 1)
@@ -310,30 +329,34 @@
     def add(self, j, s):
         ref, slot, _rows = self.held(j, s - 1)
         into, into_slot, rows = self.held(j, s)
-        start = self.keep_start(j, s)
+        starts = [self.keep_start(j, b, s) for b in range(self.subs[j])]
         step = min(48, rows)
 
         @pl.loop(0, rows // step)
         def _(i):
             for b in range(self.subs[j]):
-                here = pl.ds(pl.multiple_of(start + i * step, 8), step)
+                here = pl.ds(pl.multiple_of(starts[b] + i * step, 8), step)
                 there = pl.ds(pl.multiple_of(i * step, 8), step)
                 into[into_slot, b, there, :] += ref[slot, b, here, :]
 
     def give_credit(self, j, s):
-        if j + self.slots < self.jobs:
-            pl.semaphore_signal(
-                self.credit.at[s, j % self.slots],
-                inc=1,
-                device_id=partner(self.order(j + self.slots)[s]),
-                device_id_type=MESH,
-            )
+        after = j + self.slots
+        if after < self.jobs:
+            for b in range(self.subs[after]):
+                pl.semaphore_signal(
+                    self.credit.at[s, j % self.slots, b],
+                    inc=1,
+                    device_id=partner(self.order(after, b)[s]),
+                    device_id_type=MESH,
+                )
 
     def start_scatter(self, j, s):
         if j >= self.slots:
             self.reach(j - self.slots, s + 1)
-            pl.semaphore_wait(self.credit.at[s, j % self.slots], 1)
-        self.scatter_copy(j, s).start()
+            for b in range(self.subs[j]):
+                pl.semaphore_wait(self.credit.at[s, j % self.slots, b], 1)
+        for copy in self.scatter_copies(j, s):
+            copy.start()
         self.sent(j, s, s)
 
     def reach(self, j, event):
@@ -351,16 +374,18 @@
     def tick(self, us=0.0):
         self.advance(us)
         while True:
-            ready = {k: t for k, t in self.links.arrived.items() if t <= self.links.now}
-            if not ready:
+            j, time = self.first_due()
+            if j is None or time > self.links.now:
                 break
-            self.run(min(ready, key=ready.get)[0])
+            self.run(j)
 
     def drain(self):
         while self.due:
-            if not self.links.arrived:
+            j, _time = self.first_due()
+            if j is None:
                 self.links.forward()
-            self.run(min(self.links.arrived, key=self.links.arrived.get)[0])
+            else:
+                self.run(j)
         for j in range(self.jobs):
             for s in range(self.halvings - 1):
                 for copy in self.gather_copies(j, s):
@@ -1007,12 +1032,6 @@
     transposed(lambda i, c: silu(r.mpre[i]), width)
     comm.tick(2.5)
 
-    for i in range(hv // (2 * TILE)):
-        wide(9 + i, width, cols_of(r.vpre, 2 * i), cols_of(r.vpre, 2 * i + 1))
-    for i in range(len(gate_cols) // 2):
-        left, right = gate_cols[2 * i : 2 * i + 2]
-        wide(12 + i, 0, cols_of(r.gate, 0, left), cols_of(r.gate, 0, right))
-
     def gate_section(start, size, first, last):
         @pl.loop(0, size // LANES)
         def _(i):
@@ -1039,6 +1058,12 @@
     gate_section(0, reset0, True, False)
     gate_section(reset0, hv, False, False)
     gate_section(cand0, width, False, True)
+
+    for i in range(hv // (2 * TILE)):
+        wide(9 + i, width, cols_of(r.vpre, 2 * i), cols_of(r.vpre, 2 * i + 1))
+    for i in range(len(gate_cols) // 2):
+        left, right = gate_cols[2 * i : 2 * i + 2]
+        wide(12 + i, 0, cols_of(r.gate, 0, left), cols_of(r.gate, 0, right))
 
     end_states(r.mpre, True, r.ends)
     adj = jnp.zeros((nstate, width), f32)
@@ -1246,9 +1271,9 @@
             pltpu.SemaphoreType.DMA((seq,)),
             pltpu.SemaphoreType.DMA((seq,)),
             pltpu.VMEM((TILES, 2, BLOCK, TILE), f32),
-            pltpu.SemaphoreType.DMA((stages, slots)),
-            pltpu.SemaphoreType.DMA((stages, slots)),
-            pltpu.SemaphoreType.REGULAR((stages, slots)),
+            pltpu.SemaphoreType.DMA((stages, slots, 2)),
+            pltpu.SemaphoreType.DMA((stages, slots, 2)),
+            pltpu.SemaphoreType.REGULAR((stages, slots, 2)),
             pltpu.SemaphoreType.DMA((JOBS, 2)),
             pltpu.SemaphoreType.DMA((JOBS, HALVINGS, 2)),
             pltpu.SemaphoreType.DMA((JOBS, HALVINGS, 2)),

time: 346 us -> 331 us (0.957)
  Pallas kernels: 323 us -> 307 us
    pallas_call x1, Pallas kernels: 321 us -> 305 us  [layer(): pl.pallas_call(functools.partial(kernel, batch, seq), out_shape=(shape(ro...]
where the time goes in v5:
time: 331 us; the launch traced here: 330 us
  Pallas kernels  307 us (93%)
  local copies, waits for them, and re-layouts  22.2 us (7%)
    pallas_call x1, Pallas kernels, layer(): pl.pallas_call(functools.partial(kernel, batch, seq), out_shape=(shape(ro...  305 us
    unnamed x21, local copies, waits for them, and re-layouts  22.2 us

profile of v5, /device:TPU:1, one launch (start us, length us, event | category | flops | bytes accessed | tf_op | source)
XLA Modules:
  0.0 330.4 jit_solution(13997274934631966978)
XLA Ops:
  0.7 305.5 %shard_map.373 = (f32[512,768]{1,0:T(8,128)}, f32[512,768]{1,0:T(8,128)}, f32[768,1536]{1,0:T(8,128)}, f32[768,3200]{1,0:T(8,128)}, f32[1536,768]{1,0:T(8,128)},...) custom-call(f32[512,768]{1,0:T(8,128)} %bitcast.46, f32[512,768]{1,0:T(8,128)} %bitcast.47, ...), custom_call_target="tpu_custom_call" | custom-call | flops 51999997952 | bytes 60000000 | tf_op jit(solution)/shard_map/pallas_call | solution.py:1218
  306.2 0.0 copy-start.2
  306.2 1.9 shard_map.374
  308.1 0.0 copy-start.1
  308.1 2.8 copy.50
  310.9 0.0 copy-done.2
  310.9 0.0 copy-start
  310.9 1.1 copy.51
  312.1 0.0 copy-done.1
  312.1 0.0 slice-start.2
  312.1 2.4 copy.52
  314.5 2.6 copy-done
  317.1 0.0 slice-start.3
  317.1 3.9 %copy.53 = f32[768,3200]{1,0:T(8,128)} copy(f32[768,3200]{1,0:T(8,128)S(1)} %copy-done) | data formatting | bytes 19660800
  321.0 0.0 slice-start
  321.0 5.0 %copy.54 = f32[1536,768]{1,0:T(8,128)} copy(f32[1536,768]{1,0:T(8,128)} %get-tuple-element.101) | data formatting | bytes 9437184
  326.0 0.0 slice-done.2
  326.0 0.0 slice-done.3
  326.0 0.0 slice-start.1
  326.0 2.2 copy.55
  328.2 0.0 slice-done
  328.2 0.0 slice-done.1
  328.2 2.2 copy.56
  (2 shorter events, 0.0 us)
Async XLA Ops:
  306.2 4.8 %copy-start.2 = (f32[512,768]{1,0:T(8,128)S(1)}, f32[512,768]{1,0:T(8,128)}, u32[]{:S(2)}) copy-start(f32[512,768]{1,0:T(8,128)} %get-tuple-element.44) | copy-start | bytes 4718596
  308.1 4.0 %copy-start.1 = (f32[768,1536]{1,0:T(8,128)S(1)}, f32[768,1536]{1,0:T(8,128)}, u32[]{:S(2)}) copy-start(f32[768,1536]{1,0:T(8,128)} %get-tuple-element.95) | copy-start | bytes 14155780
  310.9 6.2 %copy-start = (f32[768,3200]{1,0:T(8,128)S(1)}, f32[768,3200]{1,0:T(8,128)}, u32[]{:S(2)}) copy-start(f32[768,3200]{1,0:T(8,128)} %get-tuple-element.97) | copy-start | bytes 29491204
  312.1 13.9 %slice-start.2 = ((s8[4718592]{0:T(1024)(128)(4,1)}), s8[4194304]{0:T(1024)(128)(4,1)S(1)}, s32[]{:S(2)}) async-start(s8[4718592]{0:T(1024)(128)(4,1)} %bitcast.34), calls=%async_computation.2 | async-start | bytes 8388608
  317.1 8.9 %slice-start.3 = ((s8[4718592]{0:T(1024)(128)(4,1)}), s8[524288]{0:T(1024)(128)(4,1)S(1)}, s32[]{:S(2)}) async-start(s8[4718592]{0:T(1024)(128)(4,1)} %bitcast.34), calls=%async_computation.3 | async-start | bytes 1048576
  321.0 7.2 %slice-start = ((s8[4718592]{0:T(1024)(128)(4,1)}), s8[4194304]{0:T(1024)(128)(4,1)S(1)}, s32[]{:S(2)}) async-start(s8[4718592]{0:T(1024)(128)(4,1)} %bitcast.32), calls=%async_computation | async-start | bytes 8388608
  326.0 2.2 slice-start.1

commit v6 on v5

--- a/solution.py
+++ b/solution.py
@@ -94,7 +94,7 @@
 TILES = 2
 SERVICE = 0.5
 JOBS = 19
-KINDS = ((0, 3), (0, 1), (1, 0), (1, 2), (0, 3), (1, 2), (0, 1), (0, 0), (1, 2), (0, 1), (1, 0), (0, 1), (1, 3), (0, 1), (0, 3), (1, 0), (0, 1), (1, 2), (1, 2))
+KINDS = ((0, 3), (1, 0), (0, 3), (0, 1), (0, 3), (1, 2), (0, 1), (0, 0), (0, 1), (1, 0), (0, 1), (1, 0), (1, 3), (0, 1), (0, 3), (1, 0), (0, 2), (1, 3), (1, 1))
 
 
 def slot_count(seq):
@@ -123,7 +123,7 @@
 
 
 class Links:
-    LATENCY = 8.0
+    LATENCY = 5.06
     CORE, LINE = 0.6, 0.041
 
     def __init__(self):

time: 331 us -> 327 us (0.988)
  Pallas kernels: 307 us -> 303 us
    pallas_call x1, Pallas kernels: 305 us -> 301 us  [layer(): pl.pallas_call(functools.partial(kernel, batch, seq), out_shape=(shape(ro...]
where the time goes in v6:
time: 327 us; the launch traced here: 326 us
  Pallas kernels  303 us (93%)
  local copies, waits for them, and re-layouts  22.2 us (7%)
    pallas_call x1, Pallas kernels, layer(): pl.pallas_call(functools.partial(kernel, batch, seq), out_shape=(shape(ro...  301 us
    unnamed x21, local copies, waits for them, and re-layouts  22.2 us

profile of v6, /device:TPU:1, one launch (start us, length us, event | category | flops | bytes accessed | tf_op | source)
XLA Modules:
  0.0 325.6 jit_solution(3915404256216986670)
XLA Ops:
  0.7 300.7 %shard_map.373 = (f32[512,768]{1,0:T(8,128)}, f32[512,768]{1,0:T(8,128)}, f32[768,1536]{1,0:T(8,128)}, f32[768,3200]{1,0:T(8,128)}, f32[1536,768]{1,0:T(8,128)},...) custom-call(f32[512,768]{1,0:T(8,128)} %bitcast.46, f32[512,768]{1,0:T(8,128)} %bitcast.47, ...), custom_call_target="tpu_custom_call" | custom-call | flops 51999997952 | bytes 60000000 | tf_op jit(solution)/shard_map/pallas_call | solution.py:1218
  301.4 0.0 copy-start.2
  301.4 1.9 shard_map.374
  303.3 0.0 copy-start.1
  303.3 2.8 copy.50
  306.1 0.0 copy-done.2
  306.1 0.0 copy-start
  306.1 1.1 copy.51
  307.3 0.0 copy-done.1
  307.3 0.0 slice-start.2
  307.3 2.4 copy.52
  309.7 2.6 copy-done
  312.3 0.0 slice-start.3
  312.3 3.9 %copy.53 = f32[768,3200]{1,0:T(8,128)} copy(f32[768,3200]{1,0:T(8,128)S(1)} %copy-done) | data formatting | bytes 19660800
  316.2 0.0 slice-start
  316.2 5.0 %copy.54 = f32[1536,768]{1,0:T(8,128)} copy(f32[1536,768]{1,0:T(8,128)} %get-tuple-element.101) | data formatting | bytes 9437184
  321.2 0.0 slice-done.2
  321.2 0.0 slice-done.3
  321.2 0.0 slice-start.1
  321.2 2.2 copy.55
  323.4 0.0 slice-done
  323.4 0.0 slice-done.1
  323.4 2.2 copy.56
  (2 shorter events, 0.0 us)
Async XLA Ops:
  301.4 4.8 %copy-start.2 = (f32[512,768]{1,0:T(8,128)S(1)}, f32[512,768]{1,0:T(8,128)}, u32[]{:S(2)}) copy-start(f32[512,768]{1,0:T(8,128)} %get-tuple-element.44) | copy-start | bytes 4718596
  303.3 4.0 %copy-start.1 = (f32[768,1536]{1,0:T(8,128)S(1)}, f32[768,1536]{1,0:T(8,128)}, u32[]{:S(2)}) copy-start(f32[768,1536]{1,0:T(8,128)} %get-tuple-element.95) | copy-start | bytes 14155780
  306.1 6.2 %copy-start = (f32[768,3200]{1,0:T(8,128)S(1)}, f32[768,3200]{1,0:T(8,128)}, u32[]{:S(2)}) copy-start(f32[768,3200]{1,0:T(8,128)} %get-tuple-element.97) | copy-start | bytes 29491204
  307.3 13.9 %slice-start.2 = ((s8[4718592]{0:T(1024)(128)(4,1)}), s8[4194304]{0:T(1024)(128)(4,1)S(1)}, s32[]{:S(2)}) async-start(s8[4718592]{0:T(1024)(128)(4,1)} %bitcast.34), calls=%async_computation.2 | async-start | bytes 8388608
  312.3 8.9 %slice-start.3 = ((s8[4718592]{0:T(1024)(128)(4,1)}), s8[524288]{0:T(1024)(128)(4,1)S(1)}, s32[]{:S(2)}) async-start(s8[4718592]{0:T(1024)(128)(4,1)} %bitcast.34), calls=%async_computation.3 | async-start | bytes 1048576
  316.2 7.2 %slice-start = ((s8[4718592]{0:T(1024)(128)(4,1)}), s8[4194304]{0:T(1024)(128)(4,1)S(1)}, s32[]{:S(2)}) async-start(s8[4718592]{0:T(1024)(128)(4,1)} %bitcast.32), calls=%async_computation | async-start | bytes 8388608
  321.2 2.2 slice-start.1

commit v7 on v6

--- a/solution.py
+++ b/solution.py
@@ -592,7 +592,7 @@
     def add768(i, value, cols=slice(None)):
         r.s768[i : i + 1, cols] += jnp.sum(value, axis=0, keepdims=True)
 
-    RC = 32
+    RC = 64
 
     def norm_stats(value):
         centre = value - jnp.mean(value, axis=-1, keepdims=True)

time: 327 us -> 323 us (0.988)
  Pallas kernels: 303 us -> 298 us
    pallas_call x1, Pallas kernels: 301 us -> 296 us  [layer(): pl.pallas_call(functools.partial(kernel, batch, seq), out_shape=(shape(ro...]
where the time goes in v7:
time: 323 us; the launch traced here: 321 us
  Pallas kernels  298 us (92%)
  local copies, waits for them, and re-layouts  22.2 us (7%)
    pallas_call x1, Pallas kernels, layer(): pl.pallas_call(functools.partial(kernel, batch, seq), out_shape=(shape(ro...  296 us
    unnamed x21, local copies, waits for them, and re-layouts  22.2 us

profile of v7, /device:TPU:1, one launch (start us, length us, event | category | flops | bytes accessed | tf_op | source)
XLA Modules:
  0.0 321.1 jit_solution(7025638712128975669)
XLA Ops:
  0.7 296.2 %shard_map.373 = (f32[512,768]{1,0:T(8,128)}, f32[512,768]{1,0:T(8,128)}, f32[768,1536]{1,0:T(8,128)}, f32[768,3200]{1,0:T(8,128)}, f32[1536,768]{1,0:T(8,128)},...) custom-call(f32[512,768]{1,0:T(8,128)} %bitcast.46, f32[512,768]{1,0:T(8,128)} %bitcast.47, ...), custom_call_target="tpu_custom_call" | custom-call | flops 51999997952 | bytes 60000000 | tf_op jit(solution)/shard_map/pallas_call | solution.py:1218
  296.9 0.0 copy-start.2
  296.9 1.9 shard_map.374
  298.9 0.0 copy-start.1
  298.9 2.8 copy.50
  301.7 0.0 copy-done.2
  301.7 0.0 copy-start
  301.7 1.1 copy.51
  302.8 0.0 copy-done.1
  302.8 0.0 slice-start.2
  302.8 2.4 copy.52
  305.2 2.6 copy-done
  307.9 0.0 slice-start.3
  307.9 3.9 %copy.53 = f32[768,3200]{1,0:T(8,128)} copy(f32[768,3200]{1,0:T(8,128)S(1)} %copy-done) | data formatting | bytes 19660800
  311.7 0.0 slice-start
  311.8 5.0 %copy.54 = f32[1536,768]{1,0:T(8,128)} copy(f32[1536,768]{1,0:T(8,128)} %get-tuple-element.101) | data formatting | bytes 9437184
  316.7 0.0 slice-done.2
  316.7 0.0 slice-done.3
  316.7 0.0 slice-start.1
  316.7 2.2 copy.55
  318.9 0.0 slice-done
  318.9 0.0 slice-done.1
  318.9 2.2 copy.56
  (2 shorter events, 0.0 us)
Async XLA Ops:
  296.9 4.8 %copy-start.2 = (f32[512,768]{1,0:T(8,128)S(1)}, f32[512,768]{1,0:T(8,128)}, u32[]{:S(2)}) copy-start(f32[512,768]{1,0:T(8,128)} %get-tuple-element.44) | copy-start | bytes 4718596
  298.9 4.0 %copy-start.1 = (f32[768,1536]{1,0:T(8,128)S(1)}, f32[768,1536]{1,0:T(8,128)}, u32[]{:S(2)}) copy-start(f32[768,1536]{1,0:T(8,128)} %get-tuple-element.95) | copy-start | bytes 14155780
  301.7 6.2 %copy-start = (f32[768,3200]{1,0:T(8,128)S(1)}, f32[768,3200]{1,0:T(8,128)}, u32[]{:S(2)}) copy-start(f32[768,3200]{1,0:T(8,128)} %get-tuple-element.97) | copy-start | bytes 29491204
  302.8 13.9 %slice-start.2 = ((s8[4718592]{0:T(1024)(128)(4,1)}), s8[4194304]{0:T(1024)(128)(4,1)S(1)}, s32[]{:S(2)}) async-start(s8[4718592]{0:T(1024)(128)(4,1)} %bitcast.34), calls=%async_computation.2 | async-start | bytes 8388608
  307.9 8.9 %slice-start.3 = ((s8[4718592]{0:T(1024)(128)(4,1)}), s8[524288]{0:T(1024)(128)(4,1)S(1)}, s32[]{:S(2)}) async-start(s8[4718592]{0:T(1024)(128)(4,1)} %bitcast.34), calls=%async_computation.3 | async-start | bytes 1048576
  311.7 7.2 %slice-start = ((s8[4718592]{0:T(1024)(128)(4,1)}), s8[4194304]{0:T(1024)(128)(4,1)S(1)}, s32[]{:S(2)}) async-start(s8[4718592]{0:T(1024)(128)(4,1)} %bitcast.32), calls=%async_computation | async-start | bytes 8388608
  316.7 2.2 slice-start.1
